TPU v7x, 512 devices: a whole 4x4x16 slice. The times are simulated.
512 devices in a mesh: lon: 32 (over x, y, z_hi), lat: 16 (over z_lo, core).
Axes of the slice: x: 4, y: 4, z: 16 (z_hi: 2, z_lo: 8; z = z_hi * 8 + z_lo), core: 2. Of those that a mesh axis runs over, the one named last changes fastest.
Arguments:
- tracer: float32 [4, 1, 2048, 4096], P(None, None, 'lat', 'lon'), may hold values from -6 to 6
- final_adjoint: float32 [4, 1, 2048, 4096], P(None, None, 'lat', 'lon'), may hold values from -6 to 6
- speed_east: float32 [1, 2048, 4096], P(None, 'lat', 'lon'), may hold values from 0.1 to 1
- speed_north: float32 [1, 2048, 4096], P(None, 'lat', 'lon'), may hold values from 0.1 to 1
- sign_east: int32 [1, 2048, 4096], P(None, 'lat', 'lon'), may hold values 0 or 1
- sign_north: int32 [1, 2048, 4096], P(None, 'lat', 'lon'), may hold values 0 or 1
- density: float32 [1, 2048, 4096], P(None, 'lat', 'lon'), may hold values from 0.6 to 1.5
- land_type: int32 [2048, 4096], P('lat', 'lon'), may hold values from 0 to 7
- source_mask: int32 [2048, 4096], P('lat', 'lon'), may hold values 0 or 1
- emission: float32 [4, 2048, 4096], P(None, 'lat', 'lon'), may hold values from 0.2 to 2
- deposition: float32 [8, 4], replicated, may hold values from 0.2 to 2
Outputs:
- adjoint_tracer: float32 [4, 1, 2048, 4096], P(None, None, 'lat', 'lon')
- density_grad: float32 [1, 2048, 4096], P(None, 'lat', 'lon')
- emission_grad: float32 [4, 2048, 4096], P(None, 'lat', 'lon')
Inputs may be any that keep to these rules, and one draw needn't show every extreme that they name: `sign_east`: 1 where the western face's wind blows toward higher longitude index, 0 where it blows the other way. `sign_north`: 1 where the southern face's wind blows toward higher latitude index, 0 where it blows the other way.
All inputs are finite; a program needn't handle non-finite values. No bound on the sum of `sign_east` or of `sign_north` or of `source_mask` on one device may be relied on, other than what follows from the above.
Results may differ from a plain program's by a relative error of at most 0.0003.
Values sent between devices are 32-bit elements; how exact they have to be, the bound alone decides.
No kernel may reach another device: no remote copies, remote signals or barrier semaphores. Data moves between devices by JAX's collectives and lax.ppermute only.
A program may use at most 64 MiB of HBM per device.

v0:
```python
import jax
import jax.numpy as jnp
from jax import lax
from jax.sharding import PartitionSpec as P

COURANT = 0.3
TIME_STEP = 0.25


def with_halo(block, sides, width):
    for axis, dim in sides:
        count = lax.axis_size(axis)
        forward = [(i, i + 1) for i in range(count - 1)]
        forward.append((count - 1, 0))
        backward = [(target, source) for source, target in forward]
        low = lax.ppermute(
            lax.slice_in_dim(block, block.shape[dim] - width, None, axis=dim), axis, forward
        )
        high = lax.ppermute(lax.slice_in_dim(block, 0, width, axis=dim), axis, backward)
        block = jnp.concatenate([low, block, high], axis=dim)
    return block


def lon_cut(values, begin_at, end_at):
    return values[..., begin_at:end_at]


def lat_cut(values, begin_at, end_at):
    return values[..., begin_at:end_at, :]


def divergence(tracer, velocity, density, cutter, extent):
    far_back = cutter(tracer, 0, extent - 3)
    behind = cutter(tracer, 1, extent - 2)
    center = cutter(tracer, 2, extent - 1)
    in_front = cutter(tracer, 3, extent)
    from_back = (-far_back + 5.0 * behind + 2.0 * center) / 6.0
    from_front = (2.0 * behind + 5.0 * center - in_front) / 6.0
    signed_wind = cutter(velocity, 2, extent - 1)
    face_mass = signed_wind * (
        0.5 * (cutter(density, 1, extent - 2) + cutter(density, 2, extent - 1))
    )
    fluxes = face_mass * jnp.where(signed_wind > 0.0, from_back, from_front)
    return cutter(fluxes, 1, extent - 3) - cutter(fluxes, 0, extent - 4)


def advance(tracer, wind_east, wind_north, density, losses, source, weight):
    row_count = tracer.shape[-2]
    col_count = tracer.shape[-1]
    east_change = divergence(
        tracer[..., 2:-2, :], wind_east[..., 2:-2, :], density[..., 2:-2, :], lon_cut, col_count
    )
    north_change = divergence(
        tracer[..., :, 2:-2], wind_north[..., :, 2:-2], density[..., :, 2:-2], lat_cut, row_count
    )
    interior = tracer[..., 2:-2, 2:-2]
    carried = interior - COURANT * (east_change + north_change) / density[..., 2:-2, 2:-2]
    surface = (
        carried[:, 0]
        - losses[..., 2:-2, 2:-2] * weight * interior[:, 0]
        + source[..., 2:-2, 2:-2] * weight
    )
    return jnp.concatenate([surface[:, None], carried[:, 1:]], axis=1)


def land_losses(land_type, deposition):
    land_kinds = deposition.shape[0]
    one_hot = (land_type[None] == lax.broadcasted_iota(jnp.int32, (land_kinds, 1, 1), 0)).astype(
        jnp.float32
    )
    return TIME_STEP * jnp.einsum(
        "kb,krc->brc", deposition, one_hot, precision=lax.Precision.HIGHEST
    )


def pole_inside(row_count, margin):
    global_rows = (
        lax.axis_index("lat") * row_count
        + lax.broadcasted_iota(jnp.int32, (row_count + 2 * margin, 1), 0)
        - margin
    )
    return (global_rows >= 0) & (global_rows < lax.axis_size("lat") * row_count)


def grow(tracer, wind_east, wind_north, density, losses, source, margin):
    bin_count, levels, row_count, col_count = tracer.shape
    stacked = tracer.reshape(bin_count * levels, row_count, col_count)
    padded = (
        with_halo(stacked, (("lon", 2), ("lat", 1)), margin),
        with_halo(wind_east, (("lon", 2), ("lat", 1)), margin),
        with_halo(wind_north, (("lon", 2), ("lat", 1)), margin),
        with_halo(density, (("lon", 2), ("lat", 1)), margin),
        with_halo(losses, (("lon", 2), ("lat", 1)), margin),
        with_halo(source, (("lon", 2), ("lat", 1)), margin),
    )
    inside = pole_inside(row_count, margin)
    tracer_padded = jnp.where(inside, padded[0], 0.0).reshape(
        bin_count, levels, row_count + 2 * margin, col_count + 2 * margin
    )
    east_padded = jnp.where(inside, padded[1], 0.0)
    north_padded = jnp.where(inside, padded[2], 0.0)
    density_padded = jnp.where(inside, padded[3], 1.0)
    losses_padded = jnp.where(inside, padded[4], 0.0)
    source_padded = jnp.where(inside, padded[5], 0.0)
    return (tracer_padded, east_padded, north_padded, density_padded, losses_padded, source_padded)


def fold_rim(values, margin):
    central = values[..., 2 * margin : -2 * margin, :]
    central = central.at[..., :margin, :].add(values[..., :margin, :])
    central = central.at[..., -margin:, :].add(values[..., -margin:, :])
    result = central[..., 2 * margin : -2 * margin]
    result = result.at[..., :margin].add(central[..., :margin])
    result = result.at[..., -margin:].add(central[..., -margin:])
    return result


def give_back(partials, margin):
    tracer_part, density_part, source_part = partials
    bin_count, levels, rows_padded, cols_padded = tracer_part.shape
    inside = pole_inside(rows_padded - 2 * margin, margin)
    stacked = jnp.where(inside, tracer_part, 0.0).reshape(
        bin_count * levels, rows_padded, cols_padded
    )
    returned = (
        with_halo(stacked, (("lon", 2), ("lat", 1)), margin),
        with_halo(jnp.where(inside, density_part, 0.0), (("lon", 2), ("lat", 1)), margin),
        with_halo(jnp.where(inside, source_part, 0.0), (("lon", 2), ("lat", 1)), margin),
    )
    folded = fold_rim(returned[0], margin).reshape(
        bin_count, levels, rows_padded - 2 * margin, cols_padded - 2 * margin
    )
    return (folded, fold_rim(returned[1], margin), fold_rim(returned[2], margin))


def shards(
    tracer,
    final_adjoint,
    speed_east,
    speed_north,
    sign_east,
    sign_north,
    density,
    land_type,
    source_mask,
    emission,
    deposition,
):
    bin_count, levels, row_count, col_count = tracer.shape
    wind_east = jnp.where(sign_east == 1, speed_east, -speed_east)
    global_rows = lax.axis_index("lat") * row_count + lax.broadcasted_iota(
        jnp.int32, (row_count, 1), 0
    )
    wind_north = jnp.where(
        global_rows == 0, 0.0, jnp.where(sign_north == 1, speed_north, -speed_north)
    )
    losses = land_losses(land_type, deposition)
    source = TIME_STEP * source_mask.astype(jnp.float32) * emission
    tracer_padded, east_padded, north_padded, density_padded, losses_padded, source_padded = grow(
        tracer, wind_east, wind_north, density, losses, source, 2
    )

    def one_step(start_tracer, step_density, step_source):
        return advance(
            start_tracer, east_padded, north_padded, step_density, losses_padded, step_source, 1.0
        )

    middle, pull_first = jax.vjp(one_step, tracer_padded, density_padded, source_padded)
    inside = pole_inside(row_count, 2)
    middle_spread = with_halo(
        middle.reshape(bin_count * levels, row_count, col_count), (("lon", 2), ("lat", 1)), 2
    )
    middle_padded = jnp.where(inside, middle_spread, 0.0).reshape(
        bin_count, levels, row_count + 4, col_count + 4
    )
    unused_final, pull_second = jax.vjp(one_step, middle_padded, density_padded, source_padded)
    middle_part, density_second, source_second = pull_second(final_adjoint)
    middle_stacked = jnp.where(inside, middle_part, 0.0).reshape(
        bin_count * levels, row_count + 4, col_count + 4
    )
    middle_return = with_halo(middle_stacked, (("lon", 2), ("lat", 1)), 2)
    middle_adjoint = fold_rim(middle_return, 2).reshape(bin_count, levels, row_count, col_count)
    tracer_part, density_first, source_first = pull_first(middle_adjoint)
    adjoint_tracer, density_grad, source_grad = give_back(
        (tracer_part, density_first + density_second, source_first + source_second), 2
    )
    emission_grad = TIME_STEP * source_mask.astype(jnp.float32) * source_grad
    return (adjoint_tracer, density_grad, emission_grad)


def solution(mesh):
    return jax.shard_map(
        shards,
        mesh=mesh,
        in_specs=(
            P(None, None, "lat", "lon"),
            P(None, None, "lat", "lon"),
            P(None, "lat", "lon"),
            P(None, "lat", "lon"),
            P(None, "lat", "lon"),
            P(None, "lat", "lon"),
            P(None, "lat", "lon"),
            P("lat", "lon"),
            P("lat", "lon"),
            P(None, "lat", "lon"),
            P(),
        ),
        out_specs=(P(None, None, "lat", "lon"), P(None, "lat", "lon"), P(None, "lat", "lon")),
        check_vma=False,
    )
```

profile of v0, /device:TPU:2, one launch (start us, length us, event | category | flops | bytes accessed | tf_op | source)
XLA Modules:
  0.0 631.0 jit_solution(11583343162077141490)
XLA Ops:
  1.7 18.1 %collective-permute-start.9 = (f32[1,128,2]{2,1,0:T(8,128)S(1)}, f32[1,128,2]{2,1,0:T(8,128)S(1)}, u32[]{:S(2)}, u32[]{:S(2)}) collective-permute-start(f32[1,128,2]{2,1,0:T(8,128)S(1)} %get-tuple-element.297), channel_id=1, source_target_pairs={{16,0},{32,16},{48,32},{64,48},{80,64},{96,80},{112,96},{128,112},... | collective-permute-start | bytes 3080 | tf_op jit(solution)/shard_map/ppermute | solution.py:19
  19.8 1.9 collective-permute-start.8
  22.1 15.6 %collective-permute-start.25 = (f32[4,128,2]{2,0,1:T(4,128)S(1)}, f32[4,128,2]{2,0,1:T(4,128)S(1)}, u32[]{:S(2)}, u32[]{:S(2)}) collective-permute-start(f32[4,128,2]{2,0,1:T(4,128)S(1)} %get-tuple-element.271), channel_id=1, source_target_pairs={{16,0},{32,16},{48,32},{64,48},{80,64},{96,80},{112,96},{128,112},... | collective-permute-start | bytes 12296 | tf_op jit(solution)/shard_map/ppermute | solution.py:19
  37.8 1.9 collective-permute-start.24
  39.9 15.6 %collective-permute-start.13 = (f32[1,128,2]{2,1,0:T(8,128)S(1)}, f32[1,128,2]{2,1,0:T(8,128)S(1)}, u32[]{:S(2)}, u32[]{:S(2)}) collective-permute-start(f32[1,128,2]{2,1,0:T(8,128)S(1)} %get-tuple-element.299), channel_id=1, source_target_pairs={{16,0},{32,16},{48,32},{64,48},{80,64},{96,80},{112,96},{128,112},... | collective-permute-start | bytes 3080 | tf_op jit(solution)/shard_map/ppermute | solution.py:19
  60.5 15.6 %collective-permute-start.1 = (f32[4,128,2]{2,0,1:T(4,128)}, f32[4,128,2]{2,0,1:T(4,128)S(1)}, u32[]{:S(2)}, u32[]{:S(2)}) collective-permute-start(f32[4,128,2]{2,0,1:T(4,128)} %get-tuple-element.275), channel_id=1, source_target_pairs={{16,0},{32,16},{48,32},{64,48},{80,64},{96,80},{112,96},{128,112},... | collective-permute-start | bytes 12296 | tf_op jit(solution)/shard_map/ppermute | solution.py:19
  76.3 7.3 %collective-permute-start.5 = (f32[1,128,2]{2,1,0:T(8,128)S(1)}, f32[1,128,2]{2,1,0:T(8,128)S(1)}, u32[]{:S(2)}, u32[]{:S(2)}) collective-permute-start(f32[1,128,2]{2,1,0:T(8,128)S(1)} %get-tuple-element.295), channel_id=1, source_target_pairs={{16,0},{32,16},{48,32},{64,48},{80,64},{96,80},{112,96},{128,112},... | collective-permute-start | bytes 3080 | tf_op jit(solution)/shard_map/ppermute | solution.py:19
  83.6 6.4 %collective-permute-done.12 = f32[1,128,2]{2,1,0:T(8,128)S(1)} collective-permute-done((f32[1,128,2]{2,1,0:T(8,128)S(1)}, f32[1,128,2]{2,1,0:T(8,128)S(1)}, u32[]{:S(2)}, u32[]{:S(2)}) %collective-permute-start.12) | collective-permute-done | bytes 1056 | tf_op jit(solution)/shard_map/ppermute | solution.py:16
  92.0 27.3 %collective-permute-done.5 = f32[1,128,2]{2,1,0:T(8,128)S(1)} collective-permute-done((f32[1,128,2]{2,1,0:T(8,128)S(1)}, f32[1,128,2]{2,1,0:T(8,128)S(1)}, u32[]{:S(2)}, u32[]{:S(2)}) %collective-permute-start.5) | collective-permute-done | bytes 1056 | tf_op jit(solution)/shard_map/ppermute | solution.py:19
  119.3 6.1 collective-permute-start.11
  125.4 1.9 collective-permute-start.10
  127.4 10.2 %collective-permute-start.15 = (f32[1,2,132]{2,1,0:T(2,128)S(1)}, f32[1,2,132]{2,1,0:T(2,128)S(1)}, u32[]{:S(2)}, u32[]{:S(2)}) collective-permute-start(f32[1,2,132]{2,1,0:T(2,128)S(1)} %get-tuple-element.281), channel_id=1, source_target_pairs={{1,0},{2,1},{3,2},{4,3},{5,4},{6,5},{7,6},{8,7},{9,8},{10,9},{11,1... | collective-permute-start | bytes 3176 | tf_op jit(solution)/shard_map/ppermute | solution.py:19
  137.7 1.9 collective-permute-start.14
  139.7 10.2 %collective-permute-start.7 = (f32[1,2,132]{2,1,0:T(2,128)S(1)}, f32[1,2,132]{2,1,0:T(2,128)S(1)}, u32[]{:S(2)}, u32[]{:S(2)}) collective-permute-start(f32[1,2,132]{2,1,0:T(2,128)S(1)} %get-tuple-element.277), channel_id=1, source_target_pairs={{1,0},{2,1},{3,2},{4,3},{5,4},{6,5},{7,6},{8,7},{9,8},{10,9},{11,1... | collective-permute-start | bytes 3176 | tf_op jit(solution)/shard_map/ppermute | solution.py:19
  150.0 1.9 collective-permute-start.6
  152.2 5.7 collective-permute-start
  157.9 7.3 %collective-permute-done.6 = f32[1,2,132]{2,1,0:T(2,128)S(1)} collective-permute-done((f32[1,2,132]{2,1,0:T(2,128)S(1)}, f32[1,2,132]{2,1,0:T(2,128)S(1)}, u32[]{:S(2)}, u32[]{:S(2)}) %collective-permute-start.6) | collective-permute-done | bytes 1088 | tf_op jit(solution)/shard_map/ppermute | solution.py:16
  166.6 2.6 collective-permute-start.27
  169.2 1.9 collective-permute-start.26
  171.2 12.8 %collective-permute-done = f32[4,128,2]{2,0,1:T(4,128)S(1)} collective-permute-done((f32[4,128,2]{2,0,1:T(4,128)}, f32[4,128,2]{2,0,1:T(4,128)S(1)}, u32[]{:S(2)}, u32[]{:S(2)}) %collective-permute-start) | collective-permute-done | bytes 4128 | tf_op jit(solution)/shard_map/ppermute | solution.py:16
  184.1 4.0 collective-permute-start.3
  188.1 2.1 collective-permute-start.2
  190.7 9.2 %collective-permute-done.2 = f32[4,2,132]{2,0,1:T(4,128)S(1)} collective-permute-done((f32[4,2,132]{2,0,1:T(4,128)S(1)}, f32[4,2,132]{2,0,1:T(4,128)S(1)}, u32[]{:S(2)}, u32[]{:S(2)}) %collective-permute-start.2) | collective-permute-done | bytes 4256 | tf_op jit(solution)/shard_map/ppermute | solution.py:16
  204.4 5.3 collective-permute-start.17
  209.7 9.3 %collective-permute-start.16 = (f32[4,132,2]{2,0,1:T(4,128)S(1)}, f32[4,132,2]{2,0,1:T(4,128)S(1)}, u32[]{:S(2)}, u32[]{:S(2)}) collective-permute-start(f32[4,132,2]{2,0,1:T(4,128)S(1)} %get-tuple-element.247), channel_id=1, source_target_pairs={{0,16},{16,32},{32,48},{48,64},{64,80},{80,96},{96,112},{112,128},... | collective-permute-start | bytes 12680 | tf_op jit(solution)/shard_map/ppermute | solution.py:16
  219.6 6.5 %collective-permute-done.17 = f32[4,132,2]{2,0,1:T(4,128)S(1)} collective-permute-done((f32[4,132,2]{2,0,1:T(4,128)S(1)}, f32[4,132,2]{2,0,1:T(4,128)S(1)}, u32[]{:S(2)}, u32[]{:S(2)}) %collective-permute-start.17) | collective-permute-done | bytes 4256 | tf_op jit(solution)/shard_map/ppermute | solution.py:19
  226.2 28.3 %collective-permute-done.16 = f32[4,132,2]{2,0,1:T(4,128)S(1)} collective-permute-done((f32[4,132,2]{2,0,1:T(4,128)S(1)}, f32[4,132,2]{2,0,1:T(4,128)S(1)}, u32[]{:S(2)}, u32[]{:S(2)}) %collective-permute-start.16) | collective-permute-done | bytes 4256 | tf_op jit(solution)/shard_map/ppermute | solution.py:16
  254.5 1.9 collective-permute-start.18
  257.0 10.4 %collective-permute-start.19 = (f32[4,2,136]{2,0,1:T(4,128)S(1)}, f32[4,2,136]{2,0,1:T(4,128)S(1)}, u32[]{:S(2)}, u32[]{:S(2)}) collective-permute-start(f32[4,2,136]{2,0,1:T(4,128)S(1)} %get-tuple-element.225), channel_id=1, source_target_pairs={{1,0},{2,1},{3,2},{4,3},{5,4},{6,5},{7,6},{8,7},{9,8},{10,9},{11,1... | collective-permute-start | bytes 13064 | tf_op jit(solution)/shard_map/ppermute | solution.py:19
  269.0 4.2 scatter-add.56
  273.6 21.4 %scatter-add.59 = f32[4,128,128]{2,0,1:T(4,128)S(1)} dynamic-update-slice(f32[4,128,128]{2,0,1:T(4,128)S(1)} %scatter-add.56, f32[4,128,2]{2,0,1:T(4,128)S(1)} %slice_add_fusion.4, s32[]{:T(128)} %constant.414.clone.1, s32[]{:T(128)} %constant.414.clone.1, s32[]{:T(128)} %constant.425.clone.1) | dynamic-update-slice | bytes 8196 | tf_op jit(solution)/shard_map/scatter-add | solution.py:114
  296.9 8.0 %collective-permute-start.41 = (f32[4,132,2]{2,0,1:T(4,128)S(1)}, f32[4,132,2]{2,0,1:T(4,128)S(1)}, u32[]{:S(2)}, u32[]{:S(2)}) collective-permute-start(f32[4,132,2]{2,0,1:T(4,128)S(1)} %get-tuple-element.244), channel_id=1, source_target_pairs={{16,0},{32,16},{48,32},{64,48},{80,64},{96,80},{112,96},{128,112},... | collective-permute-start | bytes 12680 | tf_op jit(solution)/shard_map/ppermute | solution.py:19
  304.9 6.6 %collective-permute-start.40 = (f32[4,132,2]{2,0,1:T(4,128)S(1)}, f32[4,132,2]{2,0,1:T(4,128)S(1)}, u32[]{:S(2)}, u32[]{:S(2)}) collective-permute-start(f32[4,132,2]{2,0,1:T(4,128)S(1)} %get-tuple-element.243), channel_id=1, source_target_pairs={{0,16},{16,32},{32,48},{48,64},{64,80},{80,96},{96,112},{112,128},... | collective-permute-start | bytes 12680 | tf_op jit(solution)/shard_map/ppermute | solution.py:16
  311.5 4.5 multiply_reduce_fusion.1
  316.9 18.1 %collective-permute-done.41 = f32[4,132,2]{2,0,1:T(4,128)S(1)} collective-permute-done((f32[4,132,2]{2,0,1:T(4,128)S(1)}, f32[4,132,2]{2,0,1:T(4,128)S(1)}, u32[]{:S(2)}, u32[]{:S(2)}) %collective-permute-start.41) | collective-permute-done | bytes 4256 | tf_op jit(solution)/shard_map/ppermute | solution.py:19
  335.0 4.7 collective-permute-done.40
  339.7 1.9 collective-permute-start.42
  342.2 10.2 %collective-permute-start.43 = (f32[4,2,136]{2,0,1:T(4,128)S(1)}, f32[4,2,136]{2,0,1:T(4,128)S(1)}, u32[]{:S(2)}, u32[]{:S(2)}) collective-permute-start(f32[4,2,136]{2,0,1:T(4,128)S(1)} %get-tuple-element.221), channel_id=1, source_target_pairs={{1,0},{2,1},{3,2},{4,3},{5,4},{6,5},{7,6},{8,7},{9,8},{10,9},{11,1... | collective-permute-start | bytes 13064 | tf_op jit(solution)/shard_map/ppermute | solution.py:19
  354.2 4.2 scatter-add.76
  358.8 21.4 %scatter-add.79 = f32[4,128,128]{2,0,1:T(4,128)S(1)} dynamic-update-slice(f32[4,128,128]{2,0,1:T(4,128)S(1)} %scatter-add.76, f32[4,128,2]{2,0,1:T(4,128)S(1)} %slice_add_fusion, s32[]{:T(128)} %constant.414.clone.1, s32[]{:T(128)} %constant.414.clone.1, s32[]{:T(128)} %constant.425.clone.1) | dynamic-update-slice | bytes 8196 | tf_op jit(solution)/shard_map/scatter-add | solution.py:114
  380.7 10.3 %collective-permute-start.29 = (f32[4,128,2]{2,0,1:T(4,128)S(1)}, f32[4,128,2]{2,0,1:T(4,128)S(1)}, u32[]{:S(2)}, u32[]{:S(2)}) collective-permute-start(f32[4,128,2]{2,0,1:T(4,128)S(1)} %get-tuple-element.269), channel_id=1, source_target_pairs={{16,0},{32,16},{48,32},{64,48},{80,64},{96,80},{112,96},{128,112},... | collective-permute-start | bytes 12296 | tf_op jit(solution)/shard_map/ppermute | solution.py:19
  391.0 4.5 collective-permute-start.28
  396.2 31.2 %collective-permute-done.29 = f32[4,128,2]{2,0,1:T(4,128)S(1)} collective-permute-done((f32[4,128,2]{2,0,1:T(4,128)S(1)}, f32[4,128,2]{2,0,1:T(4,128)S(1)}, u32[]{:S(2)}, u32[]{:S(2)}) %collective-permute-start.29) | collective-permute-done | bytes 4128 | tf_op jit(solution)/shard_map/ppermute | solution.py:19
  428.6 8.0 %collective-permute-start.31 = (f32[4,2,132]{2,0,1:T(4,128)S(1)}, f32[4,2,132]{2,0,1:T(4,128)S(1)}, u32[]{:S(2)}, u32[]{:S(2)}) collective-permute-start(f32[4,2,132]{2,0,1:T(4,128)S(1)} %get-tuple-element.228), channel_id=1, source_target_pairs={{1,0},{2,1},{3,2},{4,3},{5,4},{6,5},{7,6},{8,7},{9,8},{10,9},{11,1... | collective-permute-start | bytes 12680 | tf_op jit(solution)/shard_map/ppermute | solution.py:19
  436.6 1.9 collective-permute-start.30
  438.6 10.3 %collective-permute-done.30 = f32[4,2,132]{2,0,1:T(4,128)S(1)} collective-permute-done((f32[4,2,132]{2,0,1:T(4,128)S(1)}, f32[4,2,132]{2,0,1:T(4,128)S(1)}, u32[]{:S(2)}, u32[]{:S(2)}) %collective-permute-start.30) | collective-permute-done | bytes 4256 | tf_op jit(solution)/shard_map/ppermute | solution.py:16
  449.8 10.2 %collective-permute-start.33 = (f32[4,128,2]{2,0,1:T(4,128)S(1)}, f32[4,128,2]{2,0,1:T(4,128)S(1)}, u32[]{:S(2)}, u32[]{:S(2)}) collective-permute-start(f32[4,128,2]{2,0,1:T(4,128)S(1)} %get-tuple-element.266), channel_id=1, source_target_pairs={{16,0},{32,16},{48,32},{64,48},{80,64},{96,80},{112,96},{128,112},... | collective-permute-start | bytes 12296 | tf_op jit(solution)/shard_map/ppermute | solution.py:19
  460.0 6.3 collective-permute-start.32
  468.0 9.7 %collective-permute-done.33 = f32[4,128,2]{2,0,1:T(4,128)S(1)} collective-permute-done((f32[4,128,2]{2,0,1:T(4,128)S(1)}, f32[4,128,2]{2,0,1:T(4,128)S(1)}, u32[]{:S(2)}, u32[]{:S(2)}) %collective-permute-start.33) | collective-permute-done | bytes 4128 | tf_op jit(solution)/shard_map/ppermute | solution.py:19
  477.6 2.6 collective-permute-done.32
  480.7 20.7 %collective-permute-start.35 = (f32[4,2,132]{2,0,1:T(4,128)S(1)}, f32[4,2,132]{2,0,1:T(4,128)S(1)}, u32[]{:S(2)}, u32[]{:S(2)}) collective-permute-start(f32[4,2,132]{2,0,1:T(4,128)S(1)} %get-tuple-element.250), channel_id=1, source_target_pairs={{1,0},{2,1},{3,2},{4,3},{5,4},{6,5},{7,6},{8,7},{9,8},{10,9},{11,1... | collective-permute-start | bytes 12680 | tf_op jit(solution)/shard_map/ppermute | solution.py:19
  501.4 1.9 collective-permute-start.34
  503.8 9.2 %collective-permute-done.34 = f32[4,2,132]{2,0,1:T(4,128)S(1)} collective-permute-done((f32[4,2,132]{2,0,1:T(4,128)S(1)}, f32[4,2,132]{2,0,1:T(4,128)S(1)}, u32[]{:S(2)}, u32[]{:S(2)}) %collective-permute-start.34) | collective-permute-done | bytes 4256 | tf_op jit(solution)/shard_map/ppermute | solution.py:16
  519.6 9.3 %collective-permute-start.37 = (f32[1,132,2]{2,1,0:T(8,128)S(1)}, f32[1,132,2]{2,1,0:T(8,128)S(1)}, u32[]{:S(2)}, u32[]{:S(2)}) collective-permute-start(f32[1,132,2]{2,1,0:T(8,128)S(1)} %get-tuple-element.283), channel_id=1, source_target_pairs={{16,0},{32,16},{48,32},{64,48},{80,64},{96,80},{112,96},{128,112},... | collective-permute-start | bytes 3176 | tf_op jit(solution)/shard_map/ppermute | solution.py:19
  528.9 5.2 collective-permute-start.36
  535.3 12.3 %collective-permute-start.21 = (f32[4,132,2]{2,0,1:T(4,128)S(1)}, f32[4,132,2]{2,0,1:T(4,128)S(1)}, u32[]{:S(2)}, u32[]{:S(2)}) collective-permute-start(f32[4,132,2]{2,0,1:T(4,128)S(1)} %get-tuple-element.246), channel_id=1, source_target_pairs={{16,0},{32,16},{48,32},{64,48},{80,64},{96,80},{112,96},{128,112},... | collective-permute-start | bytes 12680 | tf_op jit(solution)/shard_map/ppermute | solution.py:19
  547.6 2.2 collective-permute-start.20
  552.0 10.2 %collective-permute-start.39 = (f32[1,2,136]{2,1,0:T(2,128)S(1)}, f32[1,2,136]{2,1,0:T(2,128)S(1)}, u32[]{:S(2)}, u32[]{:S(2)}) collective-permute-start(f32[1,2,136]{2,1,0:T(2,128)S(1)} %get-tuple-element.262), channel_id=1, source_target_pairs={{1,0},{2,1},{3,2},{4,3},{5,4},{6,5},{7,6},{8,7},{9,8},{10,9},{11,1... | collective-permute-start | bytes 3272 | tf_op jit(solution)/shard_map/ppermute | solution.py:19
  562.3 19.8 %collective-permute-done.38 = f32[1,2,136]{2,1,0:T(2,128)S(1)} collective-permute-done((f32[1,2,136]{2,1,0:T(2,128)S(1)}, f32[1,2,136]{2,1,0:T(2,128)S(1)}, u32[]{:S(2)}, u32[]{:S(2)}) %collective-permute-start.38) | collective-permute-done | bytes 1120 | tf_op jit(solution)/shard_map/ppermute | solution.py:16
  583.5 6.2 collective-permute-done.20
  589.8 1.9 collective-permute-start.22
  592.3 10.5 %collective-permute-start.23 = (f32[4,2,136]{2,0,1:T(4,128)S(1)}, f32[4,2,136]{2,0,1:T(4,128)S(1)}, u32[]{:S(2)}, u32[]{:S(2)}) collective-permute-start(f32[4,2,136]{2,0,1:T(4,128)S(1)} %get-tuple-element.223), channel_id=1, source_target_pairs={{1,0},{2,1},{3,2},{4,3},{5,4},{6,5},{7,6},{8,7},{9,8},{10,9},{11,1... | collective-permute-start | bytes 13064 | tf_op jit(solution)/shard_map/ppermute | solution.py:19
  604.3 4.2 scatter-add.64
  608.9 21.4 %scatter-add.65 = f32[4,1,128,128]{3,0,2,1:T(4,128)S(1)} dynamic-update-slice(f32[4,1,128,128]{3,0,2,1:T(4,128)S(1)} %bitcast.82, f32[4,1,128,2]{3,0,2,1:T(4,128)S(1)} %fusion.29, s32[]{:T(128)} %constant.414.clone.1, s32[]{:T(128)} %constant.414.clone.1, s32[]{:T(128)} %constant.414.clone.1, s32[]{:T(128)} %constant.425.clone.1) | dynamic-update-slice | bytes 8196 | tf_op jit(solution)/shard_map/scatter-add | solution.py:114
  (198 shorter events, 44.1 us)
Async XLA Ops:
  0.6 54.9 %copy-start = (f32[8,4]{0,1:T(4,128)S(1)}, f32[8,4]{0,1:T(4,128)}, u32[]{:S(2)}) copy-start(f32[8,4]{0,1:T(4,128)} %param.53) | copy-start | bytes 388
  0.6 21.1 %copy-start.20 = (f32[4,1,128,128]{3,2,1,0:T(8,128)S(1)}, f32[4,1,128,128]{3,2,1,0:T(8,128)}, u32[]{:S(2)}) copy-start(f32[4,1,128,128]{3,2,1,0:T(8,128)} %param.43) | copy-start | bytes 786436
  1.7 56.9 %collective-permute-start.9 = (f32[1,128,2]{2,1,0:T(8,128)S(1)}, f32[1,128,2]{2,1,0:T(8,128)S(1)}, u32[]{:S(2)}, u32[]{:S(2)}) collective-permute-start(f32[1,128,2]{2,1,0:T(8,128)S(1)} %get-tuple-element.297), channel_id=1, source_target_pairs={{16,0},{32,16},{48,32},{64,48},{80,64},{96,80},{112,96},{128,112},... | collective-permute-start | bytes 3080 | tf_op jit(solution)/shard_map/ppermute | solution.py:19
  19.8 40.7 %collective-permute-start.8 = (f32[1,128,2]{2,1,0:T(8,128)S(1)}, f32[1,128,2]{2,1,0:T(8,128)S(1)}, u32[]{:S(2)}, u32[]{:S(2)}) collective-permute-start(f32[1,128,2]{2,1,0:T(8,128)S(1)} %get-tuple-element.296), channel_id=1, source_target_pairs={{0,16},{16,32},{32,48},{48,64},{64,80},{80,96},{96,112},{112,128},... | collective-permute-start | bytes 3080 | tf_op jit(solution)/shard_map/ppermute | solution.py:16
  21.9 17.8 %copy-start.21 = (f32[1,128,128]{2,1,0:T(8,128)S(1)}, f32[1,128,128]{2,1,0:T(8,128)}, u32[]{:S(2)}) copy-start(f32[1,128,128]{2,1,0:T(8,128)} %param.45) | copy-start | bytes 196612
  21.9 17.8 %copy-start.22 = (s32[1,128,128]{2,1,0:T(8,128)S(1)}, s32[1,128,128]{2,1,0:T(8,128)}, u32[]{:S(2)}) copy-start(s32[1,128,128]{2,1,0:T(8,128)} %param.47) | copy-start | bytes 196612
  22.1 143.9 %collective-permute-start.25 = (f32[4,128,2]{2,0,1:T(4,128)S(1)}, f32[4,128,2]{2,0,1:T(4,128)S(1)}, u32[]{:S(2)}, u32[]{:S(2)}) collective-permute-start(f32[4,128,2]{2,0,1:T(4,128)S(1)} %get-tuple-element.271), channel_id=1, source_target_pairs={{16,0},{32,16},{48,32},{64,48},{80,64},{96,80},{112,96},{128,112},... | collective-permute-start | bytes 12296 | tf_op jit(solution)/shard_map/ppermute | solution.py:19
  37.8 128.3 %collective-permute-start.24 = (f32[4,128,2]{2,0,1:T(4,128)S(1)}, f32[4,128,2]{2,0,1:T(4,128)S(1)}, u32[]{:S(2)}, u32[]{:S(2)}) collective-permute-start(f32[4,128,2]{2,0,1:T(4,128)S(1)} %get-tuple-element.270), channel_id=1, source_target_pairs={{0,16},{16,32},{32,48},{48,64},{64,80},{80,96},{96,112},{112,128},... | collective-permute-start | bytes 12296 | tf_op jit(solution)/shard_map/ppermute | solution.py:16
  39.8 15.8 %copy-start.23 = (s32[128,128]{1,0:T(8,128)S(1)}, s32[128,128]{1,0:T(8,128)}, u32[]{:S(2)}) copy-start(s32[128,128]{1,0:T(8,128)} %param.50) | copy-start | bytes 196612
  39.9 36.4 %collective-permute-start.13 = (f32[1,128,2]{2,1,0:T(8,128)S(1)}, f32[1,128,2]{2,1,0:T(8,128)S(1)}, u32[]{:S(2)}, u32[]{:S(2)}) collective-permute-start(f32[1,128,2]{2,1,0:T(8,128)S(1)} %get-tuple-element.299), channel_id=1, source_target_pairs={{16,0},{32,16},{48,32},{64,48},{80,64},{96,80},{112,96},{128,112},... | collective-permute-start | bytes 3080 | tf_op jit(solution)/shard_map/ppermute | solution.py:19
  57.8 18.4 %copy-start.6 = (f32[1,128,128]{2,1,0:T(8,128)S(1)}, f32[1,128,128]{2,1,0:T(8,128)}, u32[]{:S(2)}) copy-start(f32[1,128,128]{2,1,0:T(8,128)} %param.49) | copy-start | bytes 196612
  58.4 144.9 %copy-start.27 = (pred[132]{0:T(512)(128)(4,1)}, pred[132]{0:T(512)(128)(4,1)S(1)}, u32[]{:S(2)}) copy-start(pred[132]{0:T(512)(128)(4,1)S(1)} %compare_and_fusion) | copy-start | bytes 400
  58.5 141.3 %copy-start.30 = (pred[128]{0:T(512)(128)(4,1)}, pred[128]{0:T(512)(128)(4,1)S(1)}, u32[]{:S(2)}) copy-start(pred[128]{0:T(512)(128)(4,1)S(1)} %slice.828) | copy-start | bytes 388
  58.6 31.4 %collective-permute-start.12 = (f32[1,128,2]{2,1,0:T(8,128)S(1)}, f32[1,128,2]{2,1,0:T(8,128)S(1)}, u32[]{:S(2)}, u32[]{:S(2)}) collective-permute-start(f32[1,128,2]{2,1,0:T(8,128)S(1)} %get-tuple-element.298), channel_id=1, source_target_pairs={{0,16},{16,32},{32,48},{48,64},{64,80},{80,96},{96,112},{112,128},... | collective-permute-start | bytes 3080 | tf_op jit(solution)/shard_map/ppermute | solution.py:16
  60.5 110.6 %collective-permute-start.1 = (f32[4,128,2]{2,0,1:T(4,128)}, f32[4,128,2]{2,0,1:T(4,128)S(1)}, u32[]{:S(2)}, u32[]{:S(2)}) collective-permute-start(f32[4,128,2]{2,0,1:T(4,128)} %get-tuple-element.275), channel_id=1, source_target_pairs={{16,0},{32,16},{48,32},{64,48},{80,64},{96,80},{112,96},{128,112},... | collective-permute-start | bytes 12296 | tf_op jit(solution)/shard_map/ppermute | solution.py:19
  76.3 43.0 %collective-permute-start.5 = (f32[1,128,2]{2,1,0:T(8,128)S(1)}, f32[1,128,2]{2,1,0:T(8,128)S(1)}, u32[]{:S(2)}, u32[]{:S(2)}) collective-permute-start(f32[1,128,2]{2,1,0:T(8,128)S(1)} %get-tuple-element.295), channel_id=1, source_target_pairs={{16,0},{32,16},{48,32},{64,48},{80,64},{96,80},{112,96},{128,112},... | collective-permute-start | bytes 3080 | tf_op jit(solution)/shard_map/ppermute | solution.py:19
  90.0 35.4 %collective-permute-start.4 = (f32[1,128,2]{2,1,0:T(8,128)S(1)}, f32[1,128,2]{2,1,0:T(8,128)S(1)}, u32[]{:S(2)}, u32[]{:S(2)}) collective-permute-start(f32[1,128,2]{2,1,0:T(8,128)S(1)} %get-tuple-element.294), channel_id=1, source_target_pairs={{0,16},{16,32},{32,48},{48,64},{64,80},{80,96},{96,112},{112,128},... | collective-permute-start | bytes 3080 | tf_op jit(solution)/shard_map/ppermute | solution.py:16
  119.3 8.1 %collective-permute-start.11 = (f32[1,2,132]{2,1,0:T(2,128)S(1)}, f32[1,2,132]{2,1,0:T(2,128)S(1)}, u32[]{:S(2)}, u32[]{:S(2)}) collective-permute-start(f32[1,2,132]{2,1,0:T(2,128)S(1)} %get-tuple-element.279), channel_id=1, source_target_pairs={{1,0},{2,1},{3,2},{4,3},{5,4},{6,5},{7,6},{8,7},{9,8},{10,9},{11,1... | collective-permute-start | bytes 3176 | tf_op jit(solution)/shard_map/ppermute | solution.py:19
  125.4 12.3 %collective-permute-start.10 = (f32[1,2,132]{2,1,0:T(2,128)S(1)}, f32[1,2,132]{2,1,0:T(2,128)S(1)}, u32[]{:S(2)}, u32[]{:S(2)}) collective-permute-start(f32[1,2,132]{2,1,0:T(2,128)S(1)} %get-tuple-element.278), channel_id=1, source_target_pairs={{0,1},{1,2},{2,3},{3,4},{4,5},{5,6},{6,7},{7,8},{8,9},{9,10},{10,1... | collective-permute-start | bytes 3176 | tf_op jit(solution)/shard_map/ppermute | solution.py:16
  127.4 12.3 %collective-permute-start.15 = (f32[1,2,132]{2,1,0:T(2,128)S(1)}, f32[1,2,132]{2,1,0:T(2,128)S(1)}, u32[]{:S(2)}, u32[]{:S(2)}) collective-permute-start(f32[1,2,132]{2,1,0:T(2,128)S(1)} %get-tuple-element.281), channel_id=1, source_target_pairs={{1,0},{2,1},{3,2},{4,3},{5,4},{6,5},{7,6},{8,7},{9,8},{10,9},{11,1... | collective-permute-start | bytes 3176 | tf_op jit(solution)/shard_map/ppermute | solution.py:19
  137.7 12.3 %collective-permute-start.14 = (f32[1,2,132]{2,1,0:T(2,128)S(1)}, f32[1,2,132]{2,1,0:T(2,128)S(1)}, u32[]{:S(2)}, u32[]{:S(2)}) collective-permute-start(f32[1,2,132]{2,1,0:T(2,128)S(1)} %get-tuple-element.280), channel_id=1, source_target_pairs={{0,1},{1,2},{2,3},{3,4},{4,5},{5,6},{6,7},{7,8},{8,9},{9,10},{10,1... | collective-permute-start | bytes 3176 | tf_op jit(solution)/shard_map/ppermute | solution.py:16
  139.7 12.5 %collective-permute-start.7 = (f32[1,2,132]{2,1,0:T(2,128)S(1)}, f32[1,2,132]{2,1,0:T(2,128)S(1)}, u32[]{:S(2)}, u32[]{:S(2)}) collective-permute-start(f32[1,2,132]{2,1,0:T(2,128)S(1)} %get-tuple-element.277), channel_id=1, source_target_pairs={{1,0},{2,1},{3,2},{4,3},{5,4},{6,5},{7,6},{8,7},{9,8},{10,9},{11,1... | collective-permute-start | bytes 3176 | tf_op jit(solution)/shard_map/ppermute | solution.py:19
  150.0 15.2 %collective-permute-start.6 = (f32[1,2,132]{2,1,0:T(2,128)S(1)}, f32[1,2,132]{2,1,0:T(2,128)S(1)}, u32[]{:S(2)}, u32[]{:S(2)}) collective-permute-start(f32[1,2,132]{2,1,0:T(2,128)S(1)} %get-tuple-element.276), channel_id=1, source_target_pairs={{0,1},{1,2},{2,3},{3,4},{4,5},{5,6},{6,7},{7,8},{8,9},{9,10},{10,1... | collective-permute-start | bytes 3176 | tf_op jit(solution)/shard_map/ppermute | solution.py:16
  152.2 31.8 %collective-permute-start = (f32[4,128,2]{2,0,1:T(4,128)}, f32[4,128,2]{2,0,1:T(4,128)S(1)}, u32[]{:S(2)}, u32[]{:S(2)}) collective-permute-start(f32[4,128,2]{2,0,1:T(4,128)} %get-tuple-element.274), channel_id=1, source_target_pairs={{0,16},{16,32},{32,48},{48,64},{64,80},{80,96},{96,112},{112,128},... | collective-permute-start | bytes 12296 | tf_op jit(solution)/shard_map/ppermute | solution.py:16
  166.1 128.9 %copy-start.7 = (f32[128,128]{1,0:T(8,128)}, f32[128,128]{1,0:T(8,128)S(1)}, u32[]{:S(2)}) copy-start(f32[128,128]{1,0:T(8,128)S(1)} %slice_bitcast_fusion) | copy-start | bytes 196612
  166.6 36.8 %collective-permute-start.27 = (f32[4,2,132]{2,0,1:T(4,128)S(1)}, f32[4,2,132]{2,0,1:T(4,128)S(1)}, u32[]{:S(2)}, u32[]{:S(2)}) collective-permute-start(f32[4,2,132]{2,0,1:T(4,128)S(1)} %get-tuple-element.252), channel_id=1, source_target_pairs={{1,0},{2,1},{3,2},{4,3},{5,4},{6,5},{7,6},{8,7},{9,8},{10,9},{11,1... | collective-permute-start | bytes 12680 | tf_op jit(solution)/shard_map/ppermute | solution.py:19
  169.2 34.1 %collective-permute-start.26 = (f32[4,2,132]{2,0,1:T(4,128)S(1)}, f32[4,2,132]{2,0,1:T(4,128)S(1)}, u32[]{:S(2)}, u32[]{:S(2)}) collective-permute-start(f32[4,2,132]{2,0,1:T(4,128)S(1)} %get-tuple-element.251), channel_id=1, source_target_pairs={{0,1},{1,2},{2,3},{3,4},{4,5},{5,6},{6,7},{7,8},{8,9},{9,10},{10,1... | collective-permute-start | bytes 12680 | tf_op jit(solution)/shard_map/ppermute | solution.py:16
  184.1 6.6 %collective-permute-start.3 = (f32[4,2,132]{2,0,1:T(4,128)S(1)}, f32[4,2,132]{2,0,1:T(4,128)S(1)}, u32[]{:S(2)}, u32[]{:S(2)}) collective-permute-start(f32[4,2,132]{2,0,1:T(4,128)S(1)} %get-tuple-element.230), channel_id=1, source_target_pairs={{1,0},{2,1},{3,2},{4,3},{5,4},{6,5},{7,6},{8,7},{9,8},{10,9},{11,1... | collective-permute-start | bytes 12680 | tf_op jit(solution)/shard_map/ppermute | solution.py:19
  188.1 11.7 %copy-start.11 = (f32[4,1,128,128]{3,2,1,0:T(8,128)S(1)}, f32[4,1,128,128]{3,2,1,0:T(8,128)}, u32[]{:S(2)}) copy-start(f32[4,1,128,128]{3,2,1,0:T(8,128)} %param.44) | copy-start | bytes 786436
  188.1 11.7 %collective-permute-start.2 = (f32[4,2,132]{2,0,1:T(4,128)S(1)}, f32[4,2,132]{2,0,1:T(4,128)S(1)}, u32[]{:S(2)}, u32[]{:S(2)}) collective-permute-start(f32[4,2,132]{2,0,1:T(4,128)S(1)} %get-tuple-element.229), channel_id=1, source_target_pairs={{0,1},{1,2},{2,3},{3,4},{4,5},{5,6},{6,7},{7,8},{8,9},{9,10},{10,1... | collective-permute-start | bytes 12680 | tf_op jit(solution)/shard_map/ppermute | solution.py:16
  204.4 21.8 %collective-permute-start.17 = (f32[4,132,2]{2,0,1:T(4,128)S(1)}, f32[4,132,2]{2,0,1:T(4,128)S(1)}, u32[]{:S(2)}, u32[]{:S(2)}) collective-permute-start(f32[4,132,2]{2,0,1:T(4,128)S(1)} %get-tuple-element.248), channel_id=1, source_target_pairs={{16,0},{32,16},{48,32},{64,48},{80,64},{96,80},{112,96},{128,112},... | collective-permute-start | bytes 12680 | tf_op jit(solution)/shard_map/ppermute | solution.py:19
  209.7 44.8 %collective-permute-start.16 = (f32[4,132,2]{2,0,1:T(4,128)S(1)}, f32[4,132,2]{2,0,1:T(4,128)S(1)}, u32[]{:S(2)}, u32[]{:S(2)}) collective-permute-start(f32[4,132,2]{2,0,1:T(4,128)S(1)} %get-tuple-element.247), channel_id=1, source_target_pairs={{0,16},{16,32},{32,48},{48,64},{64,80},{80,96},{96,112},{112,128},... | collective-permute-start | bytes 12680 | tf_op jit(solution)/shard_map/ppermute | solution.py:16
  254.5 12.9 %collective-permute-start.18 = (f32[4,2,136]{2,0,1:T(4,128)S(1)}, f32[4,2,136]{2,0,1:T(4,128)S(1)}, u32[]{:S(2)}, u32[]{:S(2)}) collective-permute-start(f32[4,2,136]{2,0,1:T(4,128)S(1)} %get-tuple-element.226), channel_id=1, source_target_pairs={{0,1},{1,2},{2,3},{3,4},{4,5},{5,6},{6,7},{7,8},{8,9},{9,10},{10,1... | collective-permute-start | bytes 13064 | tf_op jit(solution)/shard_map/ppermute | solution.py:16
  257.0 11.6 %collective-permute-start.19 = (f32[4,2,136]{2,0,1:T(4,128)S(1)}, f32[4,2,136]{2,0,1:T(4,128)S(1)}, u32[]{:S(2)}, u32[]{:S(2)}) collective-permute-start(f32[4,2,136]{2,0,1:T(4,128)S(1)} %get-tuple-element.225), channel_id=1, source_target_pairs={{1,0},{2,1},{3,2},{4,3},{5,4},{6,5},{7,6},{8,7},{9,8},{10,9},{11,1... | collective-permute-start | bytes 13064 | tf_op jit(solution)/shard_map/ppermute | solution.py:19
  296.9 38.1 %collective-permute-start.41 = (f32[4,132,2]{2,0,1:T(4,128)S(1)}, f32[4,132,2]{2,0,1:T(4,128)S(1)}, u32[]{:S(2)}, u32[]{:S(2)}) collective-permute-start(f32[4,132,2]{2,0,1:T(4,128)S(1)} %get-tuple-element.244), channel_id=1, source_target_pairs={{16,0},{32,16},{48,32},{64,48},{80,64},{96,80},{112,96},{128,112},... | collective-permute-start | bytes 12680 | tf_op jit(solution)/shard_map/ppermute | solution.py:19
  304.9 34.8 %collective-permute-start.40 = (f32[4,132,2]{2,0,1:T(4,128)S(1)}, f32[4,132,2]{2,0,1:T(4,128)S(1)}, u32[]{:S(2)}, u32[]{:S(2)}) collective-permute-start(f32[4,132,2]{2,0,1:T(4,128)S(1)} %get-tuple-element.243), channel_id=1, source_target_pairs={{0,16},{16,32},{32,48},{48,64},{64,80},{80,96},{96,112},{112,128},... | collective-permute-start | bytes 12680 | tf_op jit(solution)/shard_map/ppermute | solution.py:16
  339.7 12.7 %collective-permute-start.42 = (f32[4,2,136]{2,0,1:T(4,128)S(1)}, f32[4,2,136]{2,0,1:T(4,128)S(1)}, u32[]{:S(2)}, u32[]{:S(2)}) collective-permute-start(f32[4,2,136]{2,0,1:T(4,128)S(1)} %get-tuple-element.222), channel_id=1, source_target_pairs={{0,1},{1,2},{2,3},{3,4},{4,5},{5,6},{6,7},{7,8},{8,9},{9,10},{10,1... | collective-permute-start | bytes 13064 | tf_op jit(solution)/shard_map/ppermute | solution.py:16
  342.2 11.6 %collective-permute-start.43 = (f32[4,2,136]{2,0,1:T(4,128)S(1)}, f32[4,2,136]{2,0,1:T(4,128)S(1)}, u32[]{:S(2)}, u32[]{:S(2)}) collective-permute-start(f32[4,2,136]{2,0,1:T(4,128)S(1)} %get-tuple-element.221), channel_id=1, source_target_pairs={{1,0},{2,1},{3,2},{4,3},{5,4},{6,5},{7,6},{8,7},{9,8},{10,9},{11,1... | collective-permute-start | bytes 13064 | tf_op jit(solution)/shard_map/ppermute | solution.py:19
  358.8 21.4 %copy-start.17 = (f32[4,128,128]{2,1,0:T(8,128)S(1)}, f32[4,128,128]{2,1,0:T(8,128)}, u32[]{:S(2)}) copy-start(f32[4,128,128]{2,1,0:T(8,128)} %param.52) | copy-start | bytes 786436
  358.8 21.4 %copy-start.18 = (f32[128,128]{1,0:T(8,128)S(1)}, f32[128,128]{1,0:T(8,128)}, u32[]{:S(2)}) copy-start(f32[128,128]{1,0:T(8,128)} %convert_multiply_fusion) | copy-start | bytes 196612
  380.7 46.6 %collective-permute-start.29 = (f32[4,128,2]{2,0,1:T(4,128)S(1)}, f32[4,128,2]{2,0,1:T(4,128)S(1)}, u32[]{:S(2)}, u32[]{:S(2)}) collective-permute-start(f32[4,128,2]{2,0,1:T(4,128)S(1)} %get-tuple-element.269), channel_id=1, source_target_pairs={{16,0},{32,16},{48,32},{64,48},{80,64},{96,80},{112,96},{128,112},... | collective-permute-start | bytes 12296 | tf_op jit(solution)/shard_map/ppermute | solution.py:19
  391.0 37.5 %collective-permute-start.28 = (f32[4,128,2]{2,0,1:T(4,128)S(1)}, f32[4,128,2]{2,0,1:T(4,128)S(1)}, u32[]{:S(2)}, u32[]{:S(2)}) collective-permute-start(f32[4,128,2]{2,0,1:T(4,128)S(1)} %get-tuple-element.268), channel_id=1, source_target_pairs={{0,16},{16,32},{32,48},{48,64},{64,80},{80,96},{96,112},{112,128},... | collective-permute-start | bytes 12296 | tf_op jit(solution)/shard_map/ppermute | solution.py:16
  396.2 52.8 %copy-start.1 = (f32[4,1,128,129]{3,0,2,1:T(4,128)S(1)}, f32[4,1,128,129]{3,0,2,1:T(4,128)}, u32[]{:S(2)}) copy-start(f32[4,1,128,129]{3,0,2,1:T(4,128)} %broadcast_multiply_fusion.1) | copy-start | bytes 792580
  428.6 10.0 %collective-permute-start.31 = (f32[4,2,132]{2,0,1:T(4,128)S(1)}, f32[4,2,132]{2,0,1:T(4,128)S(1)}, u32[]{:S(2)}, u32[]{:S(2)}) collective-permute-start(f32[4,2,132]{2,0,1:T(4,128)S(1)} %get-tuple-element.228), channel_id=1, source_target_pairs={{1,0},{2,1},{3,2},{4,3},{5,4},{6,5},{7,6},{8,7},{9,8},{10,9},{11,1... | collective-permute-start | bytes 12680 | tf_op jit(solution)/shard_map/ppermute | solution.py:19
  436.6 12.4 %collective-permute-start.30 = (f32[4,2,132]{2,0,1:T(4,128)S(1)}, f32[4,2,132]{2,0,1:T(4,128)S(1)}, u32[]{:S(2)}, u32[]{:S(2)}) collective-permute-start(f32[4,2,132]{2,0,1:T(4,128)S(1)} %get-tuple-element.227), channel_id=1, source_target_pairs={{0,1},{1,2},{2,3},{3,4},{4,5},{5,6},{6,7},{7,8},{8,9},{9,10},{10,1... | collective-permute-start | bytes 12680 | tf_op jit(solution)/shard_map/ppermute | solution.py:16
  438.5 10.4 %copy-start.8 = (f32[128,128]{1,0:T(8,128)S(1)}, f32[128,128]{1,0:T(8,128)}, u32[]{:S(2)}) copy-start(f32[128,128]{1,0:T(8,128)} %copy-done.7) | copy-start | bytes 196612
  438.5 10.4 %copy-start.9 = (f32[4,128,128]{2,0,1:T(4,128)S(1)}, f32[4,128,128]{2,0,1:T(4,128)}, u32[]{:S(2)}) copy-start(f32[4,128,128]{2,0,1:T(4,128)} %get-tuple-element.212) | copy-start | bytes 786436
  438.6 10.4 %copy-start.31 = (pred[128]{0:T(512)(128)(4,1)S(1)}, pred[128]{0:T(512)(128)(4,1)}, u32[]{:S(2)}) copy-start(pred[128]{0:T(512)(128)(4,1)} %copy-done.30) | copy-start | bytes 388
  449.0 17.4 %copy-start.4 = (f32[4,1,128,129]{3,0,2,1:T(4,128)S(1)}, f32[4,1,128,129]{3,0,2,1:T(4,128)}, u32[]{:S(2)}) copy-start(f32[4,1,128,129]{3,0,2,1:T(4,128)} %get-tuple-element.241) | copy-start | bytes 792580
  449.0 17.4 %copy-start.5 = (f32[4,1,128,129]{3,0,2,1:T(4,128)S(1)}, f32[4,1,128,129]{3,0,2,1:T(4,128)}, u32[]{:S(2)}) copy-start(f32[4,1,128,129]{3,0,2,1:T(4,128)} %get-tuple-element.242) | copy-start | bytes 792580
  449.6 16.7 %copy-start.2 = (f32[4,1,128,129]{3,0,2,1:T(4,128)S(1)}, f32[4,1,128,129]{3,0,2,1:T(4,128)}, u32[]{:S(2)}) copy-start(f32[4,1,128,129]{3,0,2,1:T(4,128)} %get-tuple-element.239) | copy-start | bytes 792580
  449.6 16.7 %copy-start.3 = (f32[4,1,128,129]{3,0,2,1:T(4,128)S(1)}, f32[4,1,128,129]{3,0,2,1:T(4,128)}, u32[]{:S(2)}) copy-start(f32[4,1,128,129]{3,0,2,1:T(4,128)} %get-tuple-element.240) | copy-start | bytes 792580
  449.8 27.8 %collective-permute-start.33 = (f32[4,128,2]{2,0,1:T(4,128)S(1)}, f32[4,128,2]{2,0,1:T(4,128)S(1)}, u32[]{:S(2)}, u32[]{:S(2)}) collective-permute-start(f32[4,128,2]{2,0,1:T(4,128)S(1)} %get-tuple-element.266), channel_id=1, source_target_pairs={{16,0},{32,16},{48,32},{64,48},{80,64},{96,80},{112,96},{128,112},... | collective-permute-start | bytes 12296 | tf_op jit(solution)/shard_map/ppermute | solution.py:19
  460.0 20.2 %collective-permute-start.32 = (f32[4,128,2]{2,0,1:T(4,128)S(1)}, f32[4,128,2]{2,0,1:T(4,128)S(1)}, u32[]{:S(2)}, u32[]{:S(2)}) collective-permute-start(f32[4,128,2]{2,0,1:T(4,128)S(1)} %get-tuple-element.265), channel_id=1, source_target_pairs={{0,16},{16,32},{32,48},{48,64},{64,80},{80,96},{96,112},{112,128},... | collective-permute-start | bytes 12296 | tf_op jit(solution)/shard_map/ppermute | solution.py:16
  480.7 23.1 %collective-permute-start.35 = (f32[4,2,132]{2,0,1:T(4,128)S(1)}, f32[4,2,132]{2,0,1:T(4,128)S(1)}, u32[]{:S(2)}, u32[]{:S(2)}) collective-permute-start(f32[4,2,132]{2,0,1:T(4,128)S(1)} %get-tuple-element.250), channel_id=1, source_target_pairs={{1,0},{2,1},{3,2},{4,3},{5,4},{6,5},{7,6},{8,7},{9,8},{10,9},{11,1... | collective-permute-start | bytes 12680 | tf_op jit(solution)/shard_map/ppermute | solution.py:19
  501.4 11.6 %collective-permute-start.34 = (f32[4,2,132]{2,0,1:T(4,128)S(1)}, f32[4,2,132]{2,0,1:T(4,128)S(1)}, u32[]{:S(2)}, u32[]{:S(2)}) collective-permute-start(f32[4,2,132]{2,0,1:T(4,128)S(1)} %get-tuple-element.249), channel_id=1, source_target_pairs={{0,1},{1,2},{2,3},{3,4},{4,5},{5,6},{6,7},{7,8},{8,9},{9,10},{10,1... | collective-permute-start | bytes 12680 | tf_op jit(solution)/shard_map/ppermute | solution.py:16
  519.6 30.3 %collective-permute-start.37 = (f32[1,132,2]{2,1,0:T(8,128)S(1)}, f32[1,132,2]{2,1,0:T(8,128)S(1)}, u32[]{:S(2)}, u32[]{:S(2)}) collective-permute-start(f32[1,132,2]{2,1,0:T(8,128)S(1)} %get-tuple-element.283), channel_id=1, source_target_pairs={{16,0},{32,16},{48,32},{64,48},{80,64},{96,80},{112,96},{128,112},... | collective-permute-start | bytes 3176 | tf_op jit(solution)/shard_map/ppermute | solution.py:19
  528.9 20.9 %collective-permute-start.36 = (f32[1,132,2]{2,1,0:T(8,128)S(1)}, f32[1,132,2]{2,1,0:T(8,128)S(1)}, u32[]{:S(2)}, u32[]{:S(2)}) collective-permute-start(f32[1,132,2]{2,1,0:T(8,128)S(1)} %get-tuple-element.282), channel_id=1, source_target_pairs={{0,16},{16,32},{32,48},{48,64},{64,80},{80,96},{96,112},{112,128},... | collective-permute-start | bytes 3176 | tf_op jit(solution)/shard_map/ppermute | solution.py:16
  535.3 48.2 %collective-permute-start.21 = (f32[4,132,2]{2,0,1:T(4,128)S(1)}, f32[4,132,2]{2,0,1:T(4,128)S(1)}, u32[]{:S(2)}, u32[]{:S(2)}) collective-permute-start(f32[4,132,2]{2,0,1:T(4,128)S(1)} %get-tuple-element.246), channel_id=1, source_target_pairs={{16,0},{32,16},{48,32},{64,48},{80,64},{96,80},{112,96},{128,112},... | collective-permute-start | bytes 12680 | tf_op jit(solution)/shard_map/ppermute | solution.py:19
  547.6 42.1 %collective-permute-start.20 = (f32[4,132,2]{2,0,1:T(4,128)S(1)}, f32[4,132,2]{2,0,1:T(4,128)S(1)}, u32[]{:S(2)}, u32[]{:S(2)}) collective-permute-start(f32[4,132,2]{2,0,1:T(4,128)S(1)} %get-tuple-element.245), channel_id=1, source_target_pairs={{0,16},{16,32},{32,48},{48,64},{64,80},{80,96},{96,112},{112,128},... | collective-permute-start | bytes 12680 | tf_op jit(solution)/shard_map/ppermute | solution.py:16
  550.0 32.2 %collective-permute-start.38 = (f32[1,2,136]{2,1,0:T(2,128)S(1)}, f32[1,2,136]{2,1,0:T(2,128)S(1)}, u32[]{:S(2)}, u32[]{:S(2)}) collective-permute-start(f32[1,2,136]{2,1,0:T(2,128)S(1)} %get-tuple-element.263), channel_id=1, source_target_pairs={{0,1},{1,2},{2,3},{3,4},{4,5},{5,6},{6,7},{7,8},{8,9},{9,10},{10,1... | collective-permute-start | bytes 3272 | tf_op jit(solution)/shard_map/ppermute | solution.py:16
  552.0 30.2 %collective-permute-start.39 = (f32[1,2,136]{2,1,0:T(2,128)S(1)}, f32[1,2,136]{2,1,0:T(2,128)S(1)}, u32[]{:S(2)}, u32[]{:S(2)}) collective-permute-start(f32[1,2,136]{2,1,0:T(2,128)S(1)} %get-tuple-element.262), channel_id=1, source_target_pairs={{1,0},{2,1},{3,2},{4,3},{5,4},{6,5},{7,6},{8,7},{9,8},{10,9},{11,1... | collective-permute-start | bytes 3272 | tf_op jit(solution)/shard_map/ppermute | solution.py:19
  589.8 13.0 %collective-permute-start.22 = (f32[4,2,136]{2,0,1:T(4,128)S(1)}, f32[4,2,136]{2,0,1:T(4,128)S(1)}, u32[]{:S(2)}, u32[]{:S(2)}) collective-permute-start(f32[4,2,136]{2,0,1:T(4,128)S(1)} %get-tuple-element.224), channel_id=1, source_target_pairs={{0,1},{1,2},{2,3},{3,4},{4,5},{5,6},{6,7},{7,8},{8,9},{9,10},{10,1... | collective-permute-start | bytes 13064 | tf_op jit(solution)/shard_map/ppermute | solution.py:16
  592.3 11.6 %collective-permute-start.23 = (f32[4,2,136]{2,0,1:T(4,128)S(1)}, f32[4,2,136]{2,0,1:T(4,128)S(1)}, u32[]{:S(2)}, u32[]{:S(2)}) collective-permute-start(f32[4,2,136]{2,0,1:T(4,128)S(1)} %get-tuple-element.223), channel_id=1, source_target_pairs={{1,0},{2,1},{3,2},{4,3},{5,4},{6,5},{7,6},{8,7},{9,8},{10,9},{11,1... | collective-permute-start | bytes 13064 | tf_op jit(solution)/shard_map/ppermute | solution.py:19
  (12 other events, 15.7 us)
where the time goes:
time: 633 us; the launch traced here: 631 us
  starting transfers between devices  300 us (47%)
  waiting for transfers between devices  214 us (34%)
  local copies, waits for them, and re-layouts  89 us (14%)
  other arithmetic  25.9 us (4%)
    ppermute x22, starting transfers between devices, with_halo(): lax.ppermute(lax.slice_in_dim(block, 0, width, axis=dim), axis, backward)  231 us
    ppermute x22, waiting for transfers between devices, with_halo(): lax.ppermute(lax.slice_in_dim(block, block.shape[dim] - width, None, axis...  118 us
    ppermute x22, waiting for transfers between devices, with_halo(): lax.ppermute(lax.slice_in_dim(block, 0, width, axis=dim), axis, backward)  96.1 us
    ppermute x22, starting transfers between devices, with_halo(): lax.ppermute(lax.slice_in_dim(block, block.shape[dim] - width, None, axis...  68.7 us
    scatter-add x4, local copies, waits for them, and re-layouts, fold_rim(): result = result.at[..., -margin:].add(central[..., -margin:])  64.8 us
    scatter-add x4, local copies, waits for them, and re-layouts, fold_rim(): result = result.at[..., :margin].add(central[..., :margin])  13 us
  transfers between devices with their start and end apart: 44, of which 20 were waited for; matrix products, arithmetic and copies ran while one was open for 3% of the time, Pallas kernels for 0%

commit v1 on v0

v1 whole, which is shorter than its diff:
```python
import functools

import jax
import jax.numpy as jnp
from jax import lax
from jax.experimental import pallas as pl
from jax.experimental.pallas import tpu as pltpu
from jax.sharding import PartitionSpec as P

COURANT = 0.3
TIME_STEP = 0.25

N = 128
BINS = 4
MAIN = 2 * BINS + 3
EXTRA = BINS + 1
EAST, NORTH, RHO = 2 * BINS, 2 * BINS + 1, 2 * BINS + 2
LINES = 4 * MAIN + 2 * EXTRA
LAT_MSG = 56
LON_MSG = 64
BASE = 16
ROWS = 160
F32 = jnp.float32


def plane_readers(refs, info):
    tracer, adjoint, speed_e, speed_n, sign_e, sign_n, density, land, mask, emission = refs

    def east(at, size):
        s = speed_e[0, pl.ds(at, size), :]
        return jnp.where(sign_e[0, pl.ds(at, size), :] == 1, s, -s)

    def north(at, size):
        s = speed_n[0, pl.ds(at, size), :]
        s = jnp.where(sign_n[0, pl.ds(at, size), :] == 1, s, -s)
        row = lax.broadcasted_iota(jnp.int32, (size, N), 0) + at
        return jnp.where((row == 0) & (info[2] == 1), 0.0, s)

    def source(b):
        def read(at, size):
            m = mask[pl.ds(at, size), :].astype(F32)
            return TIME_STEP * m * emission[b, pl.ds(at, size), :]

        return read

    main = [lambda at, size, b=b: tracer[b, 0, pl.ds(at, size), :] for b in range(BINS)]
    main += [lambda at, size, b=b: adjoint[b, 0, pl.ds(at, size), :] for b in range(BINS)]
    main += [east, north, lambda at, size: density[0, pl.ds(at, size), :]]
    extra = [source(b) for b in range(BINS)]
    extra += [lambda at, size: land[pl.ds(at, size), :].astype(F32)]
    return main, extra


def pack_kernel(info, *refs):
    ins, (out0, out1, lines_out), (edge, packed) = refs[:10], refs[10:13], refs[13:]
    main, extra = plane_readers(ins, info)
    lane = lax.broadcasted_iota(jnp.int32, (N, N), 1)
    for p, read in enumerate(main):
        edge[0, 4 * p : 4 * p + 4, :] = read(0, 8)[:4]
        edge[1, 4 * p : 4 * p + 4, :] = read(N - 8, 8)[4:]
    for q, read in enumerate(extra):
        at = 4 * MAIN + 2 * q
        edge[0, at : at + 2, :] = read(0, 8)[:2]
        edge[1, at : at + 2, :] = read(N - 8, 8)[6:]
    edge[:, LINES:LAT_MSG, :] = jnp.zeros((2, LAT_MSG - LINES, N), F32)
    parity = info[0]
    out0[...] = edge[1 - parity]
    out1[...] = edge[parity]
    both = jnp.zeros((N, N), F32)
    for p, read in enumerate(main):
        turned = pltpu.roll(read(0, N), 8 * p + 4, 1)
        both = jnp.where((lane >= 8 * p) & (lane < 8 * p + 8), turned, both)
    for q, read in enumerate(extra):
        at = 8 * MAIN + 4 * q
        turned = pltpu.roll(read(0, N), at + 2, 1)
        both = jnp.where((lane >= at) & (lane < at + 4), turned, both)
    packed[...] = both.T
    for p in range(MAIN):
        lines_out[1, 4 * p : 4 * p + 4, :] = packed[8 * p : 8 * p + 4, :]
        lines_out[0, 4 * p : 4 * p + 4, :] = packed[8 * p + 4 : 8 * p + 8, :]
    for q in range(EXTRA):
        at, to = 8 * MAIN + 4 * q, 4 * MAIN + 2 * q
        lines_out[1, to : to + 2, :] = packed[at : at + 2, :]
        lines_out[0, to : to + 2, :] = packed[at + 2 : at + 4, :]
    lines_out[:, LINES:LON_MSG, :] = jnp.zeros((2, LON_MSG - LINES, N), F32)


def place_lat(info, got0, got1, halo):
    parity = info[0]
    halo[1 - parity] = got0[...]
    halo[parity] = got1[...]
    at = 4 * RHO

    @pl.when(info[2] == 1)
    def _():
        halo[0, at : at + 4, :] = jnp.ones((4, N), F32)

    @pl.when(info[3] == 1)
    def _():
        halo[1, at : at + 4, :] = jnp.ones((4, N), F32)


def corner_kernel(info, got0, got1, lines, out, halo, rows):
    place_lat(info, got0, got1, halo)
    rows[8 * MAIN :, :] = jnp.zeros((N - 8 * MAIN, N), F32)
    for p in range(MAIN):
        rows[8 * p : 8 * p + 4, :] = halo[0, 4 * p : 4 * p + 4, :]
        rows[8 * p + 4 : 8 * p + 8, :] = halo[1, 4 * p : 4 * p + 4, :]
    turned = rows[...].T
    parity = info[1]
    out[0:LON_MSG, :] = lines[1 - parity]
    out[LON_MSG:, :] = lines[parity]
    left, right = turned[0:8][:4], turned[N - 8 :][4:]

    @pl.when(parity == 0)
    def _():
        out[LINES : LINES + 4, :] = right
        out[LON_MSG + LINES : LON_MSG + LINES + 4, :] = left

    @pl.when(parity == 1)
    def _():
        out[LINES : LINES + 4, :] = left
        out[LON_MSG + LINES : LON_MSG + LINES + 4, :] = right


def main_kernel(info, deposition, *refs):
    ins = refs[:10]
    got0, got1, near, passed = refs[10:14]
    adj_out, dens_out, emis_out = refs[14:17]
    (halo, sides, turn, main, extra, mass, inv, keep, g, middle, second, flux, back, flux2, bank, hn, dens) = refs[17:]
    read_main, read_extra = plane_readers(ins, info)
    lane = lax.broadcasted_iota(jnp.int32, (8, N), 1)

    place_lat(info, got0, got1, halo)
    parity = info[1]
    sides[1 - parity] = near[0:LON_MSG, :]
    sides[parity] = passed[...]
    for p, read in enumerate(read_main):
        main[p, 0, BASE : BASE + N, :] = read(0, N)
        main[p, 0, BASE - 4 : BASE, :] = halo[0, 4 * p : 4 * p + 4, :]
        main[p, 0, BASE + N : BASE + N + 4, :] = halo[1, 4 * p : 4 * p + 4, :]
        turn[8 * p : 8 * p + 4, :] = sides[0, 4 * p : 4 * p + 4, :]
        turn[8 * p + 4 : 8 * p + 8, :] = sides[1, 4 * p : 4 * p + 4, :]
    for q, read in enumerate(read_extra):
        at, to = 4 * MAIN + 2 * q, 8 * MAIN + 4 * q
        extra[q, 0, BASE : BASE + N, :] = read(0, N)
        extra[q, 0, BASE - 2 : BASE, :] = halo[0, at : at + 2, :]
        extra[q, 0, BASE + N : BASE + N + 2, :] = halo[1, at : at + 2, :]
        turn[to : to + 2, :] = sides[0, at : at + 2, :]
        turn[to + 2 : to + 4, :] = sides[1, at : at + 2, :]
    at = 8 * MAIN + 4 * EXTRA
    turn[at:, :] = jnp.zeros((N - at, N), F32)
    turned = turn[...].T
    for p in range(MAIN):
        main[p, 1, BASE : BASE + N, :] = pltpu.roll(turned, (N - 4 - 8 * p) % N, 1)
    for q in range(EXTRA):
        extra[q, 1, BASE : BASE + N, :] = pltpu.roll(turned, (N - 2 - 8 * MAIN - 4 * q) % N, 1)
    turn[0:4, :] = sides[0, LINES : LINES + 4, :]
    turn[4:8, :] = sides[1, LINES : LINES + 4, :]
    turned = pltpu.roll(turn[...].T, N - 4, 1)
    for p in range(MAIN):
        main[p, 1, BASE - 4 : BASE, :] = turned[8 * p : 8 * p + 8][:4]
        main[p, 1, BASE + N : BASE + N + 4, :] = turned[8 * p : 8 * p + 8][4:]

    def shift(pair, s):
        a0, a1 = pair
        r0, r1 = pltpu.roll(a0, (-s) % N, 1), pltpu.roll(a1, (-s) % N, 1)
        inside = lane < N - s if s > 0 else lane >= -s
        return jnp.where(inside, r0, r1), jnp.where(inside, r1, r0)

    def load(ref, plane, row, dr=0):
        return tuple(ref[plane, i, pl.ds(row + dr, 8), :] for i in range(2))

    def save(ref, plane, row, pair):
        for i in range(2):
            ref[plane, i, pl.ds(row, 8), :] = pair[i]

    def each(function, *pairs):
        return tuple(function(*pair) for pair in zip(*pairs, strict=True))

    def face(blows, c2, c1, c0, cp):
        near_up = jnp.where(blows, c1, c0)
        far_up = jnp.where(blows, c2, cp)
        return 2.0 * (c0 + c1) + 3.0 * near_up - far_up

    def spread_east(blows, grads):
        plus = each(lambda p, x: jnp.where(p, x, 0.0), blows, grads)
        minus = each(lambda x, y: x - y, grads, plus)
        twice = each(lambda x: 2.0 * x, grads)
        after = each(lambda t, x, y: t + 3.0 * x - y, twice, plus, shift(plus, 1))
        before = each(lambda t, x, y: t + 3.0 * x - y, twice, minus, shift(minus, -1))
        return each(lambda x, y: x + y, shift(after, 1), before)

    def spread_north(winds, grads):
        total = 2.0 * (grads[1] + grads[2])
        total += 3.0 * (jnp.where(winds[2], grads[2], 0.0) + jnp.where(winds[1], 0.0, grads[1]))
        return total - jnp.where(winds[3], grads[3], 0.0) - jnp.where(winds[0], 0.0, grads[0])

    def prepare(t, carry):
        row = pl.multiple_of(t * 8, 8)
        rho = load(main, RHO, row)
        low = load(main, RHO, row, -1)
        left = shift(rho, -1)
        east, north = load(main, EAST, row), load(main, NORTH, row)
        save(mass, 0, row, each(lambda w, x, y: w * (x + y) * (1.0 / 12.0), east, rho, left))
        save(mass, 1, row, each(lambda w, x, y: w * (x + y) * (1.0 / 12.0), north, rho, low))
        scale = each(lambda x: COURANT / x, rho)
        save(inv, 0, row, scale)
        land = load(extra, BINS, row)
        for b in range(BINS):
            save(g, b, row, each(lambda x, y: x * y, load(main, BINS + b, row), scale))
            kept = each(lambda x: jnp.zeros_like(x), land)
            for kind in range(8):
                kept = each(lambda k, x: jnp.where(k == float(kind), deposition[kind, b], x), land, kept)
            save(keep, b, row, each(lambda x: 1.0 - TIME_STEP * x, kept))
        return carry

    lax.fori_loop(1, 19, prepare, 0)

    def first(t, carry):
        row = pl.multiple_of(t * 8, 8)
        blows_e = each(lambda w: w > 0.0, load(main, EAST, row))
        blows_n = each(lambda w: w > 0.0, load(main, NORTH, row))
        mass_e, mass_n, scale = load(mass, 0, row), load(mass, 1, row), load(inv, 0, row)
        for b in range(BINS):
            c = load(main, b, row)
            kept = load(keep, b, row)
            fe = each(lambda m, *x: m * face(*x), mass_e, blows_e, shift(c, -2), shift(c, -1), c, shift(c, 1))
            fn = each(
                lambda m, *x: m * face(*x),
                mass_n, blows_n, load(main, b, row, -2), load(main, b, row, -1), c, load(main, b, row, 1),
            )
            save(flux, b, row, fe)
            save(flux, BINS + b, row, fn)
            save(
                middle, b, row,
                each(lambda x, k, s, i, n, f: x * k + s - i * (n - f), c, kept, load(extra, b, row), scale, shift(fe, 1), fe),
            )
            gb = load(g, b, row)
            ge = each(lambda m, x, y: m * (x - y), mass_e, gb, shift(gb, -1))
            save(back, b, row, each(lambda m, x, y: m * (x - y), mass_n, gb, load(g, b, row, -1)))
            save(second, b, row, each(lambda f, k, s: f * k + s, load(main, BINS + b, row), kept, spread_east(blows_e, ge)))
        return carry

    lax.fori_loop(1, 19, first, 0)

    def join(t, carry):
        row = pl.multiple_of(t * 8, 8)
        winds = [each(lambda w: w > 0.0, load(main, NORTH, row, dr)) for dr in (-1, 0, 1, 2)]
        scale = load(inv, 0, row)
        for b in range(BINS):
            fn, up = load(flux, BINS + b, row), load(flux, BINS + b, row, 1)
            save(middle, b, row, each(lambda m, i, n, f: m - i * (n - f), load(middle, b, row), scale, up, fn))
            grads = [load(back, b, row, dr) for dr in (-1, 0, 1, 2)]
            whole = tuple(
                second[b, i, pl.ds(row, 8), :] + spread_north([w[i] for w in winds], [x[i] for x in grads]) for i in range(2)
            )
            save(second, b, row, whole)
            save(second, BINS + b, row, each(lambda m, i: m * i, whole, scale))
        return carry

    lax.fori_loop(1, 19, join, 0)

    def last(t, carry):
        row = pl.multiple_of(t * 8, 8)
        blows_e = each(lambda w: w > 0.0, load(main, EAST, row))
        blows_n = main[NORTH, 0, pl.ds(row, 8), :] > 0.0
        mass_e, mass_n = load(mass, 0, row), mass[1, 0, pl.ds(row, 8), :]
        rho = load(main, RHO, row)
        rim_e = rim_n = None
        own = 0.0
        for b in range(BINS):
            c = load(middle, b, row)
            fe = each(lambda m, *x: m * face(*x), mass_e, blows_e, shift(c, -2), shift(c, -1), c, shift(c, 1))
            rows = [middle[b, 0, pl.ds(row + dr, 8), :] for dr in (-2, -1, 1)]
            fn = mass_n * face(blows_n, rows[0], rows[1], c[0], rows[2])
            flux2[b, pl.ds(row, 8), :] = fn
            ga, gb = load(g, b, row), load(second, BINS + b, row)
            dea = each(lambda x, y: x - y, ga, shift(ga, -1))
            deb = each(lambda x, y: x - y, gb, shift(gb, -1))
            dna = ga[0] - g[b, 0, pl.ds(row - 1, 8), :]
            dnb = gb[0] - second[BINS + b, 0, pl.ds(row - 1, 8), :]
            old = load(flux, b, row)
            old_n = flux[BINS + b, 0, pl.ds(row, 8), :]
            add_e = each(lambda x, y, z, w: x * y + z * w, fe, dea, old, deb)
            add_n = fn * dna + old_n * dnb
            rim_e = add_e if rim_e is None else each(lambda x, y: x + y, rim_e, add_e)
            rim_n = add_n if rim_n is None else rim_n + add_n
            own = own + ga[0] * (shift(fe, 1)[0] - fe[0]) + gb[0] * (shift(old, 1)[0] - old[0])
            bank[b, pl.ds(row, 8), :] = mass_n * dnb
            ge = each(lambda m, x: m * x, mass_e, deb)
            moved = second[b, 0, pl.ds(row, 8), :] * keep[b, 0, pl.ds(row, 8), :]
            second[b, 0, pl.ds(row, 8), :] = moved + spread_east(blows_e, ge)[0]
        left = shift(rho, -1)
        rim_e = each(lambda x, a, b: x / (a + b), rim_e, rho, left)
        hn[pl.ds(row, 8), :] = rim_n / (rho[0] + main[RHO, 0, pl.ds(row - 1, 8), :])
        dens[0, pl.ds(row, 8), :] = own
        dens[1, pl.ds(row, 8), :] = rim_e[0] + shift(rim_e, 1)[0]
        return carry

    def emission(t, carry):
        row = pl.multiple_of(t * 8, 8)
        at = pl.multiple_of(t * 8 - BASE, 8)
        ground = (TIME_STEP * ins[8][pl.ds(at, 8), :].astype(F32))
        for b in range(BINS):
            total = main[BINS + b, 0, pl.ds(row, 8), :] + second[b, 0, pl.ds(row, 8), :]
            emis_out[b, pl.ds(at, 8), :] = ground * total
        return carry

    lax.fori_loop(2, 18, emission, 0)
    lax.fori_loop(1, 19, last, 0)

    def finish(t, carry):
        row = pl.multiple_of(t * 8, 8)
        at = pl.multiple_of(t * 8 - BASE, 8)
        winds = [main[NORTH, 0, pl.ds(row + dr, 8), :] > 0.0 for dr in (-1, 0, 1, 2)]
        own = dens[0, pl.ds(row, 8), :]
        for b in range(BINS):
            grads = [bank[b, pl.ds(row + dr, 8), :] for dr in (-1, 0, 1, 2)]
            adj_out[b, 0, pl.ds(at, 8), :] = second[b, 0, pl.ds(row, 8), :] + spread_north(winds, grads)
            ga, gb = g[b, 0, pl.ds(row, 8), :], second[BINS + b, 0, pl.ds(row, 8), :]
            own += ga * (flux2[b, pl.ds(row + 1, 8), :] - flux2[b, pl.ds(row, 8), :])
            own += gb * (flux[BINS + b, 0, pl.ds(row + 1, 8), :] - flux[BINS + b, 0, pl.ds(row, 8), :])
        total = own / main[RHO, 0, pl.ds(row, 8), :] + dens[1, pl.ds(row, 8), :]
        dens_out[0, pl.ds(at, 8), :] = total + hn[pl.ds(row, 8), :] + hn[pl.ds(row + 1, 8), :]
        return carry

    lax.fori_loop(2, 18, finish, 0)


def swaps(count, offset, closed):
    pairs = []
    for low in range(offset, count, 2):
        high = low + 1
        if high >= count and closed:
            continue
        pairs += [(low, high % count), (high % count, low)]
    return pairs


SMEM = pl.BlockSpec(memory_space=pltpu.SMEM)
VMEM = pl.BlockSpec(memory_space=pltpu.VMEM)


def kernel_call(body, smem_count, arrays, out_shapes, scratch, flops=0):
    return pl.pallas_call(
        body,
        out_shape=[jax.ShapeDtypeStruct(s, F32) for s in out_shapes],
        in_specs=[SMEM] * smem_count + [VMEM] * (len(arrays) - smem_count),
        out_specs=[VMEM] * len(out_shapes),
        scratch_shapes=[pltpu.VMEM(s, F32) for s in scratch],
        compiler_params=pltpu.CompilerParams(vmem_limit_bytes=40 * 1024 * 1024),
    )(*arrays)


def shards(*args):
    ins, deposition = args[:10], args[10]
    lat, lon = lax.axis_index("lat"), lax.axis_index("lon")
    lats, lons = lax.axis_size("lat"), lax.axis_size("lon")
    info = jnp.stack([lat % 2, lon % 2, (lat == 0).astype(jnp.int32), (lat == lats - 1).astype(jnp.int32)]).astype(jnp.int32)
    msg = (LAT_MSG, N)
    out0, out1, lines = kernel_call(
        pack_kernel, 1, (info, *ins), [msg, msg, (2, LON_MSG, N)], [(2, *msg), (N, N)]
    )
    got0 = lax.ppermute(out0, "lat", swaps(lats, 0, True))
    got1 = lax.ppermute(out1, "lat", swaps(lats, 1, True))
    (both,) = kernel_call(
        corner_kernel, 1, (info, got0, got1, lines), [(2 * LON_MSG, N)], [(2, *msg), (N, N)]
    )
    near = lax.ppermute(both, "lon", swaps(lons, 0, False))
    onward = [(i, (i + (2 if i % 2 == 0 else lons - 2)) % lons) for i in range(lons)]
    passed = lax.ppermute(near[LON_MSG:], "lon", onward)
    pair = (2, ROWS, N)
    outs = kernel_call(
        main_kernel,
        2,
        (info, deposition, *ins, got0, got1, near, passed),
        [(BINS, 1, N, N), (1, N, N), (BINS, N, N)],
        [
            (2, *msg),
            (2, LON_MSG, N),
            (N, N),
            (MAIN, *pair),
            (EXTRA, *pair),
            (2, *pair),
            (1, *pair),
            (BINS, *pair),
            (BINS, *pair),
            (BINS, *pair),
            (2 * BINS, *pair),
            (2 * BINS, *pair),
            (BINS, *pair),
            (BINS, ROWS, N),
            (BINS, ROWS, N),
            (ROWS, N),
            (2, ROWS, N),
        ],
    )
    return tuple(outs)


def solution(mesh):
    return jax.shard_map(
        shards,
        mesh=mesh,
        in_specs=(
            P(None, None, "lat", "lon"),
            P(None, None, "lat", "lon"),
            P(None, "lat", "lon"),
            P(None, "lat", "lon"),
            P(None, "lat", "lon"),
            P(None, "lat", "lon"),
            P(None, "lat", "lon"),
            P("lat", "lon"),
            P("lat", "lon"),
            P(None, "lat", "lon"),
            P(),
        ),
        out_specs=(P(None, None, "lat", "lon"), P(None, "lat", "lon"), P(None, "lat", "lon")),
        check_vma=False,
    )
```

time: 633 us -> 61.1 us (0.10)
  the two profiles are of different devices: /device:TPU:2 before, /device:TPU:32 now
where the time goes in v1:
time: 61.1 us; the launch traced here: 60.5 us
  starting transfers between devices  22.4 us (37%)
  Pallas kernels  14.3 us (23%)
  waiting for transfers between devices  14.1 us (23%)
  local copies, waits for them, and re-layouts  8.74 us (14%)
  between operations  0.84 us (1%)
    pallas_call x3, Pallas kernels, kernel_call(): pl.pallas_call(body, out_shape=[jax.ShapeDtypeStruct(s, F32) for s in out...  14.3 us
    ppermute x1, starting transfers between devices, shards(): near = lax.ppermute(both, 'lon', swaps(lons, 0, False))  11 us
    unnamed x41, local copies, waits for them, and re-layouts  8.74 us
    ppermute x1, starting transfers between devices, shards(): got1 = lax.ppermute(out1, 'lat', swaps(lats, 1, True))  7.49 us
    ppermute x1, waiting for transfers between devices, shards(): passed = lax.ppermute(near[LON_MSG:], 'lon', onward)  7.11 us
    ppermute x1, waiting for transfers between devices, shards(): near = lax.ppermute(both, 'lon', swaps(lons, 0, False))  5.45 us
    ppermute x1, starting transfers between devices, shards(): got0 = lax.ppermute(out0, 'lat', swaps(lats, 0, True))  2.05 us
    ppermute x1, starting transfers between devices, shards(): passed = lax.ppermute(near[LON_MSG:], 'lon', onward)  1.91 us
  transfers between devices with their start and end apart: 4, of which 3 were waited for; matrix products, arithmetic and copies ran while one was open for 0% of the time, Pallas kernels for 0%

profile of v1, /device:TPU:32, one launch (start us, length us, event | category | flops | bytes accessed | tf_op | source)
XLA Modules:
  0.0 60.5 jit_solution(9671182962539061375)
XLA Ops:
  0.6 0.0 copy-start.6
  0.7 0.1 pad_add_fusion.info
  0.7 0.7 %copy-done.6 = f32[1,128,128]{2,1,0:T(8,128)S(1)} copy-done((f32[1,128,128]{2,1,0:T(8,128)S(1)}, f32[1,128,128]{2,1,0:T(8,128)}, u32[]{:S(2)}) %copy-start.6) | copy-done | bytes 65560
  1.5 0.0 copy-start
  1.5 0.9 %copy-done = f32[4,1,128,128]{3,2,1,0:T(8,128)S(1)} copy-done((f32[4,1,128,128]{3,2,1,0:T(8,128)S(1)}, f32[4,1,128,128]{3,2,1,0:T(8,128)}, u32[]{:S(2)}) %copy-start) | copy-done | bytes 262168
  2.4 0.0 copy-start.2
  2.4 0.9 %copy-done.2 = f32[4,1,128,128]{3,2,1,0:T(8,128)S(1)} copy-done((f32[4,1,128,128]{3,2,1,0:T(8,128)S(1)}, f32[4,1,128,128]{3,2,1,0:T(8,128)}, u32[]{:S(2)}) %copy-start.2) | copy-done | bytes 262168
  3.4 0.0 copy-start.4
  3.4 0.9 %copy-done.4 = f32[4,128,128]{2,1,0:T(8,128)S(1)} copy-done((f32[4,128,128]{2,1,0:T(8,128)S(1)}, f32[4,128,128]{2,1,0:T(8,128)}, u32[]{:S(2)}) %copy-start.4) | copy-done | bytes 262168
  4.3 0.0 copy-start.7
  4.3 0.8 %copy-done.7 = f32[1,128,128]{2,1,0:T(8,128)S(1)} copy-done((f32[1,128,128]{2,1,0:T(8,128)S(1)}, f32[1,128,128]{2,1,0:T(8,128)}, u32[]{:S(2)}) %copy-start.7) | copy-done | bytes 65560
  5.2 0.0 copy-start.9
  5.2 0.8 %copy-done.9 = s32[1,128,128]{2,1,0:T(8,128)S(1)} copy-done((s32[1,128,128]{2,1,0:T(8,128)S(1)}, s32[1,128,128]{2,1,0:T(8,128)}, u32[]{:S(2)}) %copy-start.9) | copy-done | bytes 65560
  6.0 0.0 copy-start.11
  6.0 0.8 %copy-done.11 = s32[1,128,128]{2,1,0:T(8,128)S(1)} copy-done((s32[1,128,128]{2,1,0:T(8,128)S(1)}, s32[1,128,128]{2,1,0:T(8,128)}, u32[]{:S(2)}) %copy-start.11) | copy-done | bytes 65560
  6.8 0.0 copy-start.13
  6.8 0.8 %copy-done.13 = f32[1,128,128]{2,1,0:T(8,128)S(1)} copy-done((f32[1,128,128]{2,1,0:T(8,128)S(1)}, f32[1,128,128]{2,1,0:T(8,128)}, u32[]{:S(2)}) %copy-start.13) | copy-done | bytes 65560
  7.7 0.0 copy-start.15
  7.7 0.8 %copy-done.15 = s32[128,128]{1,0:T(8,128)S(1)} copy-done((s32[128,128]{1,0:T(8,128)S(1)}, s32[128,128]{1,0:T(8,128)}, u32[]{:S(2)}) %copy-start.15) | copy-done | bytes 65560
  8.5 0.0 copy-start.17
  8.5 0.8 %copy-done.17 = s32[128,128]{1,0:T(8,128)S(1)} copy-done((s32[128,128]{1,0:T(8,128)S(1)}, s32[128,128]{1,0:T(8,128)}, u32[]{:S(2)}) %copy-start.17) | copy-done | bytes 65560
  9.4 0.0 copy-start.19
  9.4 0.0 copy-start.3
  9.4 0.0 copy-start.5
  9.4 0.0 copy-start.8
  9.4 0.0 copy-start.10
  9.4 0.0 copy-start.12
  9.4 0.0 copy-start.14
  9.4 0.0 copy-start.16
  9.4 0.0 copy-start.18
  9.4 1.0 %shard_map.130 = (f32[56,128]{1,0:T(8,128)S(1)}, f32[56,128]{1,0:T(8,128)S(1)}, f32[2,64,128]{2,1,0:T(8,128)S(1)}) custom-call(s32[4]{0:T(128)S(1)} %pad_add_fusion.info, f32[4,1,128,128]{3,2,1,0:T(8,128)S(1)} %copy-done, f32[4,1,128,128]{3,2,1,0:T(8,128)S(1)} %copy-done.2, f32[1,128,128]{2,1,0:T(8,128)S(1)} %copy-done.6, f32[1,128,128]{2,1,0:T(8,128)S(1)} %copy-done.7, ...), custom_call_target="tpu_custom_call" | custom-call | tf_op jit(solution)/shard_map/pallas_call | solution.py:346
  10.4 0.0 copy-start.1
  10.4 2.1 %collective-permute-start = (f32[56,128]{1,0:T(8,128)S(1)}, f32[56,128]{1,0:T(8,128)S(1)}, u32[]{:S(2)}, u32[]{:S(2)}) collective-permute-start(f32[56,128]{1,0:T(8,128)S(1)} %get-tuple-element.6), channel_id=1, source_target_pairs={{0,1},{1,0},{2,3},{3,2},{4,5},{5,4},{6,7},{7,6},{8,9},{9,8},{10,11... | collective-permute-start | bytes 86024 | tf_op jit(solution)/shard_map/ppermute | solution.py:365
  12.5 7.5 %collective-permute-start.1 = (f32[56,128]{1,0:T(8,128)S(1)}, f32[56,128]{1,0:T(8,128)S(1)}, u32[]{:S(2)}, u32[]{:S(2)}) collective-permute-start(f32[56,128]{1,0:T(8,128)S(1)} %get-tuple-element.7), channel_id=1, source_target_pairs={{1,2},{2,1},{3,4},{4,3},{5,6},{6,5},{7,8},{8,7},{9,10},{10,9},{11,... | collective-permute-start | bytes 86024 | tf_op jit(solution)/shard_map/ppermute | solution.py:366
  20.0 0.0 collective-permute-done.got0.refs_10_
  20.0 1.5 %collective-permute-done.1.got1.refs_11_ = f32[56,128]{1,0:T(8,128)S(1)} collective-permute-done((f32[56,128]{1,0:T(8,128)S(1)}, f32[56,128]{1,0:T(8,128)S(1)}, u32[]{:S(2)}, u32[]{:S(2)}) %collective-permute-start.1) | collective-permute-done | bytes 28704 | tf_op jit(solution)/shard_map/ppermute | solution.py:366
  21.5 0.6 %shard_map.131 = f32[128,128]{1,0:T(8,128)S(1)} custom-call(s32[4]{0:T(128)S(1)} %pad_add_fusion.info, f32[56,128]{1,0:T(8,128)S(1)} %collective-permute-done.got0.refs_10_, f32[56,128]{1,0:T(8,128)S(1)} %collective-permute-done.1.got1.refs_11_, f32[2,64,128]{2,1,0:T(8,128)S(1)} %get-tuple-element.8.lines), custom_call_target="tpu_custom_call" | custom-call | tf_op jit(solution)/shard_map/pallas_call | solution.py:346
  22.1 11.0 %collective-permute-start.2 = (f32[128,128]{1,0:T(8,128)S(1)}, f32[128,128]{1,0:T(8,128)S(1)}, u32[]{:S(2)}, u32[]{:S(2)}) collective-permute-start(f32[128,128]{1,0:T(8,128)S(1)} %shard_map.131), channel_id=1, source_target_pairs={{0,16},{16,0},{32,48},{48,32},{64,80},{80,64},{96,112},{112,96},{1... | collective-permute-start | bytes 196616 | tf_op jit(solution)/shard_map/ppermute | solution.py:370
  33.1 5.4 %collective-permute-done.2.refs_12_ = f32[128,128]{1,0:T(8,128)S(1)} collective-permute-done((f32[128,128]{1,0:T(8,128)S(1)}, f32[128,128]{1,0:T(8,128)S(1)}, u32[]{:S(2)}, u32[]{:S(2)}) %collective-permute-start.2) | collective-permute-done | bytes 65568 | tf_op jit(solution)/shard_map/ppermute | solution.py:370
  38.6 1.9 %collective-permute-start.3 = (f32[64,128]{1,0:T(8,128)S(1)}, f32[64,128]{1,0:T(8,128)S(1)}, u32[]{:S(2)}, u32[]{:S(2)}) collective-permute-start(f32[64,128]{1,0:T(8,128)S(1)} %slice.4), channel_id=1, source_target_pairs={{0,32},{16,496},{32,64},{48,16},{64,96},{80,48},{96,128},{112,80},... | collective-permute-start | bytes 98312 | tf_op jit(solution)/shard_map/ppermute | solution.py:372
  40.5 0.0 copy-done.19
  40.5 0.1 copy.14.deposition
  40.6 7.1 %collective-permute-done.3.refs_13_ = f32[64,128]{1,0:T(8,128)S(1)} collective-permute-done((f32[64,128]{1,0:T(8,128)S(1)}, f32[64,128]{1,0:T(8,128)S(1)}, u32[]{:S(2)}, u32[]{:S(2)}) %collective-permute-start.3) | collective-permute-done | bytes 32800 | tf_op jit(solution)/shard_map/ppermute | solution.py:372
  47.7 0.0 copy-done.3
  47.7 0.0 copy-done.5
  47.7 0.0 copy-done.8
  47.7 0.0 copy-done.10
  47.7 0.0 copy-done.12
  47.7 0.0 copy-done.14
  47.7 0.0 copy-done.16
  47.8 0.0 copy-done.18
  47.8 0.0 copy-done.1
  47.8 12.7 %shard_map.132 = (f32[4,1,128,128]{3,2,1,0:T(8,128)}, f32[1,128,128]{2,1,0:T(8,128)}, f32[4,128,128]{2,1,0:T(8,128)}) custom-call(s32[4]{0:T(128)S(1)} %pad_add_fusion.info, f32[8,4]{1,0:T(8,128)S(1)} %copy.14.deposition, f32[4,1,128,128]{3,2,1,0:T(8,128)S(1)} %copy-done.1, f32[4,1,128,128]{3,2,1,0:T(8,128)S(1)} %copy-done.3, f32[1,128,128]{2,1,0:T(8,128)S(1)} %copy-done.6, ...), custom_call_target="tpu_custom_call" | custom-call | tf_op jit(solution)/shard_map/pallas_call | solution.py:346
  (1 shorter events, 0.0 us)
Async XLA Ops:
  0.6 0.8 %copy-start.6 = (f32[1,128,128]{2,1,0:T(8,128)S(1)}, f32[1,128,128]{2,1,0:T(8,128)}, u32[]{:S(2)}) copy-start(f32[1,128,128]{2,1,0:T(8,128)} %refs_2_.3) | copy-start | bytes 196612
  1.5 0.9 %copy-start = (f32[4,1,128,128]{3,2,1,0:T(8,128)S(1)}, f32[4,1,128,128]{3,2,1,0:T(8,128)}, u32[]{:S(2)}) copy-start(f32[4,1,128,128]{3,2,1,0:T(8,128)} %refs_0_.3) | copy-start | bytes 786436
  2.4 0.9 %copy-start.2 = (f32[4,1,128,128]{3,2,1,0:T(8,128)S(1)}, f32[4,1,128,128]{3,2,1,0:T(8,128)}, u32[]{:S(2)}) copy-start(f32[4,1,128,128]{3,2,1,0:T(8,128)} %refs_1_.3) | copy-start | bytes 786436
  3.4 0.9 %copy-start.4 = (f32[4,128,128]{2,1,0:T(8,128)S(1)}, f32[4,128,128]{2,1,0:T(8,128)}, u32[]{:S(2)}) copy-start(f32[4,128,128]{2,1,0:T(8,128)} %refs_9_.3) | copy-start | bytes 786436
  4.3 0.8 %copy-start.7 = (f32[1,128,128]{2,1,0:T(8,128)S(1)}, f32[1,128,128]{2,1,0:T(8,128)}, u32[]{:S(2)}) copy-start(f32[1,128,128]{2,1,0:T(8,128)} %refs_3_.3) | copy-start | bytes 196612
  5.2 0.8 %copy-start.9 = (s32[1,128,128]{2,1,0:T(8,128)S(1)}, s32[1,128,128]{2,1,0:T(8,128)}, u32[]{:S(2)}) copy-start(s32[1,128,128]{2,1,0:T(8,128)} %refs_4_.3) | copy-start | bytes 196612
  6.0 0.8 %copy-start.11 = (s32[1,128,128]{2,1,0:T(8,128)S(1)}, s32[1,128,128]{2,1,0:T(8,128)}, u32[]{:S(2)}) copy-start(s32[1,128,128]{2,1,0:T(8,128)} %refs_5_.3) | copy-start | bytes 196612
  6.8 0.8 %copy-start.13 = (f32[1,128,128]{2,1,0:T(8,128)S(1)}, f32[1,128,128]{2,1,0:T(8,128)}, u32[]{:S(2)}) copy-start(f32[1,128,128]{2,1,0:T(8,128)} %refs_6_.3) | copy-start | bytes 196612
  7.7 0.8 %copy-start.15 = (s32[128,128]{1,0:T(8,128)S(1)}, s32[128,128]{1,0:T(8,128)}, u32[]{:S(2)}) copy-start(s32[128,128]{1,0:T(8,128)} %refs_7_.3) | copy-start | bytes 196612
  8.5 0.8 %copy-start.17 = (s32[128,128]{1,0:T(8,128)S(1)}, s32[128,128]{1,0:T(8,128)}, u32[]{:S(2)}) copy-start(s32[128,128]{1,0:T(8,128)} %refs_8_.3) | copy-start | bytes 196612
  9.4 31.1 %copy-start.19 = (f32[8,4]{0,1:T(4,128)S(1)}, f32[8,4]{0,1:T(4,128)}, u32[]{:S(2)}) copy-start(f32[8,4]{0,1:T(4,128)} %param.21) | copy-start | bytes 388
  9.4 38.3 %copy-start.3 = (f32[4,1,128,128]{3,2,1,0:T(8,128)S(1)}, f32[4,1,128,128]{3,2,1,0:T(8,128)}, u32[]{:S(2)}) copy-start(f32[4,1,128,128]{3,2,1,0:T(8,128)} %refs_1_.3) | copy-start | bytes 786436
  9.4 38.3 %copy-start.5 = (f32[4,128,128]{2,1,0:T(8,128)S(1)}, f32[4,128,128]{2,1,0:T(8,128)}, u32[]{:S(2)}) copy-start(f32[4,128,128]{2,1,0:T(8,128)} %refs_9_.3) | copy-start | bytes 786436
  9.4 38.3 %copy-start.8 = (f32[1,128,128]{2,1,0:T(8,128)S(1)}, f32[1,128,128]{2,1,0:T(8,128)}, u32[]{:S(2)}) copy-start(f32[1,128,128]{2,1,0:T(8,128)} %refs_3_.3) | copy-start | bytes 196612
  9.4 38.3 %copy-start.10 = (s32[1,128,128]{2,1,0:T(8,128)S(1)}, s32[1,128,128]{2,1,0:T(8,128)}, u32[]{:S(2)}) copy-start(s32[1,128,128]{2,1,0:T(8,128)} %refs_4_.3) | copy-start | bytes 196612
  9.4 38.3 %copy-start.12 = (s32[1,128,128]{2,1,0:T(8,128)S(1)}, s32[1,128,128]{2,1,0:T(8,128)}, u32[]{:S(2)}) copy-start(s32[1,128,128]{2,1,0:T(8,128)} %refs_5_.3) | copy-start | bytes 196612
  9.4 38.3 %copy-start.14 = (f32[1,128,128]{2,1,0:T(8,128)S(1)}, f32[1,128,128]{2,1,0:T(8,128)}, u32[]{:S(2)}) copy-start(f32[1,128,128]{2,1,0:T(8,128)} %refs_6_.3) | copy-start | bytes 196612
  9.4 38.3 %copy-start.16 = (s32[128,128]{1,0:T(8,128)S(1)}, s32[128,128]{1,0:T(8,128)}, u32[]{:S(2)}) copy-start(s32[128,128]{1,0:T(8,128)} %refs_7_.3) | copy-start | bytes 196612
  9.4 38.3 %copy-start.18 = (s32[128,128]{1,0:T(8,128)S(1)}, s32[128,128]{1,0:T(8,128)}, u32[]{:S(2)}) copy-start(s32[128,128]{1,0:T(8,128)} %refs_8_.3) | copy-start | bytes 196612
  10.4 37.4 %copy-start.1 = (f32[4,1,128,128]{3,2,1,0:T(8,128)S(1)}, f32[4,1,128,128]{3,2,1,0:T(8,128)}, u32[]{:S(2)}) copy-start(f32[4,1,128,128]{3,2,1,0:T(8,128)} %refs_0_.3) | copy-start | bytes 786436
  10.4 9.6 %collective-permute-start = (f32[56,128]{1,0:T(8,128)S(1)}, f32[56,128]{1,0:T(8,128)S(1)}, u32[]{:S(2)}, u32[]{:S(2)}) collective-permute-start(f32[56,128]{1,0:T(8,128)S(1)} %get-tuple-element.6), channel_id=1, source_target_pairs={{0,1},{1,0},{2,3},{3,2},{4,5},{5,4},{6,7},{7,6},{8,9},{9,8},{10,11... | collective-permute-start | bytes 86024 | tf_op jit(solution)/shard_map/ppermute | solution.py:365
  12.5 9.0 %collective-permute-start.1 = (f32[56,128]{1,0:T(8,128)S(1)}, f32[56,128]{1,0:T(8,128)S(1)}, u32[]{:S(2)}, u32[]{:S(2)}) collective-permute-start(f32[56,128]{1,0:T(8,128)S(1)} %get-tuple-element.7), channel_id=1, source_target_pairs={{1,2},{2,1},{3,4},{4,3},{5,6},{6,5},{7,8},{8,7},{9,10},{10,9},{11,... | collective-permute-start | bytes 86024 | tf_op jit(solution)/shard_map/ppermute | solution.py:366
  22.1 16.4 %collective-permute-start.2 = (f32[128,128]{1,0:T(8,128)S(1)}, f32[128,128]{1,0:T(8,128)S(1)}, u32[]{:S(2)}, u32[]{:S(2)}) collective-permute-start(f32[128,128]{1,0:T(8,128)S(1)} %shard_map.131), channel_id=1, source_target_pairs={{0,16},{16,0},{32,48},{48,32},{64,80},{80,64},{96,112},{112,96},{1... | collective-permute-start | bytes 196616 | tf_op jit(solution)/shard_map/ppermute | solution.py:370
  38.6 9.1 %collective-permute-start.3 = (f32[64,128]{1,0:T(8,128)S(1)}, f32[64,128]{1,0:T(8,128)S(1)}, u32[]{:S(2)}, u32[]{:S(2)}) collective-permute-start(f32[64,128]{1,0:T(8,128)S(1)} %slice.4), channel_id=1, source_target_pairs={{0,32},{16,496},{32,64},{48,16},{64,96},{80,48},{96,128},{112,80},... | collective-permute-start | bytes 98312 | tf_op jit(solution)/shard_map/ppermute | solution.py:372

commit v2 on v1

v2 whole, which is shorter than its diff:
```python
import jax
import jax.numpy as jnp
from jax import lax
from jax.experimental import pallas as pl
from jax.experimental.pallas import tpu as pltpu
from jax.sharding import PartitionSpec as P

COURANT = 0.3
TIME_STEP = 0.25

N = 128
BINS = 4
MAIN = 2 * BINS + 3
EXTRA = BINS + 1
EAST, NORTH, RHO = 2 * BINS, 2 * BINS + 1, 2 * BINS + 2
LINES = 4 * MAIN + 2 * EXTRA
LAT_MSG = 56
LON_MSG = 64
BASE = 16
ROWS = 160
OWN_FLOPS = 3_000_000
OWN_TALL, OWN_END = 24, 32
EDGE_TALL, EDGE_END = 48, 64
PLANES = MAIN + EXTRA + 1
GROUND = MAIN + EXTRA
F32 = jnp.float32


def position():
    lat, lon = lax.axis_index("lat"), lax.axis_index("lon")
    last = lax.axis_size("lat") - 1
    return lat % 2, lon % 2, (lat == 0).astype(jnp.int32), (lat == last).astype(jnp.int32)


def plane_readers(refs, info):
    tracer, adjoint, speed_e, speed_n, sign_e, sign_n, density, land, mask, emission = refs

    def east(at, size):
        s = speed_e[0, pl.ds(at, size), :]
        return jnp.where(sign_e[0, pl.ds(at, size), :] == 1, s, -s)

    def north(at, size):
        s = speed_n[0, pl.ds(at, size), :]
        s = jnp.where(sign_n[0, pl.ds(at, size), :] == 1, s, -s)
        row = lax.broadcasted_iota(jnp.int32, (size, N), 0) + at
        return jnp.where((row == 0) & (info[2] == 1), 0.0, s)

    def source(b):
        def read(at, size):
            m = mask[pl.ds(at, size), :].astype(F32)
            return TIME_STEP * m * emission[b, pl.ds(at, size), :]

        return read

    main = [lambda at, size, b=b: tracer[b, 0, pl.ds(at, size), :] for b in range(BINS)]
    main += [lambda at, size, b=b: adjoint[b, 0, pl.ds(at, size), :] for b in range(BINS)]
    main += [east, north, lambda at, size: density[0, pl.ds(at, size), :]]
    extra = [source(b) for b in range(BINS)]
    extra += [lambda at, size: land[pl.ds(at, size), :].astype(F32)]
    return main, extra


def pack_kernel(*refs):
    info = position()
    sources, (out0, out1, lines_out, planes), ins = refs[:10], refs[10:14], refs[14:24]
    edge, packed, sem = refs[24:]
    copies = [pltpu.make_async_copy(x, y, sem.at[i]) for i, (x, y) in enumerate(zip(sources, ins, strict=True))]
    for copy in copies:
        copy.start()
    for copy in copies:
        copy.wait()
    main, extra = plane_readers(ins, info)
    lane = lax.broadcasted_iota(jnp.int32, (N, N), 1)
    for p, read in enumerate(main + extra):
        planes[p] = read(0, N)
    planes[GROUND] = TIME_STEP * ins[8][...].astype(F32)
    for p in range(MAIN):
        edge[0, 4 * p : 4 * p + 4, :] = planes[p, 0:4, :]
        edge[1, 4 * p : 4 * p + 4, :] = planes[p, N - 4 :, :]
    for q in range(EXTRA):
        at = 4 * MAIN + 2 * q
        edge[0, at : at + 2, :] = planes[MAIN + q, 0:2, :]
        edge[1, at : at + 2, :] = planes[MAIN + q, N - 2 :, :]
    edge[:, LINES:LAT_MSG, :] = jnp.zeros((2, LAT_MSG - LINES, N), F32)
    parity = info[0]
    out0[...] = edge[1 - parity]
    out1[...] = edge[parity]
    both = jnp.zeros((N, N), F32)
    for p in range(MAIN):
        turned = pltpu.roll(planes[p], 8 * p + 4, 1)
        both = jnp.where((lane >= 8 * p) & (lane < 8 * p + 8), turned, both)
    for q in range(EXTRA):
        at = 8 * MAIN + 4 * q
        turned = pltpu.roll(planes[MAIN + q], at + 2, 1)
        both = jnp.where((lane >= at) & (lane < at + 4), turned, both)
    packed[...] = both.T
    for p in range(MAIN):
        lines_out[1, 4 * p : 4 * p + 4, :] = packed[8 * p : 8 * p + 4, :]
        lines_out[0, 4 * p : 4 * p + 4, :] = packed[8 * p + 4 : 8 * p + 8, :]
    for q in range(EXTRA):
        at, to = 8 * MAIN + 4 * q, 4 * MAIN + 2 * q
        lines_out[1, to : to + 2, :] = packed[at : at + 2, :]
        lines_out[0, to : to + 2, :] = packed[at + 2 : at + 4, :]
    lines_out[:, LINES:LON_MSG, :] = jnp.zeros((2, LON_MSG - LINES, N), F32)


def place_lat(info, got0, got1, halo):
    parity = info[0]
    halo[1 - parity] = got0[...]
    halo[parity] = got1[...]
    at = 4 * RHO

    @pl.when(info[2] == 1)
    def _():
        halo[0, at : at + 4, :] = jnp.ones((4, N), F32)

    @pl.when(info[3] == 1)
    def _():
        halo[1, at : at + 4, :] = jnp.ones((4, N), F32)


def corner_kernel(got0, got1, lines, out, halo, rows):
    info = position()
    place_lat(info, got0, got1, halo)
    rows[8 * MAIN :, :] = jnp.zeros((N - 8 * MAIN, N), F32)
    for p in range(MAIN):
        rows[8 * p : 8 * p + 4, :] = halo[0, 4 * p : 4 * p + 4, :]
        rows[8 * p + 4 : 8 * p + 8, :] = halo[1, 4 * p : 4 * p + 4, :]
    turned = rows[...].T
    parity = info[1]
    out[0:LON_MSG, :] = lines[1 - parity]
    out[LON_MSG:, :] = lines[parity]
    left, right = turned[0:8][:4], turned[N - 8 :][4:]

    @pl.when(parity == 0)
    def _():
        out[LINES : LINES + 4, :] = right
        out[LON_MSG + LINES : LON_MSG + LINES + 4, :] = left

    @pl.when(parity == 1)
    def _():
        out[LINES : LINES + 4, :] = left
        out[LON_MSG + LINES : LON_MSG + LINES + 4, :] = right


def shift(x, s):
    return pltpu.roll(x, (-s) % N, 1)


def face(blows, c2, c1, c0, cp):
    near_up = jnp.where(blows, c1, c0)
    far_up = jnp.where(blows, c2, cp)
    return 2.0 * (c0 + c1) + 3.0 * near_up - far_up


def spread_east(blows, grads):
    plus = jnp.where(blows, grads, 0.0)
    minus = grads - plus
    twice = 2.0 * grads
    after = twice + 3.0 * plus - shift(plus, 1)
    before = twice + 3.0 * minus - shift(minus, -1)
    return shift(after, 1) + before


def spread_north(winds, grads):
    total = 2.0 * (grads[1] + grads[2])
    total += 3.0 * (jnp.where(winds[2], grads[2], 0.0) + jnp.where(winds[1], 0.0, grads[1]))
    return total - jnp.where(winds[3], grads[3], 0.0) - jnp.where(winds[0], 0.0, grads[0])


def places(count):
    at, total = {}, 0
    for name, size in (("mass", 2), ("keep", count), ("g", count), ("middle", count), ("seen", count), ("gm", count), ("flux", 2 * count)):
        at[name] = total
        total += size
    return at, total


def first_half(tall, count, field_of, keep_of, state, back, scale_ref):
    field = field_of(tall)
    at, _ = places(count)

    def get(name, b, row):
        return state[at[name] + b, pl.ds(row, tall), :]

    def put(name, b, row, value):
        state[at[name] + b, pl.ds(row, tall), :] = value

    def prepare(t, carry):
        row = pl.multiple_of(8 + t * tall, 8)
        rho = field("rho", 0, row)
        put("mass", 0, row, field("east", 0, row) * (rho + shift(rho, -1)) * (1.0 / 12.0))
        put("mass", 1, row, field("north", 0, row) * (rho + field("rho", 0, row - 1)) * (1.0 / 12.0))
        scale = COURANT / rho
        scale_ref[pl.ds(row, tall), :] = scale
        for b, kept in enumerate(keep_of(row)):
            put("g", b, row, field("adjoint", b, row) * scale)
            put("keep", b, row, kept)
        return carry

    lax.fori_loop(0, 144 // tall, prepare, 0)

    def first(t, carry):
        row = pl.multiple_of(8 + t * tall, 8)
        blows_e, blows_n = field("east", 0, row) > 0.0, field("north", 0, row) > 0.0
        mass_e, mass_n, scale = get("mass", 0, row), get("mass", 1, row), scale_ref[pl.ds(row, tall), :]
        for b in range(count):
            c, kept = field("tracer", b, row), get("keep", b, row)
            fe = mass_e * face(blows_e, shift(c, -2), shift(c, -1), c, shift(c, 1))
            fn = mass_n * face(
                blows_n, field("tracer", b, row - 2), field("tracer", b, row - 1), c, field("tracer", b, row + 1)
            )
            put("flux", b, row, fe)
            put("flux", count + b, row, fn)
            put("middle", b, row, c * kept + field("source", b, row) - scale * (shift(fe, 1) - fe))
            gb = get("g", b, row)
            back[b, pl.ds(row, tall), :] = mass_n * (gb - get("g", b, row - 1))
            ge = mass_e * (gb - shift(gb, -1))
            put("seen", b, row, field("adjoint", b, row) * kept + spread_east(blows_e, ge))
        return carry

    lax.fori_loop(0, 144 // tall, first, 0)

    def join(t, carry):
        row = pl.multiple_of(8 + t * tall, 8)
        winds = [field("north", 0, row + dr) > 0.0 for dr in (-1, 0, 1, 2)]
        scale = scale_ref[pl.ds(row, tall), :]
        for b in range(count):
            change = get("flux", count + b, row + 1) - get("flux", count + b, row)
            put("middle", b, row, get("middle", b, row) - scale * change)
            whole = get("seen", b, row) + spread_north(winds, [back[b, pl.ds(row + dr, tall), :] for dr in (-1, 0, 1, 2)])
            put("seen", b, row, whole)
            put("gm", b, row, whole * scale)
        return carry

    lax.fori_loop(0, 144 // tall, join, 0)


def second_half(tall, end_tall, count, field_of, state, flux2, bank, part, rim, give):
    at, _ = places(count)
    field = field_of(tall)

    def get(name, b, row, size=tall):
        return state[at[name] + b, pl.ds(row, size), :]

    def last(t, carry):
        row = pl.multiple_of(8 + t * tall, 8)
        blows_e, blows_n = field("east", 0, row) > 0.0, field("north", 0, row) > 0.0
        mass_e, mass_n = get("mass", 0, row), get("mass", 1, row)
        rho = field("rho", 0, row)
        rim_e = rim_n = own = jnp.zeros((tall, N), F32)
        for b in range(count):
            c = get("middle", b, row)
            fe = mass_e * face(blows_e, shift(c, -2), shift(c, -1), c, shift(c, 1))
            fn = mass_n * face(blows_n, get("middle", b, row - 2), get("middle", b, row - 1), c, get("middle", b, row + 1))
            flux2[b, pl.ds(row, tall), :] = fn
            ga, gb = get("g", b, row), get("gm", b, row)
            old, old_n = get("flux", b, row), get("flux", count + b, row)
            deb = gb - shift(gb, -1)
            dnb = gb - get("gm", b, row - 1)
            rim_e += fe * (ga - shift(ga, -1)) + old * deb
            rim_n += fn * (ga - get("g", b, row - 1)) + old_n * dnb
            own += ga * (shift(fe, 1) - fe) + gb * (shift(old, 1) - old)
            bank[b, pl.ds(row, tall), :] = mass_n * dnb
            part[b, pl.ds(row, tall), :] = get("seen", b, row) * get("keep", b, row) + spread_east(blows_e, mass_e * deb)
        rim_e = rim_e / (rho + shift(rho, -1))
        rim[0, pl.ds(row, tall), :] = rim_n / (rho + field("rho", 0, row - 1))
        rim[1, pl.ds(row, tall), :] = own
        rim[2, pl.ds(row, tall), :] = rim_e + shift(rim_e, 1)
        return carry

    lax.fori_loop(0, 144 // tall, last, 0)

    def finish(t, carry):
        row = pl.multiple_of(BASE + t * end_tall, 8)
        field = field_of(end_tall)
        winds = [field("north", 0, row + dr) > 0.0 for dr in (-1, 0, 1, 2)]
        own = rim[1, pl.ds(row, end_tall), :]
        adjoints = []
        for b in range(count):
            grads = [bank[b, pl.ds(row + dr, end_tall), :] for dr in (-1, 0, 1, 2)]
            adjoints.append(part[b, pl.ds(row, end_tall), :] + spread_north(winds, grads))
            own += get("g", b, row, end_tall) * (flux2[b, pl.ds(row + 1, end_tall), :] - flux2[b, pl.ds(row, end_tall), :])
            own += get("gm", b, row, end_tall) * (get("flux", count + b, row + 1, end_tall) - get("flux", count + b, row, end_tall))
        total = own / field("rho", 0, row) + rim[2, pl.ds(row, end_tall), :] + rim[0, pl.ds(row, end_tall), :]
        seen = [field("adjoint", b, row) + get("seen", b, row, end_tall) for b in range(count)]
        give(row, pl.multiple_of(t * end_tall, 8), adjoints, total + rim[0, pl.ds(row + 1, end_tall), :], seen)
        return carry

    lax.fori_loop(0, N // end_tall, finish, 0)


PLACE = {"tracer": 0, "adjoint": BINS, "east": EAST, "north": NORTH, "rho": RHO, "source": MAIN, "land": MAIN + BINS}


def block_field(planes):
    return lambda tall: lambda name, b, row: planes[PLACE[name] + b, pl.ds(row, tall), :]


STRIPS = ("tracer", "adjoint", "source", "east", "north", "rho", "land")


def strip_field(strips):
    return lambda tall: lambda name, b, row: strips[STRIPS.index(name), pl.ds(row, tall), :]


def own_kernel(deposition, *refs):
    info = position()
    block, got0, got1, _, planes, state, strips, halo, back, scale = refs
    place_lat(info, got0, got1, halo)
    for p in range(MAIN):
        planes[p, BASE : BASE + N, :] = block[p]
        planes[p, BASE - 4 : BASE, :] = halo[0, 4 * p : 4 * p + 4, :]
        planes[p, BASE + N : BASE + N + 4, :] = halo[1, 4 * p : 4 * p + 4, :]
    for q in range(EXTRA):
        at, p = 4 * MAIN + 2 * q, MAIN + q
        planes[p, BASE : BASE + N, :] = block[p]
        planes[p, BASE - 2 : BASE, :] = halo[0, at : at + 2, :]
        planes[p, BASE + N : BASE + N + 2, :] = halo[1, at : at + 2, :]
    field = block_field(planes)(OWN_TALL)

    def keep_of(row):
        land = field("land", 0, row)
        for b in range(BINS):
            rate = jnp.zeros_like(land)
            for kind in range(8):
                rate = jnp.where(land == float(kind), deposition[b, kind], rate)
            yield 1.0 - TIME_STEP * rate

    first_half(OWN_TALL, BINS, block_field(planes), keep_of, state, back, scale)
    lane = lax.broadcasted_iota(jnp.int32, (OWN_TALL, N), 1)

    def cut(t, carry):
        row = pl.multiple_of(8 + t * OWN_TALL, 8)
        for i, name in enumerate(STRIPS):
            if name in ("tracer", "adjoint", "source"):
                both = jnp.zeros((OWN_TALL, N), F32)
                for b in range(BINS):
                    x, low = field(name, b, row), 32 * b
                    both = jnp.where((lane >= low) & (lane < low + 12), pltpu.roll(x, (low + 12) % N, 1), both)
                    both = jnp.where((lane >= low + 20) & (lane < low + 32), pltpu.roll(x, (low + 20) % N, 1), both)
            else:
                x = field(name, 0, row)
                both = jnp.where(lane < 12, pltpu.roll(x, 12, 1), 0.0)
                both = jnp.where((lane >= 20) & (lane < 32), pltpu.roll(x, 20, 1), both)
                both = jnp.where(lane % 64 < 32, both, pltpu.roll(both, 32, 1))
                both = jnp.where(lane < 64, both, pltpu.roll(both, 64, 1))
            strips[i, pl.ds(row, OWN_TALL), :] = both
        return carry

    lax.fori_loop(0, 144 // OWN_TALL, cut, 0)


def rest_kernel(planes, state, block, near, adj_out, dens_out, emis_out, flux2, bank, part, rim):
    del near

    def give(row, at, adjoints, dens, seen):
        ground = block[GROUND, pl.ds(at, OWN_END), :]
        for b in range(BINS):
            adj_out[b, 0, pl.ds(at, OWN_END), :] = adjoints[b]
            emis_out[b, pl.ds(at, OWN_END), :] = ground * seen[b]
        dens_out[0, pl.ds(at, OWN_END), :] = dens

    second_half(OWN_TALL, OWN_END, BINS, block_field(planes), state, flux2, bank, part, rim, give)


def edge_kernel(deposition, strips_in, near, passed, adj, dens, emis, block, *refs):
    adj_out, dens_out, emis_out, strips, sides, turn, state, back, scale, flux2, bank, part, rim = refs
    lane = lax.broadcasted_iota(jnp.int32, (8, N), 1)
    parity = position()[1]
    sides[1 - parity] = near[0:LON_MSG, :]
    sides[parity] = passed[...]
    tall = lax.broadcasted_iota(jnp.int32, (N, N), 1) % 32
    strips[:, 8:BASE, :] = strips_in[:, 8:BASE, :]
    strips[:, BASE + N : BASE + N + 8, :] = strips_in[:, BASE + N : BASE + N + 8, :]
    for i, name in enumerate(STRIPS):
        wide = 2 if name in ("source", "land") else 4
        inside = (tall >= 16 - wide - (4 - wide)) & (tall < 12 + wide) | (tall >= 20 - wide) & (tall < 20)
        for b in range(BINS):
            p = PLACE[name] + (b if name in ("tracer", "adjoint", "source") else 0)
            at = 4 * p if p < MAIN else 4 * MAIN + 2 * (p - MAIN)
            turn[i, 32 * b + 12 : 32 * b + 12 + wide, :] = sides[1, at : at + wide, :]
            turn[i, 32 * b + 20 - wide : 32 * b + 20, :] = sides[0, at : at + wide, :]
        strips[i, BASE : BASE + N, :] = jnp.where(inside, turn[i].T, strips_in[i, BASE : BASE + N, :])
    turn[0, 0:4, :] = sides[1, LINES : LINES + 4, :]
    turn[0, 4:8, :] = sides[0, LINES : LINES + 4, :]
    turned = turn[0].T
    for i, name in enumerate(STRIPS):
        if name in ("source", "land"):
            continue
        low, high = strips[i, BASE - 8 : BASE, :], strips[i, BASE + N : BASE + N + 8, :]
        sub = lax.broadcasted_iota(jnp.int32, (8, N), 0)
        for b in range(BINS):
            p = PLACE[name] + (b if name in ("tracer", "adjoint") else 0)
            eight = pltpu.roll(turned[8 * p : 8 * p + 8], 32 * b + 12, 1)
            inside = (lane >= 32 * b + 12) & (lane < 32 * b + 20)
            half = pltpu.roll(eight, 4, 0)
            low = jnp.where(inside & (sub >= 4), half, low)
            high = jnp.where(inside & (sub < 4), half, high)
        strips[i, BASE - 8 : BASE, :] = low
        strips[i, BASE + N : BASE + N + 8, :] = high
    field = strip_field(strips)(EDGE_TALL)
    lane = lax.broadcasted_iota(jnp.int32, (EDGE_TALL, N), 1)
    rates = []
    for kind in range(8):
        rate = jnp.where(lane < 32, deposition[0, kind], deposition[1, kind])
        rate = jnp.where(lane < 64, rate, jnp.where(lane < 96, deposition[2, kind], deposition[3, kind]))
        rates.append(rate)

    def keep_of(row):
        land = field("land", 0, row)
        rate = jnp.zeros_like(land)
        for kind in range(8):
            rate = jnp.where(land == float(kind), rates[kind], rate)
        yield 1.0 - TIME_STEP * rate

    first_half(EDGE_TALL, 1, strip_field(strips), keep_of, state, back, scale)
    lane = lax.broadcasted_iota(jnp.int32, (EDGE_END, N), 1)
    left, right = lane < 4, lane >= N - 4

    def patch(value, b, old):
        value_right = pltpu.roll(value, (116 - 32 * b) % N, 1)
        value_left = pltpu.roll(value, (-32 * b - 20) % N, 1)
        return jnp.where(left, value_left, jnp.where(right, value_right, old))

    def give(row, at, adjoints, total, seen):
        ground = block[GROUND, pl.ds(at, EDGE_END), :]
        for b in range(BINS):
            adj_out[b, 0, pl.ds(at, EDGE_END), :] = patch(adjoints[0], b, adj[b, 0, pl.ds(at, EDGE_END), :])
            old = emis[b, pl.ds(at, EDGE_END), :]
            emis_out[b, pl.ds(at, EDGE_END), :] = jnp.where(left | right, ground * patch(seen[0], b, old), old)
        total = total + pltpu.roll(total, 32, 1)
        total = total + pltpu.roll(total, 64, 1)
        dens_out[0, pl.ds(at, EDGE_END), :] = patch(total, 0, dens[0, pl.ds(at, EDGE_END), :])

    second_half(EDGE_TALL, EDGE_END, 1, strip_field(strips), state, flux2, bank, part, rim, give)


def swaps(count, offset, closed):
    pairs = []
    for low in range(offset, count, 2):
        high = low + 1
        if high >= count and closed:
            continue
        pairs += [(low, high % count), (high % count, low)]
    return pairs


SMEM = pl.BlockSpec(memory_space=pltpu.SMEM)
VMEM = pl.BlockSpec(memory_space=pltpu.VMEM)
HBM = pl.BlockSpec(memory_space=pltpu.HBM)


def kernel_call(body, smem, arrays, out_shapes, scratch, place=VMEM, extra=(), flops=0, fast=True):
    return pl.pallas_call(
        body,
        out_shape=[pltpu.VMEM(s, F32) if fast else jax.ShapeDtypeStruct(s, F32) for s in out_shapes],
        in_specs=[SMEM] * smem + [place] * (len(arrays) - smem),
        out_specs=[VMEM] * len(out_shapes),
        scratch_shapes=[pltpu.VMEM(s, F32) for s in scratch] + list(extra),
        compiler_params=pltpu.CompilerParams(vmem_limit_bytes=24 * 1024 * 1024),
        cost_estimate=pl.CostEstimate(flops=flops, bytes_accessed=0, transcendentals=0) if flops else None,
    )(*arrays)


def shards(*args):
    ins, deposition = args[:10], args[10].T
    lats, lons = lax.axis_size("lat"), lax.axis_size("lon")
    msg = (LAT_MSG, N)
    ins = [pltpu.with_memory_space_constraint(x, pltpu.HBM) for x in ins]
    out0, out1, lines, block = kernel_call(
        pack_kernel,
        0,
        ins,
        [msg, msg, (2, LON_MSG, N), (PLANES, N, N)],
        [],
        HBM,
        [pltpu.VMEM(x.shape, x.dtype) for x in ins]
        + [pltpu.VMEM((2, *msg), F32), pltpu.VMEM((N, N), F32), pltpu.SemaphoreType.DMA((10,))],
    )
    got0 = lax.ppermute(out0, "lat", swaps(lats, 0, True))
    got1 = lax.ppermute(out1, "lat", swaps(lats, 1, True))
    (both,) = kernel_call(corner_kernel, 0, (got0, got1, lines), [(2 * LON_MSG, N)], [(2, *msg), (N, N)])
    near = lax.ppermute(both, "lon", swaps(lons, 0, False))
    plane = (ROWS, N)
    planes, state, strips = kernel_call(
        own_kernel,
        1,
        (deposition, block, got0, got1, both),
        [(MAIN + EXTRA, *plane), (places(BINS)[1], *plane), (len(STRIPS), *plane)],
        [(2, *msg), (BINS, *plane), plane],
        flops=OWN_FLOPS,
    )
    onward = [(i, (i + (2 if i % 2 == 0 else lons - 2)) % lons) for i in range(lons)]
    near, strips = lax.optimization_barrier((near, strips))
    passed = lax.ppermute(near[LON_MSG:], "lon", onward)
    shapes = [(BINS, 1, N, N), (1, N, N), (BINS, N, N)]
    adj, dens, emis = kernel_call(
        rest_kernel,
        0,
        (planes, state, block, near),
        shapes,
        [(BINS, *plane), (BINS, *plane), (BINS, *plane), (3, *plane)],
        flops=OWN_FLOPS,
    )
    outs = kernel_call(
        edge_kernel,
        1,
        (deposition, strips, near, passed, adj, dens, emis, block),
        shapes,
        [
            (len(STRIPS), *plane),
            (2, LON_MSG, N),
            (len(STRIPS), N, N),
            (places(1)[1], *plane),
            (1, *plane),
            plane,
            (1, *plane),
            (1, *plane),
            (1, *plane),
            (3, *plane),
        ],
        fast=False,
    )
    return tuple(outs)


def solution(mesh):
    return jax.shard_map(
        shards,
        mesh=mesh,
        in_specs=(
            P(None, None, "lat", "lon"),
            P(None, None, "lat", "lon"),
            P(None, "lat", "lon"),
            P(None, "lat", "lon"),
            P(None, "lat", "lon"),
            P(None, "lat", "lon"),
            P(None, "lat", "lon"),
            P("lat", "lon"),
            P("lat", "lon"),
            P(None, "lat", "lon"),
            P(),
        ),
        out_specs=(P(None, None, "lat", "lon"), P(None, "lat", "lon"), P(None, "lat", "lon")),
        check_vma=False,
    )
```

time: 61.1 us -> 43.2 us (0.71)
  the two profiles are of different devices: /device:TPU:32 before, /device:TPU:1 now
where the time goes in v2:
time: 43.2 us; the launch traced here: 43 us
  starting transfers between devices  24 us (56%)
  Pallas kernels  11.9 us (28%)
  waiting for transfers between devices  6.36 us (15%)
  between operations  0.74 us (2%)
    pallas_call x5, Pallas kernels, kernel_call(): pl.pallas_call(body, out_shape=[pltpu.VMEM(s, F32) if fast else jax.Shape...  11.9 us
    ppermute x1, starting transfers between devices, shards(): near = lax.ppermute(both, 'lon', swaps(lons, 0, False))  10.1 us
    ppermute x1, starting transfers between devices, shards(): got0 = lax.ppermute(out0, 'lat', swaps(lats, 0, True))  8.79 us
    ppermute x1, waiting for transfers between devices, shards(): got1 = lax.ppermute(out1, 'lat', swaps(lats, 1, True))  3.25 us
    ppermute x1, starting transfers between devices, shards(): passed = lax.ppermute(near[LON_MSG:], 'lon', onward)  3.2 us
    ppermute x1, waiting for transfers between devices, shards(): passed = lax.ppermute(near[LON_MSG:], 'lon', onward)  3.1 us
    ppermute x1, starting transfers between devices, shards(): got1 = lax.ppermute(out1, 'lat', swaps(lats, 1, True))  1.92 us
  transfers between devices with their start and end apart: 4, of which 2 were waited for; matrix products, arithmetic and copies ran while one was open for 0% of the time, Pallas kernels for 14%

profile of v2, /device:TPU:1, one launch (start us, length us, event | category | flops | bytes accessed | tf_op | source)
XLA Modules:
  0.0 43.0 jit_solution(11333524784457442476)
XLA Ops:
  0.6 0.0 copy-start
  0.6 1.8 %shard_map.130 = (f32[56,128]{1,0:T(8,128)S(1)}, f32[56,128]{1,0:T(8,128)S(1)}, f32[2,64,128]{2,1,0:T(8,128)S(1)}, f32[17,128,128]{2,1,0:T(8,128)S(1)}) custom-call(f32[4,1,128,128]{3,2,1,0:T(8,128)} %refs_0_.1, f32[4,1,128,128]{3,2,1,0:T(8,128)} %refs_1_.1, f32[1,128,128]{2,1,0:T(8,128)} %refs_2_.1, f32[1,128,128]{2,1,0:T(8,128)} %refs_3_.1, ...), custom_call_target="tpu_custom_call" | custom-call | tf_op jit(solution)/shard_map/pallas_call | solution.py:455
  2.4 8.8 %collective-permute-start = (f32[56,128]{1,0:T(8,128)S(1)}, f32[56,128]{1,0:T(8,128)S(1)}, u32[]{:S(2)}, u32[]{:S(2)}) collective-permute-start(f32[56,128]{1,0:T(8,128)S(1)} %get-tuple-element.15), channel_id=1, source_target_pairs={{0,1},{1,0},{2,3},{3,2},{4,5},{5,4},{6,7},{7,6},{8,9},{9,8},{10,11... | collective-permute-start | bytes 86024 | tf_op jit(solution)/shard_map/ppermute | solution.py:481
  11.2 1.9 %collective-permute-start.1 = (f32[56,128]{1,0:T(8,128)S(1)}, f32[56,128]{1,0:T(8,128)S(1)}, u32[]{:S(2)}, u32[]{:S(2)}) collective-permute-start(f32[56,128]{1,0:T(8,128)S(1)} %get-tuple-element.16), channel_id=1, source_target_pairs={{1,2},{2,1},{3,4},{4,3},{5,6},{6,5},{7,8},{8,7},{9,10},{10,9},{11,... | collective-permute-start | bytes 86024 | tf_op jit(solution)/shard_map/ppermute | solution.py:482
  13.2 0.0 collective-permute-done.got0.refs_1_
  13.2 3.3 %collective-permute-done.1.got1.refs_2_ = f32[56,128]{1,0:T(8,128)S(1)} collective-permute-done((f32[56,128]{1,0:T(8,128)S(1)}, f32[56,128]{1,0:T(8,128)S(1)}, u32[]{:S(2)}, u32[]{:S(2)}) %collective-permute-start.1) | collective-permute-done | bytes 28704 | tf_op jit(solution)/shard_map/ppermute | solution.py:482
  16.4 0.1 shard_map.131.refs_3_
  16.5 10.1 %collective-permute-start.2 = (f32[128,128]{1,0:T(8,128)S(1)}, f32[128,128]{1,0:T(8,128)S(1)}, u32[]{:S(2)}, u32[]{:S(2)}) collective-permute-start(f32[128,128]{1,0:T(8,128)S(1)} %shard_map.131.refs_3_), channel_id=1, source_target_pairs={{0,16},{16,0},{32,48},{48,32},{64,80},{80,64},{96,112},{112,96},{1... | collective-permute-start | bytes 196616 | tf_op jit(solution)/shard_map/ppermute | solution.py:484
  26.6 0.0 copy-done
  26.6 4.3 %shard_map.132 = (f32[16,160,128]{2,1,0:T(8,128)S(1)}, f32[30,160,128]{2,1,0:T(8,128)S(1)}, f32[7,160,128]{2,1,0:T(8,128)S(1)}) custom-call(f32[4,8]{1,0:T(4,128)S(1)} %bitcast.1, f32[17,128,128]{2,1,0:T(8,128)S(1)} %get-tuple-element.18.refs_0_.block, f32[56,128]{1,0:T(8,128)S(1)} %collective-permute-done.got0.refs_1_, ...), custom_call_target="tpu_custom_call" | custom-call | flops 3000000 | tf_op jit(solution)/shard_map/pallas_call | solution.py:455
  30.9 0.0 collective-permute-done.2.near
  31.0 3.2 %collective-permute-start.3 = (f32[64,128]{1,0:T(8,128)S(1)}, f32[64,128]{1,0:T(8,128)S(1)}, u32[]{:S(2)}, u32[]{:S(2)}) collective-permute-start(f32[64,128]{1,0:T(8,128)S(1)} %slice.3), channel_id=1, source_target_pairs={{0,32},{16,496},{32,64},{48,16},{64,96},{80,48},{96,128},{112,80},... | collective-permute-start | bytes 98312 | tf_op jit(solution)/shard_map/ppermute | solution.py:496
  34.2 1.8 %shard_map.133 = (f32[4,1,128,128]{3,2,1,0:T(8,128)S(1)}, f32[1,128,128]{2,1,0:T(8,128)S(1)}, f32[4,128,128]{2,1,0:T(8,128)S(1)}) custom-call(f32[16,160,128]{2,1,0:T(8,128)S(1)} %get-tuple-element.22.planes, f32[30,160,128]{2,1,0:T(8,128)S(1)} %get-tuple-element.23.state, f32[17,128,128]{2,1,0:T(8,128)S(1)} %get-tuple-element.18.refs_0_.block, ...), custom_call_target="tpu_custom_call" | custom-call | flops 3000000 | tf_op jit(solution)/shard_map/pallas_call | solution.py:455
  36.0 3.1 %collective-permute-done.3.passed = f32[64,128]{1,0:T(8,128)S(1)} collective-permute-done((f32[64,128]{1,0:T(8,128)S(1)}, f32[64,128]{1,0:T(8,128)S(1)}, u32[]{:S(2)}, u32[]{:S(2)}) %collective-permute-start.3) | collective-permute-done | bytes 32800 | tf_op jit(solution)/shard_map/ppermute | solution.py:496
  39.1 3.9 %shard_map.134 = (f32[4,1,128,128]{3,2,1,0:T(8,128)}, f32[1,128,128]{2,1,0:T(8,128)}, f32[4,128,128]{2,1,0:T(8,128)}) custom-call(f32[4,8]{1,0:T(4,128)S(1)} %bitcast.2, f32[7,160,128]{2,1,0:T(8,128)S(1)} %get-tuple-element.20.strips_in, f32[128,128]{1,0:T(8,128)S(1)} %collective-permute-done.2.near, f32[64,128]{1,0:T(8,128)S(1)} %collective-permute-done.3.passed, ...), custom_call_target="tpu_custom_call" | custom-call | tf_op jit(solution)/shard_map/pallas_call | solution.py:455
  (1 shorter events, 0.0 us)
Async XLA Ops:
  0.6 26.0 %copy-start = (f32[8,4]{0,1:T(4,128)S(1)}, f32[8,4]{0,1:T(4,128)}, u32[]{:S(2)}) copy-start(f32[8,4]{0,1:T(4,128)} %param.21) | copy-start | bytes 388
  2.4 10.7 %collective-permute-start = (f32[56,128]{1,0:T(8,128)S(1)}, f32[56,128]{1,0:T(8,128)S(1)}, u32[]{:S(2)}, u32[]{:S(2)}) collective-permute-start(f32[56,128]{1,0:T(8,128)S(1)} %get-tuple-element.15), channel_id=1, source_target_pairs={{0,1},{1,0},{2,3},{3,2},{4,5},{5,4},{6,7},{7,6},{8,9},{9,8},{10,11... | collective-permute-start | bytes 86024 | tf_op jit(solution)/shard_map/ppermute | solution.py:481
  11.2 5.2 %collective-permute-start.1 = (f32[56,128]{1,0:T(8,128)S(1)}, f32[56,128]{1,0:T(8,128)S(1)}, u32[]{:S(2)}, u32[]{:S(2)}) collective-permute-start(f32[56,128]{1,0:T(8,128)S(1)} %get-tuple-element.16), channel_id=1, source_target_pairs={{1,2},{2,1},{3,4},{4,3},{5,6},{6,5},{7,8},{8,7},{9,10},{10,9},{11,... | collective-permute-start | bytes 86024 | tf_op jit(solution)/shard_map/ppermute | solution.py:482
  16.5 14.4 %collective-permute-start.2 = (f32[128,128]{1,0:T(8,128)S(1)}, f32[128,128]{1,0:T(8,128)S(1)}, u32[]{:S(2)}, u32[]{:S(2)}) collective-permute-start(f32[128,128]{1,0:T(8,128)S(1)} %shard_map.131.refs_3_), channel_id=1, source_target_pairs={{0,16},{16,0},{32,48},{48,32},{64,80},{80,64},{96,112},{112,96},{1... | collective-permute-start | bytes 196616 | tf_op jit(solution)/shard_map/ppermute | solution.py:484
  31.0 8.1 %collective-permute-start.3 = (f32[64,128]{1,0:T(8,128)S(1)}, f32[64,128]{1,0:T(8,128)S(1)}, u32[]{:S(2)}, u32[]{:S(2)}) collective-permute-start(f32[64,128]{1,0:T(8,128)S(1)} %slice.3), channel_id=1, source_target_pairs={{0,32},{16,496},{32,64},{48,16},{64,96},{80,48},{96,128},{112,80},... | collective-permute-start | bytes 98312 | tf_op jit(solution)/shard_map/ppermute | solution.py:496

commit v3 on v2

--- a/solution.py
+++ b/solution.py
@@ -15,12 +15,14 @@
 EAST, NORTH, RHO = 2 * BINS, 2 * BINS + 1, 2 * BINS + 2
 LINES = 4 * MAIN + 2 * EXTRA
 LAT_MSG = 56
-LON_MSG = 64
+LON_MSG = 56
 BASE = 16
 ROWS = 160
 OWN_FLOPS = 3_000_000
-OWN_TALL, OWN_END = 24, 32
-EDGE_TALL, EDGE_END = 48, 64
+OWN_TALL, FIRST_TALL = 48, 48
+REST_TALL, REST_END = 24, 32
+EARLY = 10
+EDGE_TALL, EDGE_END = 144, 128
 PLANES = MAIN + EXTRA + 1
 GROUND = MAIN + EXTRA
 F32 = jnp.float32
@@ -106,7 +108,7 @@
 
 def place_lat(info, got0, got1, halo):
     parity = info[0]
-    halo[1 - parity] = got0[...]
+    halo[1 - parity] = got0[1 - parity]
     halo[parity] = got1[...]
     at = 4 * RHO
 
@@ -119,7 +121,7 @@
         halo[1, at : at + 4, :] = jnp.ones((4, N), F32)
 
 
-def corner_kernel(got0, got1, lines, out, halo, rows):
+def corner_kernel(got1, got0, lines, out, halo, rows):
     info = position()
     place_lat(info, got0, got1, halo)
     rows[8 * MAIN :, :] = jnp.zeros((N - 8 * MAIN, N), F32)
@@ -130,17 +132,17 @@
     parity = info[1]
     out[0:LON_MSG, :] = lines[1 - parity]
     out[LON_MSG:, :] = lines[parity]
-    left, right = turned[0:8][:4], turned[N - 8 :][4:]
+    left, right = turned[0:8][:2], turned[N - 8 :][6:]
 
     @pl.when(parity == 0)
     def _():
-        out[LINES : LINES + 4, :] = right
-        out[LON_MSG + LINES : LON_MSG + LINES + 4, :] = left
+        out[LINES : LON_MSG, :] = right
+        out[LON_MSG + LINES : 2 * LON_MSG, :] = left
 
     @pl.when(parity == 1)
     def _():
-        out[LINES : LINES + 4, :] = left
-        out[LON_MSG + LINES : LON_MSG + LINES + 4, :] = right
+        out[LINES : LON_MSG, :] = left
+        out[LON_MSG + LINES : 2 * LON_MSG, :] = right
 
 
 def shift(x, s):
@@ -168,20 +170,25 @@
     return total - jnp.where(winds[3], grads[3], 0.0) - jnp.where(winds[0], 0.0, grads[0])
 
 
-def places(count):
+def lay(sizes):
     at, total = {}, 0
-    for name, size in (("mass", 2), ("keep", count), ("g", count), ("middle", count), ("seen", count), ("gm", count), ("flux", 2 * count)):
+    for name, size in sizes:
         at[name] = total
         total += size
     return at, total
 
 
-def first_half(tall, count, field_of, keep_of, state, back, scale_ref):
+def places(count):
+    return lay((("mass", 2), ("scale", 1), ("keep", count), ("g", count)))
+
+
+def results(count):
+    return lay((("middle", count), ("seen", count), ("gm", count), ("flux", 2 * count)))
+
+
+def prepare_half(tall, count, field_of, keep_of, state):
     field = field_of(tall)
     at, _ = places(count)
-
-    def get(name, b, row):
-        return state[at[name] + b, pl.ds(row, tall), :]
 
     def put(name, b, row, value):
         state[at[name] + b, pl.ds(row, tall), :] = value
@@ -192,7 +199,7 @@
         put("mass", 0, row, field("east", 0, row) * (rho + shift(rho, -1)) * (1.0 / 12.0))
         put("mass", 1, row, field("north", 0, row) * (rho + field("rho", 0, row - 1)) * (1.0 / 12.0))
         scale = COURANT / rho
-        scale_ref[pl.ds(row, tall), :] = scale
+        put("scale", 0, row, scale)
         for b, kept in enumerate(keep_of(row)):
             put("g", b, row, field("adjoint", b, row) * scale)
             put("keep", b, row, kept)
@@ -200,10 +207,24 @@
 
     lax.fori_loop(0, 144 // tall, prepare, 0)
 
+
+def first_half(tall, count, field_of, start, state, back):
+    field = field_of(tall)
+    at, _ = places(count)
+    to, _ = results(count)
+
+    def get(name, b, row):
+        if name in at:
+            return start[at[name] + b, pl.ds(row, tall), :]
+        return state[to[name] + b, pl.ds(row, tall), :]
+
+    def put(name, b, row, value):
+        state[to[name] + b, pl.ds(row, tall), :] = value
+
     def first(t, carry):
         row = pl.multiple_of(8 + t * tall, 8)
         blows_e, blows_n = field("east", 0, row) > 0.0, field("north", 0, row) > 0.0
-        mass_e, mass_n, scale = get("mass", 0, row), get("mass", 1, row), scale_ref[pl.ds(row, tall), :]
+        mass_e, mass_n, scale = get("mass", 0, row), get("mass", 1, row), get("scale", 0, row)
         for b in range(count):
             c, kept = field("tracer", b, row), get("keep", b, row)
             fe = mass_e * face(blows_e, shift(c, -2), shift(c, -1), c, shift(c, 1))
@@ -224,7 +245,7 @@
     def join(t, carry):
         row = pl.multiple_of(8 + t * tall, 8)
         winds = [field("north", 0, row + dr) > 0.0 for dr in (-1, 0, 1, 2)]
-        scale = scale_ref[pl.ds(row, tall), :]
+        scale = get("scale", 0, row)
         for b in range(count):
             change = get("flux", count + b, row + 1) - get("flux", count + b, row)
             put("middle", b, row, get("middle", b, row) - scale * change)
@@ -236,12 +257,15 @@
     lax.fori_loop(0, 144 // tall, join, 0)
 
 
-def second_half(tall, end_tall, count, field_of, state, flux2, bank, part, rim, give):
+def second_half(tall, end_tall, count, field_of, start, state, flux2, bank, part, rim, give):
     at, _ = places(count)
+    to, _ = results(count)
     field = field_of(tall)
 
     def get(name, b, row, size=tall):
-        return state[at[name] + b, pl.ds(row, size), :]
+        if name in at:
+            return start[at[name] + b, pl.ds(row, size), :]
+        return state[to[name] + b, pl.ds(row, size), :]
 
     def last(t, carry):
         row = pl.multiple_of(8 + t * tall, 8)
@@ -306,7 +330,8 @@
 
 def own_kernel(deposition, *refs):
     info = position()
-    block, got0, got1, _, planes, state, strips, halo, back, scale = refs
+    block, got0, got1, _, planes, start, strips, *outs, halo = refs[:11]
+    work = refs[11:]
     place_lat(info, got0, got1, halo)
     for p in range(MAIN):
         planes[p, BASE : BASE + N, :] = block[p]
@@ -327,7 +352,7 @@
                 rate = jnp.where(land == float(kind), deposition[b, kind], rate)
             yield 1.0 - TIME_STEP * rate
 
-    first_half(OWN_TALL, BINS, block_field(planes), keep_of, state, back, scale)
+    prepare_half(OWN_TALL, BINS, block_field(planes), keep_of, start)
     lane = lax.broadcasted_iota(jnp.int32, (OWN_TALL, N), 1)
 
     def cut(t, carry):
@@ -350,22 +375,40 @@
 
     lax.fori_loop(0, 144 // OWN_TALL, cut, 0)
 
-
-def rest_kernel(planes, state, block, near, adj_out, dens_out, emis_out, flux2, bank, part, rim):
+    @pl.when(runs_early())
+    def _():
+        both_halves(planes, start, block, outs, work)
+
+
+def runs_early():
+    return (lax.axis_index("lon") % 2 == 1) | (lax.axis_index("lat") >= EARLY * lax.axis_size("lat") // 16)
+
+
+def both_halves(planes, start, block, outs, work):
+    adj_out, dens_out, emis_out = outs
+    state, back, flux2, bank, part, rim = work
+    first_half(FIRST_TALL, BINS, block_field(planes), start, state, back)
+
+    def give(row, at, adjoints, dens, seen):
+        ground = block[GROUND, pl.ds(at, REST_END), :]
+        for b in range(BINS):
+            adj_out[b, 0, pl.ds(at, REST_END), :] = adjoints[b]
+            emis_out[b, pl.ds(at, REST_END), :] = ground * seen[b]
+        dens_out[0, pl.ds(at, REST_END), :] = dens
+
+    second_half(REST_TALL, REST_END, BINS, block_field(planes), start, state, flux2, bank, part, rim, give)
+
+
+def rest_kernel(planes, start, block, near, *refs):
     del near
 
-    def give(row, at, adjoints, dens, seen):
-        ground = block[GROUND, pl.ds(at, OWN_END), :]
-        for b in range(BINS):
-            adj_out[b, 0, pl.ds(at, OWN_END), :] = adjoints[b]
-            emis_out[b, pl.ds(at, OWN_END), :] = ground * seen[b]
-        dens_out[0, pl.ds(at, OWN_END), :] = dens
-
-    second_half(OWN_TALL, OWN_END, BINS, block_field(planes), state, flux2, bank, part, rim, give)
+    @pl.when(jnp.logical_not(runs_early()))
+    def _():
+        both_halves(planes, start, block, refs[3:6], refs[6:])
 
 
 def edge_kernel(deposition, strips_in, near, passed, adj, dens, emis, block, *refs):
-    adj_out, dens_out, emis_out, strips, sides, turn, state, back, scale, flux2, bank, part, rim = refs
+    adj_out, dens_out, emis_out, strips, sides, turn, start, state, back, flux2, bank, part, rim = refs
     lane = lax.broadcasted_iota(jnp.int32, (8, N), 1)
     parity = position()[1]
     sides[1 - parity] = near[0:LON_MSG, :]
@@ -382,8 +425,8 @@
             turn[i, 32 * b + 12 : 32 * b + 12 + wide, :] = sides[1, at : at + wide, :]
             turn[i, 32 * b + 20 - wide : 32 * b + 20, :] = sides[0, at : at + wide, :]
         strips[i, BASE : BASE + N, :] = jnp.where(inside, turn[i].T, strips_in[i, BASE : BASE + N, :])
-    turn[0, 0:4, :] = sides[1, LINES : LINES + 4, :]
-    turn[0, 4:8, :] = sides[0, LINES : LINES + 4, :]
+    turn[0, 0:2, :] = sides[1, LINES:LON_MSG, :]
+    turn[0, 6:8, :] = sides[0, LINES:LON_MSG, :]
     turned = turn[0].T
     for i, name in enumerate(STRIPS):
         if name in ("source", "land"):
@@ -414,7 +457,8 @@
             rate = jnp.where(land == float(kind), rates[kind], rate)
         yield 1.0 - TIME_STEP * rate
 
-    first_half(EDGE_TALL, 1, strip_field(strips), keep_of, state, back, scale)
+    prepare_half(EDGE_TALL, 1, strip_field(strips), keep_of, start)
+    first_half(EDGE_TALL, 1, strip_field(strips), start, state, back)
     lane = lax.broadcasted_iota(jnp.int32, (EDGE_END, N), 1)
     left, right = lane < 4, lane >= N - 4
 
@@ -433,7 +477,7 @@
         total = total + pltpu.roll(total, 64, 1)
         dens_out[0, pl.ds(at, EDGE_END), :] = patch(total, 0, dens[0, pl.ds(at, EDGE_END), :])
 
-    second_half(EDGE_TALL, EDGE_END, 1, strip_field(strips), state, flux2, bank, part, rim, give)
+    second_half(EDGE_TALL, EDGE_END, 1, strip_field(strips), start, state, flux2, bank, part, rim, give)
 
 
 def swaps(count, offset, closed):
@@ -451,13 +495,14 @@
 HBM = pl.BlockSpec(memory_space=pltpu.HBM)
 
 
-def kernel_call(body, smem, arrays, out_shapes, scratch, place=VMEM, extra=(), flops=0, fast=True):
+def kernel_call(body, smem, arrays, out_shapes, scratch, place=VMEM, extra=(), flops=0, fast=True, aliases=None):
     return pl.pallas_call(
         body,
         out_shape=[pltpu.VMEM(s, F32) if fast else jax.ShapeDtypeStruct(s, F32) for s in out_shapes],
         in_specs=[SMEM] * smem + [place] * (len(arrays) - smem),
         out_specs=[VMEM] * len(out_shapes),
         scratch_shapes=[pltpu.VMEM(s, F32) for s in scratch] + list(extra),
+        input_output_aliases=aliases or {},
         compiler_params=pltpu.CompilerParams(vmem_limit_bytes=24 * 1024 * 1024),
         cost_estimate=pl.CostEstimate(flops=flops, bytes_accessed=0, transcendentals=0) if flops else None,
     )(*arrays)
@@ -478,29 +523,31 @@
         [pltpu.VMEM(x.shape, x.dtype) for x in ins]
         + [pltpu.VMEM((2, *msg), F32), pltpu.VMEM((N, N), F32), pltpu.SemaphoreType.DMA((10,))],
     )
-    got0 = lax.ppermute(out0, "lat", swaps(lats, 0, True))
     got1 = lax.ppermute(out1, "lat", swaps(lats, 1, True))
-    (both,) = kernel_call(corner_kernel, 0, (got0, got1, lines), [(2 * LON_MSG, N)], [(2, *msg), (N, N)])
+    got0 = lax.all_gather(out0, "lat", axis_index_groups=[[i, i + 1] for i in range(0, lats, 2)])
+    (both,) = kernel_call(corner_kernel, 0, (got1, got0, lines), [(2 * LON_MSG, N)], [(2, *msg), (N, N)])
     near = lax.ppermute(both, "lon", swaps(lons, 0, False))
     plane = (ROWS, N)
-    planes, state, strips = kernel_call(
+    shapes = [(BINS, 1, N, N), (1, N, N), (BINS, N, N)]
+    work = [(results(BINS)[1], *plane)] + [(BINS, *plane)] * 4 + [(3, *plane)]
+    planes, start, strips, *first_outs = kernel_call(
         own_kernel,
         1,
         (deposition, block, got0, got1, both),
-        [(MAIN + EXTRA, *plane), (places(BINS)[1], *plane), (len(STRIPS), *plane)],
-        [(2, *msg), (BINS, *plane), plane],
+        [(MAIN + EXTRA, *plane), (places(BINS)[1], *plane), (len(STRIPS), *plane), *shapes],
+        [(2, *msg), *work],
         flops=OWN_FLOPS,
     )
     onward = [(i, (i + (2 if i % 2 == 0 else lons - 2)) % lons) for i in range(lons)]
     near, strips = lax.optimization_barrier((near, strips))
     passed = lax.ppermute(near[LON_MSG:], "lon", onward)
-    shapes = [(BINS, 1, N, N), (1, N, N), (BINS, N, N)]
     adj, dens, emis = kernel_call(
         rest_kernel,
         0,
-        (planes, state, block, near),
+        (planes, start, block, near, *first_outs),
         shapes,
-        [(BINS, *plane), (BINS, *plane), (BINS, *plane), (3, *plane)],
+        work,
+        aliases={4: 0, 5: 1, 6: 2},
         flops=OWN_FLOPS,
     )
     outs = kernel_call(
@@ -513,8 +560,8 @@
             (2, LON_MSG, N),
             (len(STRIPS), N, N),
             (places(1)[1], *plane),
+            (results(1)[1], *plane),
             (1, *plane),
-            plane,
             (1, *plane),
             (1, *plane),
             (1, *plane),

time: 43.2 us -> 38.2 us (0.88)
  the two profiles are of different devices: /device:TPU:1 before, /device:TPU:414 now
where the time goes in v3:
time: 38.2 us; the launch traced here: 38 us
  waiting for transfers between devices  15.6 us (41%)
  Pallas kernels  9.92 us (26%)
  starting transfers between devices  9.88 us (26%)
  blocking collectives  1.85 us (5%)
  between operations  0.7 us (2%)
    pallas_call x5, Pallas kernels, kernel_call(): pl.pallas_call(body, out_shape=[pltpu.VMEM(s, F32) if fast else jax.Shape...  9.92 us
    ppermute x1, waiting for transfers between devices, shards(): near = lax.ppermute(both, 'lon', swaps(lons, 0, False))  8.27 us
    ppermute x1, waiting for transfers between devices, shards(): passed = lax.ppermute(near[LON_MSG:], 'lon', onward)  6.39 us
    ppermute x1, starting transfers between devices, shards(): near = lax.ppermute(both, 'lon', swaps(lons, 0, False))  3.68 us
    ppermute x1, starting transfers between devices, shards(): got1 = lax.ppermute(out1, 'lat', swaps(lats, 1, True))  3.56 us
    ppermute x1, starting transfers between devices, shards(): passed = lax.ppermute(near[LON_MSG:], 'lon', onward)  2.64 us
    all_gather x1, blocking collectives, shards(): lax.all_gather(out0, 'lat', axis_index_groups=[[i, i + 1] for i in range(...  1.85 us
    ppermute x1, waiting for transfers between devices, shards(): got1 = lax.ppermute(out1, 'lat', swaps(lats, 1, True))  0.98 us
  transfers between devices with their start and end apart: 3, of which 3 were waited for; matrix products, arithmetic and copies ran while one was open for 0% of the time, Pallas kernels for 14%

profile of v3, /device:TPU:414, one launch (start us, length us, event | category | flops | bytes accessed | tf_op | source)
XLA Modules:
  0.0 38.0 jit_solution(4718405382506399074)
XLA Ops:
  0.6 0.0 copy-start
  0.6 1.8 %shard_map.130 = (f32[56,128]{1,0:T(8,128)S(1)}, f32[56,128]{1,0:T(8,128)S(1)}, f32[2,56,128]{2,1,0:T(8,128)S(1)}, f32[17,128,128]{2,1,0:T(8,128)S(1)}) custom-call(f32[4,1,128,128]{3,2,1,0:T(8,128)} %refs_0_.1, f32[4,1,128,128]{3,2,1,0:T(8,128)} %refs_1_.1, f32[1,128,128]{2,1,0:T(8,128)} %refs_2_.1, f32[1,128,128]{2,1,0:T(8,128)} %refs_3_.1, ...), custom_call_target="tpu_custom_call" | custom-call | tf_op jit(solution)/shard_map/pallas_call | solution.py:499
  2.4 3.6 %collective-permute-start = (f32[56,128]{1,0:T(8,128)S(1)}, f32[56,128]{1,0:T(8,128)S(1)}, u32[]{:S(2)}, u32[]{:S(2)}) collective-permute-start(f32[56,128]{1,0:T(8,128)S(1)} %get-tuple-element.18), channel_id=1, source_target_pairs={{1,2},{2,1},{3,4},{4,3},{5,6},{6,5},{7,8},{8,7},{9,10},{10,9},{11,... | collective-permute-start | bytes 86024 | tf_op jit(solution)/shard_map/ppermute | solution.py:526
  6.0 1.8 %all-gather = f32[112,128]{1,0:T(8,128)S(1)} all-gather(f32[56,128]{1,0:T(8,128)S(1)} %get-tuple-element.19), channel_id=2, replica_groups={{0,1},{2,3},{4,5},{6,7},{8,9},{10,11},{12,13},{14,15},{16,17},{18,19},{..., dimensions={0}, use_global_device_ids=true | all-gather | bytes 86016 | tf_op jit(solution)/shard_map/all_gather | solution.py:527
  7.9 1.0 %collective-permute-done.got1.refs_2_ = f32[56,128]{1,0:T(8,128)S(1)} collective-permute-done((f32[56,128]{1,0:T(8,128)S(1)}, f32[56,128]{1,0:T(8,128)S(1)}, u32[]{:S(2)}, u32[]{:S(2)}) %collective-permute-start) | collective-permute-done | bytes 28704 | tf_op jit(solution)/shard_map/ppermute | solution.py:526
  8.8 0.1 shard_map.131.refs_3_
  8.9 3.7 %collective-permute-start.1 = (f32[112,128]{1,0:T(8,128)S(1)}, f32[112,128]{1,0:T(8,128)S(1)}, u32[]{:S(2)}, u32[]{:S(2)}) collective-permute-start(f32[112,128]{1,0:T(8,128)S(1)} %shard_map.131.refs_3_), channel_id=1, source_target_pairs={{0,16},{16,0},{32,48},{48,32},{64,80},{80,64},{96,112},{112,96},{1... | collective-permute-start | bytes 172040 | tf_op jit(solution)/shard_map/ppermute | solution.py:529
  12.6 0.0 copy-done
  12.6 5.3 %shard_map.132 = (f32[16,160,128]{2,1,0:T(8,128)S(1)}, f32[11,160,128]{2,1,0:T(8,128)S(1)}, f32[7,160,128]{2,1,0:T(8,128)S(1)}, f32[4,1,128,128]{3,2,1,0:T(8,128...) custom-call(f32[4,8]{1,0:T(4,128)S(1)} %bitcast.4, f32[17,128,128]{2,1,0:T(8,128)S(1)} %get-tuple-element.21.refs_0_.block, ...), custom_call_target="tpu_custom_call" | custom-call | flops 3000000 | tf_op jit(solution)/shard_map/pallas_call | solution.py:499
  17.9 8.3 %collective-permute-done.1.near = f32[112,128]{1,0:T(8,128)S(1)} collective-permute-done((f32[112,128]{1,0:T(8,128)S(1)}, f32[112,128]{1,0:T(8,128)S(1)}, u32[]{:S(2)}, u32[]{:S(2)}) %collective-permute-start.1) | collective-permute-done | bytes 57376 | tf_op jit(solution)/shard_map/ppermute | solution.py:529
  26.2 2.6 %collective-permute-start.2 = (f32[56,128]{1,0:T(8,128)S(1)}, f32[56,128]{1,0:T(8,128)S(1)}, u32[]{:S(2)}, u32[]{:S(2)}) collective-permute-start(f32[56,128]{1,0:T(8,128)S(1)} %slice.3), channel_id=1, source_target_pairs={{0,32},{16,496},{32,64},{48,16},{64,96},{80,48},{96,128},{112,80},... | collective-permute-start | bytes 86024 | tf_op jit(solution)/shard_map/ppermute | solution.py:543
  28.9 6.4 %collective-permute-done.2.passed = f32[56,128]{1,0:T(8,128)S(1)} collective-permute-done((f32[56,128]{1,0:T(8,128)S(1)}, f32[56,128]{1,0:T(8,128)S(1)}, u32[]{:S(2)}, u32[]{:S(2)}) %collective-permute-start.2) | collective-permute-done | bytes 28704 | tf_op jit(solution)/shard_map/ppermute | solution.py:543
  35.3 2.7 %shard_map.134 = (f32[4,1,128,128]{3,2,1,0:T(8,128)}, f32[1,128,128]{2,1,0:T(8,128)}, f32[4,128,128]{2,1,0:T(8,128)}) custom-call(f32[4,8]{1,0:T(4,128)S(1)} %bitcast.5, f32[7,160,128]{2,1,0:T(8,128)S(1)} %get-tuple-element.23.strips_in, f32[112,128]{1,0:T(8,128)S(1)} %collective-permute-done.1.near, f32[56,128]{1,0:T(8,128)S(1)} %collective-permute-done.2.passed, ...), custom_call_target="tpu_custom_call" | custom-call | tf_op jit(solution)/shard_map/pallas_call | solution.py:499
  (2 shorter events, 0.0 us)
Async XLA Ops:
  0.6 12.0 %copy-start = (f32[8,4]{0,1:T(4,128)S(1)}, f32[8,4]{0,1:T(4,128)}, u32[]{:S(2)}) copy-start(f32[8,4]{0,1:T(4,128)} %param.21) | copy-start | bytes 388
  2.4 6.4 %collective-permute-start = (f32[56,128]{1,0:T(8,128)S(1)}, f32[56,128]{1,0:T(8,128)S(1)}, u32[]{:S(2)}, u32[]{:S(2)}) collective-permute-start(f32[56,128]{1,0:T(8,128)S(1)} %get-tuple-element.18), channel_id=1, source_target_pairs={{1,2},{2,1},{3,4},{4,3},{5,6},{6,5},{7,8},{8,7},{9,10},{10,9},{11,... | collective-permute-start | bytes 86024 | tf_op jit(solution)/shard_map/ppermute | solution.py:526
  8.9 17.3 %collective-permute-start.1 = (f32[112,128]{1,0:T(8,128)S(1)}, f32[112,128]{1,0:T(8,128)S(1)}, u32[]{:S(2)}, u32[]{:S(2)}) collective-permute-start(f32[112,128]{1,0:T(8,128)S(1)} %shard_map.131.refs_3_), channel_id=1, source_target_pairs={{0,16},{16,0},{32,48},{48,32},{64,80},{80,64},{96,112},{112,96},{1... | collective-permute-start | bytes 172040 | tf_op jit(solution)/shard_map/ppermute | solution.py:529
  26.2 9.1 %collective-permute-start.2 = (f32[56,128]{1,0:T(8,128)S(1)}, f32[56,128]{1,0:T(8,128)S(1)}, u32[]{:S(2)}, u32[]{:S(2)}) collective-permute-start(f32[56,128]{1,0:T(8,128)S(1)} %slice.3), channel_id=1, source_target_pairs={{0,32},{16,496},{32,64},{48,16},{64,96},{80,48},{96,128},{112,80},... | collective-permute-start | bytes 86024 | tf_op jit(solution)/shard_map/ppermute | solution.py:543

commit v4 on v3

--- a/solution.py
+++ b/solution.py
@@ -330,8 +330,8 @@
 
 def own_kernel(deposition, *refs):
     info = position()
-    block, got0, got1, _, planes, start, strips, *outs, halo = refs[:11]
-    work = refs[11:]
+    block, got0, got1, _, planes, start, strips, rates, *outs, halo = refs[:12]
+    work = refs[12:]
     place_lat(info, got0, got1, halo)
     for p in range(MAIN):
         planes[p, BASE : BASE + N, :] = block[p]
@@ -354,6 +354,12 @@
 
     prepare_half(OWN_TALL, BINS, block_field(planes), keep_of, start)
     lane = lax.broadcasted_iota(jnp.int32, (OWN_TALL, N), 1)
+
+    bins = lax.broadcasted_iota(jnp.int32, (1, N), 1) // 32
+    for kind in range(8):
+        rate = jnp.where(bins == 0, deposition[0, kind], deposition[1, kind])
+        rate = jnp.where(bins < 2, rate, jnp.where(bins == 2, deposition[2, kind], deposition[3, kind]))
+        rates[kind : kind + 1, :] = rate
 
     def cut(t, carry):
         row = pl.multiple_of(8 + t * OWN_TALL, 8)
@@ -407,7 +413,7 @@
         both_halves(planes, start, block, refs[3:6], refs[6:])
 
 
-def edge_kernel(deposition, strips_in, near, passed, adj, dens, emis, block, *refs):
+def edge_kernel(rates, strips_in, near, passed, adj, dens, emis, block, *refs):
     adj_out, dens_out, emis_out, strips, sides, turn, start, state, back, flux2, bank, part, rim = refs
     lane = lax.broadcasted_iota(jnp.int32, (8, N), 1)
     parity = position()[1]
@@ -443,18 +449,11 @@
         strips[i, BASE - 8 : BASE, :] = low
         strips[i, BASE + N : BASE + N + 8, :] = high
     field = strip_field(strips)(EDGE_TALL)
-    lane = lax.broadcasted_iota(jnp.int32, (EDGE_TALL, N), 1)
-    rates = []
-    for kind in range(8):
-        rate = jnp.where(lane < 32, deposition[0, kind], deposition[1, kind])
-        rate = jnp.where(lane < 64, rate, jnp.where(lane < 96, deposition[2, kind], deposition[3, kind]))
-        rates.append(rate)
-
     def keep_of(row):
         land = field("land", 0, row)
         rate = jnp.zeros_like(land)
         for kind in range(8):
-            rate = jnp.where(land == float(kind), rates[kind], rate)
+            rate = jnp.where(land == float(kind), rates[kind : kind + 1, :], rate)
         yield 1.0 - TIME_STEP * rate
 
     prepare_half(EDGE_TALL, 1, strip_field(strips), keep_of, start)
@@ -530,11 +529,11 @@
     plane = (ROWS, N)
     shapes = [(BINS, 1, N, N), (1, N, N), (BINS, N, N)]
     work = [(results(BINS)[1], *plane)] + [(BINS, *plane)] * 4 + [(3, *plane)]
-    planes, start, strips, *first_outs = kernel_call(
+    planes, start, strips, rates, *first_outs = kernel_call(
         own_kernel,
         1,
         (deposition, block, got0, got1, both),
-        [(MAIN + EXTRA, *plane), (places(BINS)[1], *plane), (len(STRIPS), *plane), *shapes],
+        [(MAIN + EXTRA, *plane), (places(BINS)[1], *plane), (len(STRIPS), *plane), (8, N), *shapes],
         [(2, *msg), *work],
         flops=OWN_FLOPS,
     )
@@ -552,8 +551,8 @@
     )
     outs = kernel_call(
         edge_kernel,
-        1,
-        (deposition, strips, near, passed, adj, dens, emis, block),
+        0,
+        (rates, strips, near, passed, adj, dens, emis, block),
         shapes,
         [
             (len(STRIPS), *plane),

time: 38.2 us -> 37.6 us (0.984)
  Pallas kernels: 9.92 us -> 9.39 us
    pallas_call x5, Pallas kernels: 9.92 us -> 9.39 us  [kernel_call(): pl.pallas_call(body, out_shape=[pltpu.VMEM(s, F32) if fast else jax.Shape...]
where the time goes in v4:
time: 37.6 us; the launch traced here: 37.4 us
  waiting for transfers between devices  15.6 us (41%)
  starting transfers between devices  9.88 us (26%)
  Pallas kernels  9.39 us (25%)
  blocking collectives  1.85 us (5%)
  between operations  0.7 us (2%)
    pallas_call x5, Pallas kernels, kernel_call(): pl.pallas_call(body, out_shape=[pltpu.VMEM(s, F32) if fast else jax.Shape...  9.39 us
    ppermute x1, waiting for transfers between devices, shards(): near = lax.ppermute(both, 'lon', swaps(lons, 0, False))  8.24 us
    ppermute x1, waiting for transfers between devices, shards(): passed = lax.ppermute(near[LON_MSG:], 'lon', onward)  6.39 us
    ppermute x1, starting transfers between devices, shards(): near = lax.ppermute(both, 'lon', swaps(lons, 0, False))  3.68 us
    ppermute x1, starting transfers between devices, shards(): got1 = lax.ppermute(out1, 'lat', swaps(lats, 1, True))  3.56 us
    ppermute x1, starting transfers between devices, shards(): passed = lax.ppermute(near[LON_MSG:], 'lon', onward)  2.64 us
    all_gather x1, blocking collectives, shards(): lax.all_gather(out0, 'lat', axis_index_groups=[[i, i + 1] for i in range(...  1.85 us
    ppermute x1, waiting for transfers between devices, shards(): got1 = lax.ppermute(out1, 'lat', swaps(lats, 1, True))  0.98 us
  transfers between devices with their start and end apart: 3, of which 3 were waited for; matrix products, arithmetic and copies ran while one was open for 0% of the time, Pallas kernels for 14%

profile of v4, /device:TPU:414, one launch (start us, length us, event | category | flops | bytes accessed | tf_op | source)
XLA Modules:
  0.0 37.4 jit_solution(13332430872652829977)
XLA Ops:
  0.6 0.0 copy-start
  0.6 1.8 %shard_map.130 = (f32[56,128]{1,0:T(8,128)S(1)}, f32[56,128]{1,0:T(8,128)S(1)}, f32[2,56,128]{2,1,0:T(8,128)S(1)}, f32[17,128,128]{2,1,0:T(8,128)S(1)}) custom-call(f32[4,1,128,128]{3,2,1,0:T(8,128)} %refs_0_.1, f32[4,1,128,128]{3,2,1,0:T(8,128)} %refs_1_.1, f32[1,128,128]{2,1,0:T(8,128)} %refs_2_.1, f32[1,128,128]{2,1,0:T(8,128)} %refs_3_.1, ...), custom_call_target="tpu_custom_call" | custom-call | tf_op jit(solution)/shard_map/pallas_call | solution.py:498
  2.4 3.6 %collective-permute-start = (f32[56,128]{1,0:T(8,128)S(1)}, f32[56,128]{1,0:T(8,128)S(1)}, u32[]{:S(2)}, u32[]{:S(2)}) collective-permute-start(f32[56,128]{1,0:T(8,128)S(1)} %get-tuple-element.21), channel_id=1, source_target_pairs={{1,2},{2,1},{3,4},{4,3},{5,6},{6,5},{7,8},{8,7},{9,10},{10,9},{11,... | collective-permute-start | bytes 86024 | tf_op jit(solution)/shard_map/ppermute | solution.py:525
  6.0 1.8 %all-gather = f32[112,128]{1,0:T(8,128)S(1)} all-gather(f32[56,128]{1,0:T(8,128)S(1)} %get-tuple-element.20), channel_id=2, replica_groups={{0,1},{2,3},{4,5},{6,7},{8,9},{10,11},{12,13},{14,15},{16,17},{18,19},{..., dimensions={0}, use_global_device_ids=true | all-gather | bytes 86016 | tf_op jit(solution)/shard_map/all_gather | solution.py:526
  7.9 1.0 %collective-permute-done.got1.refs_2_ = f32[56,128]{1,0:T(8,128)S(1)} collective-permute-done((f32[56,128]{1,0:T(8,128)S(1)}, f32[56,128]{1,0:T(8,128)S(1)}, u32[]{:S(2)}, u32[]{:S(2)}) %collective-permute-start) | collective-permute-done | bytes 28704 | tf_op jit(solution)/shard_map/ppermute | solution.py:525
  8.8 0.1 shard_map.131.refs_3_
  8.9 3.7 %collective-permute-start.1 = (f32[112,128]{1,0:T(8,128)S(1)}, f32[112,128]{1,0:T(8,128)S(1)}, u32[]{:S(2)}, u32[]{:S(2)}) collective-permute-start(f32[112,128]{1,0:T(8,128)S(1)} %shard_map.131.refs_3_), channel_id=1, source_target_pairs={{0,16},{16,0},{32,48},{48,32},{64,80},{80,64},{96,112},{112,96},{1... | collective-permute-start | bytes 172040 | tf_op jit(solution)/shard_map/ppermute | solution.py:528
  12.6 0.0 copy-done
  12.6 5.3 %shard_map.132 = (f32[16,160,128]{2,1,0:T(8,128)S(1)}, f32[11,160,128]{2,1,0:T(8,128)S(1)}, f32[7,160,128]{2,1,0:T(8,128)S(1)}, f32[8,128]{1,0:T(8,128)S(1)}, f3...) custom-call(f32[4,8]{1,0:T(4,128)S(1)} %bitcast.4, ...), custom_call_target="tpu_custom_call" | custom-call | flops 3000000 | tf_op jit(solution)/shard_map/pallas_call | solution.py:498
  17.9 8.2 %collective-permute-done.1.near = f32[112,128]{1,0:T(8,128)S(1)} collective-permute-done((f32[112,128]{1,0:T(8,128)S(1)}, f32[112,128]{1,0:T(8,128)S(1)}, u32[]{:S(2)}, u32[]{:S(2)}) %collective-permute-start.1) | collective-permute-done | bytes 57376 | tf_op jit(solution)/shard_map/ppermute | solution.py:528
  26.2 2.6 %collective-permute-start.2 = (f32[56,128]{1,0:T(8,128)S(1)}, f32[56,128]{1,0:T(8,128)S(1)}, u32[]{:S(2)}, u32[]{:S(2)}) collective-permute-start(f32[56,128]{1,0:T(8,128)S(1)} %slice.3), channel_id=1, source_target_pairs={{0,32},{16,496},{32,64},{48,16},{64,96},{80,48},{96,128},{112,80},... | collective-permute-start | bytes 86024 | tf_op jit(solution)/shard_map/ppermute | solution.py:542
  28.9 6.4 %collective-permute-done.2.passed = f32[56,128]{1,0:T(8,128)S(1)} collective-permute-done((f32[56,128]{1,0:T(8,128)S(1)}, f32[56,128]{1,0:T(8,128)S(1)}, u32[]{:S(2)}, u32[]{:S(2)}) %collective-permute-start.2) | collective-permute-done | bytes 28704 | tf_op jit(solution)/shard_map/ppermute | solution.py:542
  35.3 2.2 %shard_map.134 = (f32[4,1,128,128]{3,2,1,0:T(8,128)}, f32[1,128,128]{2,1,0:T(8,128)}, f32[4,128,128]{2,1,0:T(8,128)}) custom-call(f32[8,128]{1,0:T(8,128)S(1)} %get-tuple-element.23.rates, f32[7,160,128]{2,1,0:T(8,128)S(1)} %get-tuple-element.25.strips_in, f32[112,128]{1,0:T(8,128)S(1)} %collective-permute-done.1.near, ...), custom_call_target="tpu_custom_call" | custom-call | tf_op jit(solution)/shard_map/pallas_call | solution.py:498
  (2 shorter events, 0.0 us)
Async XLA Ops:
  0.6 12.0 %copy-start = (f32[8,4]{0,1:T(4,128)S(1)}, f32[8,4]{0,1:T(4,128)}, u32[]{:S(2)}) copy-start(f32[8,4]{0,1:T(4,128)} %param.21) | copy-start | bytes 388
  2.4 6.4 %collective-permute-start = (f32[56,128]{1,0:T(8,128)S(1)}, f32[56,128]{1,0:T(8,128)S(1)}, u32[]{:S(2)}, u32[]{:S(2)}) collective-permute-start(f32[56,128]{1,0:T(8,128)S(1)} %get-tuple-element.21), channel_id=1, source_target_pairs={{1,2},{2,1},{3,4},{4,3},{5,6},{6,5},{7,8},{8,7},{9,10},{10,9},{11,... | collective-permute-start | bytes 86024 | tf_op jit(solution)/shard_map/ppermute | solution.py:525
  8.9 17.3 %collective-permute-start.1 = (f32[112,128]{1,0:T(8,128)S(1)}, f32[112,128]{1,0:T(8,128)S(1)}, u32[]{:S(2)}, u32[]{:S(2)}) collective-permute-start(f32[112,128]{1,0:T(8,128)S(1)} %shard_map.131.refs_3_), channel_id=1, source_target_pairs={{0,16},{16,0},{32,48},{48,32},{64,80},{80,64},{96,112},{112,96},{1... | collective-permute-start | bytes 172040 | tf_op jit(solution)/shard_map/ppermute | solution.py:528
  26.2 9.1 %collective-permute-start.2 = (f32[56,128]{1,0:T(8,128)S(1)}, f32[56,128]{1,0:T(8,128)S(1)}, u32[]{:S(2)}, u32[]{:S(2)}) collective-permute-start(f32[56,128]{1,0:T(8,128)S(1)} %slice.3), channel_id=1, source_target_pairs={{0,32},{16,496},{32,64},{48,16},{64,96},{80,48},{96,128},{112,80},... | collective-permute-start | bytes 86024 | tf_op jit(solution)/shard_map/ppermute | solution.py:542

commit v5 on v4

--- a/solution.py
+++ b/solution.py
@@ -23,8 +23,6 @@
 REST_TALL, REST_END = 24, 32
 EARLY = 10
 EDGE_TALL, EDGE_END = 144, 128
-PLANES = MAIN + EXTRA + 1
-GROUND = MAIN + EXTRA
 F32 = jnp.float32
 
 
@@ -34,59 +32,54 @@
     return lat % 2, lon % 2, (lat == 0).astype(jnp.int32), (lat == last).astype(jnp.int32)
 
 
-def plane_readers(refs, info):
-    tracer, adjoint, speed_e, speed_n, sign_e, sign_n, density, land, mask, emission = refs
-
-    def east(at, size):
-        s = speed_e[0, pl.ds(at, size), :]
-        return jnp.where(sign_e[0, pl.ds(at, size), :] == 1, s, -s)
-
-    def north(at, size):
-        s = speed_n[0, pl.ds(at, size), :]
-        s = jnp.where(sign_n[0, pl.ds(at, size), :] == 1, s, -s)
-        row = lax.broadcasted_iota(jnp.int32, (size, N), 0) + at
-        return jnp.where((row == 0) & (info[2] == 1), 0.0, s)
-
-    def source(b):
-        def read(at, size):
-            m = mask[pl.ds(at, size), :].astype(F32)
-            return TIME_STEP * m * emission[b, pl.ds(at, size), :]
-
-        return read
-
-    main = [lambda at, size, b=b: tracer[b, 0, pl.ds(at, size), :] for b in range(BINS)]
-    main += [lambda at, size, b=b: adjoint[b, 0, pl.ds(at, size), :] for b in range(BINS)]
-    main += [east, north, lambda at, size: density[0, pl.ds(at, size), :]]
-    extra = [source(b) for b in range(BINS)]
-    extra += [lambda at, size: land[pl.ds(at, size), :].astype(F32)]
-    return main, extra
-
-
-def pack_kernel(*refs):
+def block_planes(tracer, adjoint, emission, few):
+    planes = [tracer[b, 0] for b in range(BINS)] + [adjoint[b, 0] for b in range(BINS)]
+    planes += [few[i] for i in range(3)] + [few[4] * emission[b] for b in range(BINS)]
+    return [*planes, few[3]]
+
+
+def rows_kernel(*refs):
+    large, small, (out0, out1, few) = refs[:3], refs[3:10], refs[10:13]
+    tiles, (speed_e, speed_n, sign_e, sign_n, land, mask), (edge, sem) = refs[13:16], refs[16:22], refs[22:]
     info = position()
-    sources, (out0, out1, lines_out, planes), ins = refs[:10], refs[10:14], refs[14:24]
-    edge, packed, sem = refs[24:]
-    copies = [pltpu.make_async_copy(x, y, sem.at[i]) for i, (x, y) in enumerate(zip(sources, ins, strict=True))]
+    whole = [speed_e, speed_n, sign_e, sign_n, few.at[pl.ds(2, 1)], land, mask]
+    copies = [pltpu.make_async_copy(x, y, sem.at[i]) for i, (x, y) in enumerate(zip(small, whole, strict=True))]
+    for i, (x, y) in enumerate(zip(large, tiles, strict=True)):
+        x = x.at[:, 0] if i < 2 else x
+        for side, at in enumerate((0, N - 8)):
+            copies.append(pltpu.make_async_copy(x.at[:, pl.ds(at, 8)], y.at[side], sem.at[7 + 2 * i + side]))
     for copy in copies:
         copy.start()
     for copy in copies:
         copy.wait()
-    main, extra = plane_readers(ins, info)
-    lane = lax.broadcasted_iota(jnp.int32, (N, N), 1)
-    for p, read in enumerate(main + extra):
-        planes[p] = read(0, N)
-    planes[GROUND] = TIME_STEP * ins[8][...].astype(F32)
-    for p in range(MAIN):
-        edge[0, 4 * p : 4 * p + 4, :] = planes[p, 0:4, :]
-        edge[1, 4 * p : 4 * p + 4, :] = planes[p, N - 4 :, :]
-    for q in range(EXTRA):
-        at = 4 * MAIN + 2 * q
-        edge[0, at : at + 2, :] = planes[MAIN + q, 0:2, :]
-        edge[1, at : at + 2, :] = planes[MAIN + q, N - 2 :, :]
+    row = lax.broadcasted_iota(jnp.int32, (N, N), 0)
+    few[0] = jnp.where(sign_e[0] == 1, speed_e[0], -speed_e[0])
+    wind = jnp.where(sign_n[0] == 1, speed_n[0], -speed_n[0])
+    few[1] = jnp.where((row == 0) & (info[2] == 1), 0.0, wind)
+    few[3] = land[...].astype(F32)
+    few[4] = TIME_STEP * mask[...].astype(F32)
+    tracer, adjoint, emission = tiles
+    for side, at in enumerate((0, N - 8)):
+        low, high = (0, 4) if side == 0 else (4, 8)
+        main = [tracer[side, b] for b in range(BINS)] + [adjoint[side, b] for b in range(BINS)]
+        for p, value in enumerate(main + [few[i, at : at + 8, :] for i in range(3)]):
+            edge[side, 4 * p : 4 * p + 4, :] = value[low:high]
+        ground = few[4, at : at + 8, :]
+        extra = [ground * emission[side, b] for b in range(BINS)] + [few[3, at : at + 8, :]]
+        low, high = (0, 2) if side == 0 else (6, 8)
+        for q, value in enumerate(extra):
+            to = 4 * MAIN + 2 * q
+            edge[side, to : to + 2, :] = value[low:high]
     edge[:, LINES:LAT_MSG, :] = jnp.zeros((2, LAT_MSG - LINES, N), F32)
     parity = info[0]
     out0[...] = edge[1 - parity]
     out1[...] = edge[parity]
+
+
+def pack_kernel(*refs):
+    tracer, adjoint, emission, few, _, lines_out, packed = refs
+    lane = lax.broadcasted_iota(jnp.int32, (N, N), 1)
+    planes = block_planes(tracer, adjoint, emission, few)
     both = jnp.zeros((N, N), F32)
     for p in range(MAIN):
         turned = pltpu.roll(planes[p], 8 * p + 4, 1)
@@ -330,8 +323,9 @@
 
 def own_kernel(deposition, *refs):
     info = position()
-    block, got0, got1, _, planes, start, strips, rates, *outs, halo = refs[:12]
-    work = refs[12:]
+    tracer, adjoint, emission, few, got0, got1, _, planes, start, strips, rates, *outs, halo = refs[:15]
+    block = block_planes(tracer, adjoint, emission, few)
+    work = refs[15:]
     place_lat(info, got0, got1, halo)
     for p in range(MAIN):
         planes[p, BASE : BASE + N, :] = block[p]
@@ -383,7 +377,7 @@
 
     @pl.when(runs_early())
     def _():
-        both_halves(planes, start, block, outs, work)
+        both_halves(planes, start, few, outs, work)
 
 
 def runs_early():
@@ -396,7 +390,7 @@
     first_half(FIRST_TALL, BINS, block_field(planes), start, state, back)
 
     def give(row, at, adjoints, dens, seen):
-        ground = block[GROUND, pl.ds(at, REST_END), :]
+        ground = block[4, pl.ds(at, REST_END), :]
         for b in range(BINS):
             adj_out[b, 0, pl.ds(at, REST_END), :] = adjoints[b]
             emis_out[b, pl.ds(at, REST_END), :] = ground * seen[b]
@@ -467,7 +461,7 @@
         return jnp.where(left, value_left, jnp.where(right, value_right, old))
 
     def give(row, at, adjoints, total, seen):
-        ground = block[GROUND, pl.ds(at, EDGE_END), :]
+        ground = block[4, pl.ds(at, EDGE_END), :]
         for b in range(BINS):
             adj_out[b, 0, pl.ds(at, EDGE_END), :] = patch(adjoints[0], b, adj[b, 0, pl.ds(at, EDGE_END), :])
             old = emis[b, pl.ds(at, EDGE_END), :]
@@ -511,17 +505,19 @@
     ins, deposition = args[:10], args[10].T
     lats, lons = lax.axis_size("lat"), lax.axis_size("lon")
     msg = (LAT_MSG, N)
-    ins = [pltpu.with_memory_space_constraint(x, pltpu.HBM) for x in ins]
-    out0, out1, lines, block = kernel_call(
-        pack_kernel,
+    large, small = [ins[0], ins[1], ins[9]], list(ins[2:9])
+    out0, out1, few = kernel_call(
+        rows_kernel,
         0,
-        ins,
-        [msg, msg, (2, LON_MSG, N), (PLANES, N, N)],
+        [pltpu.with_memory_space_constraint(x, pltpu.HBM) for x in large + small],
+        [msg, msg, (5, N, N)],
         [],
         HBM,
-        [pltpu.VMEM(x.shape, x.dtype) for x in ins]
-        + [pltpu.VMEM((2, *msg), F32), pltpu.VMEM((N, N), F32), pltpu.SemaphoreType.DMA((10,))],
+        [pltpu.VMEM((2, BINS, 8, N), F32)] * 3
+        + [pltpu.VMEM(x.shape, x.dtype) for i, x in enumerate(small) if i != 4]
+        + [pltpu.VMEM((2, *msg), F32), pltpu.SemaphoreType.DMA((13,))],
     )
+    (lines,) = kernel_call(pack_kernel, 0, (*large, few, out1), [(2, LON_MSG, N)], [(N, N)])
     got1 = lax.ppermute(out1, "lat", swaps(lats, 1, True))
     got0 = lax.all_gather(out0, "lat", axis_index_groups=[[i, i + 1] for i in range(0, lats, 2)])
     (both,) = kernel_call(corner_kernel, 0, (got1, got0, lines), [(2 * LON_MSG, N)], [(2, *msg), (N, N)])
@@ -532,7 +528,7 @@
     planes, start, strips, rates, *first_outs = kernel_call(
         own_kernel,
         1,
-        (deposition, block, got0, got1, both),
+        (deposition, *large, few, got0, got1, both),
         [(MAIN + EXTRA, *plane), (places(BINS)[1], *plane), (len(STRIPS), *plane), (8, N), *shapes],
         [(2, *msg), *work],
         flops=OWN_FLOPS,
@@ -543,7 +539,7 @@
     adj, dens, emis = kernel_call(
         rest_kernel,
         0,
-        (planes, start, block, near, *first_outs),
+        (planes, start, few, near, *first_outs),
         shapes,
         work,
         aliases={4: 0, 5: 1, 6: 2},
@@ -552,7 +548,7 @@
     outs = kernel_call(
         edge_kernel,
         0,
-        (rates, strips, near, passed, adj, dens, emis, block),
+        (rates, strips, near, passed, adj, dens, emis, few),
         shapes,
         [
             (len(STRIPS), *plane),

time: 37.6 us -> 37.9 us (level)
  the two profiles are of different devices: /device:TPU:414 before, /device:TPU:64 now
where the time goes in v5:
time: 37.9 us; the launch traced here: 37.7 us
  starting transfers between devices  18.6 us (49%)
  Pallas kernels  9.3 us (25%)
  waiting for transfers between devices  5.52 us (15%)
  blocking collectives  3.52 us (9%)
  between operations  0.77 us (2%)
    ppermute x1, starting transfers between devices, shards(): near = lax.ppermute(both, 'lon', swaps(lons, 0, False))  13.2 us
    pallas_call x6, Pallas kernels, kernel_call(): pl.pallas_call(body, out_shape=[pltpu.VMEM(s, F32) if fast else jax.Shape...  9.3 us
    all_gather x1, blocking collectives, shards(): lax.all_gather(out0, 'lat', axis_index_groups=[[i, i + 1] for i in range(...  3.52 us
    ppermute x1, starting transfers between devices, shards(): passed = lax.ppermute(near[LON_MSG:], 'lon', onward)  3.47 us
    ppermute x1, waiting for transfers between devices, shards(): near = lax.ppermute(both, 'lon', swaps(lons, 0, False))  3.11 us
    ppermute x1, waiting for transfers between devices, shards(): passed = lax.ppermute(near[LON_MSG:], 'lon', onward)  2.41 us
    ppermute x1, starting transfers between devices, shards(): got1 = lax.ppermute(out1, 'lat', swaps(lats, 1, True))  1.92 us
  transfers between devices with their start and end apart: 3, of which 2 were waited for; matrix products, arithmetic and copies ran while one was open for 0% of the time, Pallas kernels for 15%

profile of v5, /device:TPU:64, one launch (start us, length us, event | category | flops | bytes accessed | tf_op | source)
XLA Modules:
  0.0 37.7 jit_solution(17824113700145608170)
XLA Ops:
  0.6 0.0 copy-start.2
  0.6 0.0 copy-start.1
  0.7 0.0 copy-start
  0.7 0.0 copy-start.3
  0.7 1.3 %shard_map.130 = (f32[56,128]{1,0:T(8,128)S(1)}, f32[56,128]{1,0:T(8,128)S(1)}, f32[5,128,128]{2,1,0:T(8,128)S(1)}) custom-call(f32[4,1,128,128]{3,2,1,0:T(8,128)} %refs_0_.5, f32[4,1,128,128]{3,2,1,0:T(8,128)} %refs_1_.5, f32[4,128,128]{2,1,0:T(8,128)} %refs_2_.5, f32[1,128,128]{2,1,0:T(8,128)} %refs_3_.1, f32[1,128,128]{2,1,0:T(8,128)} %refs_4_.1, ...), custom_call_target="tpu_custom_call" | custom-call | tf_op jit(solution)/shard_map/pallas_call | solution.py:492
  1.9 1.9 %collective-permute-start = (f32[56,128]{1,0:T(8,128)S(1)}, f32[56,128]{1,0:T(8,128)S(1)}, u32[]{:S(2)}, u32[]{:S(2)}) collective-permute-start(f32[56,128]{1,0:T(8,128)S(1)} %get-tuple-element.20.refs_4_), channel_id=1, source_target_pairs={{1,2},{2,1},{3,4},{4,3},{5,6},{6,5},{7,8},{8,7},{9,10},{10,9},{11,... | collective-permute-start | bytes 86024 | tf_op jit(solution)/shard_map/ppermute | solution.py:521
  3.9 0.0 copy-done.2
  3.9 0.0 copy-done.1
  3.9 0.0 copy-done
  3.9 0.4 %shard_map.131.lines = f32[2,56,128]{2,1,0:T(8,128)S(1)} custom-call(f32[4,1,128,128]{3,2,1,0:T(8,128)S(1)} %copy-done, f32[4,1,128,128]{3,2,1,0:T(8,128)S(1)} %copy-done.1, f32[4,128,128]{2,1,0:T(8,128)S(1)} %copy-done.2, f32[5,128,128]{2,1,0:T(8,128)S(1)} %get-tuple-element.18.refs_3_.block, f32[56,128]{1,0:T(8,128)S(1)} %get-tuple-element.20.refs_4_), custom_call_target="tpu_custom_call" | custom-call | tf_op jit(solution)/shard_map/pallas_call | solution.py:492
  4.3 3.5 %all-gather = f32[112,128]{1,0:T(8,128)S(1)} all-gather(f32[56,128]{1,0:T(8,128)S(1)} %get-tuple-element.19), channel_id=2, replica_groups={{0,1},{2,3},{4,5},{6,7},{8,9},{10,11},{12,13},{14,15},{16,17},{18,19},{..., dimensions={0}, use_global_device_ids=true | all-gather | bytes 86016 | tf_op jit(solution)/shard_map/all_gather | solution.py:522
  7.8 0.0 collective-permute-done.got1.refs_5_
  7.9 0.1 shard_map.132.refs_6_
  7.9 13.2 %collective-permute-start.1 = (f32[112,128]{1,0:T(8,128)S(1)}, f32[112,128]{1,0:T(8,128)S(1)}, u32[]{:S(2)}, u32[]{:S(2)}) collective-permute-start(f32[112,128]{1,0:T(8,128)S(1)} %shard_map.132.refs_6_), channel_id=1, source_target_pairs={{0,16},{16,0},{32,48},{48,32},{64,80},{80,64},{96,112},{112,96},{1... | collective-permute-start | bytes 172040 | tf_op jit(solution)/shard_map/ppermute | solution.py:524
  21.2 0.0 copy-done.3
  21.2 2.2 %shard_map.133 = (f32[16,160,128]{2,1,0:T(8,128)S(1)}, f32[11,160,128]{2,1,0:T(8,128)S(1)}, f32[7,160,128]{2,1,0:T(8,128)S(1)}, f32[8,128]{1,0:T(8,128)S(1)}, f3...) custom-call(f32[4,8]{1,0:T(4,128)S(1)} %bitcast.4, ...), custom_call_target="tpu_custom_call" | custom-call | flops 3000000 | tf_op jit(solution)/shard_map/pallas_call | solution.py:492
  23.4 3.1 %collective-permute-done.1.near = f32[112,128]{1,0:T(8,128)S(1)} collective-permute-done((f32[112,128]{1,0:T(8,128)S(1)}, f32[112,128]{1,0:T(8,128)S(1)}, u32[]{:S(2)}, u32[]{:S(2)}) %collective-permute-start.1) | collective-permute-done | bytes 57376 | tf_op jit(solution)/shard_map/ppermute | solution.py:524
  26.5 3.5 %collective-permute-start.2 = (f32[56,128]{1,0:T(8,128)S(1)}, f32[56,128]{1,0:T(8,128)S(1)}, u32[]{:S(2)}, u32[]{:S(2)}) collective-permute-start(f32[56,128]{1,0:T(8,128)S(1)} %slice.3), channel_id=1, source_target_pairs={{0,32},{16,496},{32,64},{48,16},{64,96},{80,48},{96,128},{112,80},... | collective-permute-start | bytes 86024 | tf_op jit(solution)/shard_map/ppermute | solution.py:538
  30.0 3.2 %shard_map.134 = (f32[4,1,128,128]{3,2,1,0:T(8,128)S(1)}, f32[1,128,128]{2,1,0:T(8,128)S(1)}, f32[4,128,128]{2,1,0:T(8,128)S(1)}) custom-call(f32[16,160,128]{2,1,0:T(8,128)S(1)} %get-tuple-element.25.planes, f32[11,160,128]{2,1,0:T(8,128)S(1)} %get-tuple-element.26.start, ...), custom_call_target="tpu_custom_call", output_to_operand_aliasing={{0}: (4, {}), {1}: (5, {}), {2}: (6, {})} | custom-call | flops 3000000 | tf_op jit(solution)/shard_map/pallas_call | solution.py:492
  33.2 2.4 %collective-permute-done.2.passed = f32[56,128]{1,0:T(8,128)S(1)} collective-permute-done((f32[56,128]{1,0:T(8,128)S(1)}, f32[56,128]{1,0:T(8,128)S(1)}, u32[]{:S(2)}, u32[]{:S(2)}) %collective-permute-start.2) | collective-permute-done | bytes 28704 | tf_op jit(solution)/shard_map/ppermute | solution.py:538
  35.6 2.2 %shard_map.135 = (f32[4,1,128,128]{3,2,1,0:T(8,128)}, f32[1,128,128]{2,1,0:T(8,128)}, f32[4,128,128]{2,1,0:T(8,128)}) custom-call(f32[8,128]{1,0:T(8,128)S(1)} %get-tuple-element.21.rates, f32[7,160,128]{2,1,0:T(8,128)S(1)} %get-tuple-element.23.strips_in, f32[112,128]{1,0:T(8,128)S(1)} %collective-permute-done.1.near, ...), custom_call_target="tpu_custom_call" | custom-call | tf_op jit(solution)/shard_map/pallas_call | solution.py:492
  (1 shorter events, 0.0 us)
Async XLA Ops:
  0.6 3.2 %copy-start.2 = (f32[4,128,128]{2,1,0:T(8,128)S(1)}, f32[4,128,128]{2,1,0:T(8,128)}, u32[]{:S(2)}) copy-start(f32[4,128,128]{2,1,0:T(8,128)} %refs_2_.5) | copy-start | bytes 786436
  0.6 3.2 %copy-start.1 = (f32[4,1,128,128]{3,2,1,0:T(8,128)S(1)}, f32[4,1,128,128]{3,2,1,0:T(8,128)}, u32[]{:S(2)}) copy-start(f32[4,1,128,128]{3,2,1,0:T(8,128)} %refs_1_.5) | copy-start | bytes 786436
  0.7 3.2 %copy-start = (f32[4,1,128,128]{3,2,1,0:T(8,128)S(1)}, f32[4,1,128,128]{3,2,1,0:T(8,128)}, u32[]{:S(2)}) copy-start(f32[4,1,128,128]{3,2,1,0:T(8,128)} %refs_0_.5) | copy-start | bytes 786436
  0.7 20.5 %copy-start.3 = (f32[8,4]{0,1:T(4,128)S(1)}, f32[8,4]{0,1:T(4,128)}, u32[]{:S(2)}) copy-start(f32[8,4]{0,1:T(4,128)} %param.21) | copy-start | bytes 388
  1.9 5.9 %collective-permute-start = (f32[56,128]{1,0:T(8,128)S(1)}, f32[56,128]{1,0:T(8,128)S(1)}, u32[]{:S(2)}, u32[]{:S(2)}) collective-permute-start(f32[56,128]{1,0:T(8,128)S(1)} %get-tuple-element.20.refs_4_), channel_id=1, source_target_pairs={{1,2},{2,1},{3,4},{4,3},{5,6},{6,5},{7,8},{8,7},{9,10},{10,9},{11,... | collective-permute-start | bytes 86024 | tf_op jit(solution)/shard_map/ppermute | solution.py:521
  7.9 18.5 %collective-permute-start.1 = (f32[112,128]{1,0:T(8,128)S(1)}, f32[112,128]{1,0:T(8,128)S(1)}, u32[]{:S(2)}, u32[]{:S(2)}) collective-permute-start(f32[112,128]{1,0:T(8,128)S(1)} %shard_map.132.refs_6_), channel_id=1, source_target_pairs={{0,16},{16,0},{32,48},{48,32},{64,80},{80,64},{96,112},{112,96},{1... | collective-permute-start | bytes 172040 | tf_op jit(solution)/shard_map/ppermute | solution.py:524
  26.5 9.1 %collective-permute-start.2 = (f32[56,128]{1,0:T(8,128)S(1)}, f32[56,128]{1,0:T(8,128)S(1)}, u32[]{:S(2)}, u32[]{:S(2)}) collective-permute-start(f32[56,128]{1,0:T(8,128)S(1)} %slice.3), channel_id=1, source_target_pairs={{0,32},{16,496},{32,64},{48,16},{64,96},{80,48},{96,128},{112,80},... | collective-permute-start | bytes 86024 | tf_op jit(solution)/shard_map/ppermute | solution.py:538
